TPU v7x, 32 devices: a whole 2x2x4 slice. The times are simulated.
32 devices in a mesh: grp: 2 (over x), orbit: 4 (over y, core), chan: 4 (over z).
Axes of the slice: x: 2, y: 2, z: 4, core: 2. Of those that a mesh axis runs over, the one named last changes fastest.
Arguments:
- innovation: bfloat16 [65536, 1024], P(('grp', 'orbit'), 'chan'), parts along dimension 0, may hold values from -6 to 6
- perturbation: bfloat16 [65536, 1024], P(('grp', 'orbit'), 'chan'), parts along dimension 0, may hold values from -6 to 6
- quality: int32 [65536], P(('grp', 'orbit')), parts along dimension 0, may hold values 0 or 1
- neighbours: int32 [512, 6], P(('grp', 'orbit')), parts along dimension 0, may hold values from 0 to 255, as said below
- counts: int32 [512], P(('grp', 'orbit')), parts along dimension 0, may hold values from 1 to 6
- spatial_blocks: bfloat16 [512, 6, 128, 128], P(('grp', 'orbit')), parts along dimension 0, may hold values from -0.21875 to 0.21875
- chan_op: bfloat16 [1024, 1024], replicated, may hold values from -0.1875 to 0.1875
Outputs:
- weighted_innovation: bfloat16 [65536, 1024], P(('grp', 'orbit'), 'chan'), parts along dimension 0
- weighted_perturbation: bfloat16 [65536, 1024], P(('grp', 'orbit'), 'chan'), parts along dimension 0
There are 2 independent parts, one for each index of `grp`. A program takes and returns all parts, laid end to end along the dimension named above; an argument that names none is the same for every part. Nothing has to cross between parts.
Inputs may be any that keep to these rules, and one draw needn't show every extreme that they name: `neighbours`: each neighbour of block b lies within 64 blocks of b.
All inputs are finite; a program needn't handle non-finite values. No bound on the sum of `quality` on one device may be relied on, other than what follows from the above.
Results may differ from a plain program's by a relative error of at most 0.0049.
Values may be sent and summed in bfloat16 or wider, within the bound.
No kernel may reach another device: no remote copies, remote signals or barrier semaphores. Data moves between devices by JAX's collectives and lax.ppermute only.
A program may use at most 256 MiB of HBM per device.

v0:
```python
import jax
import jax.numpy as jnp
from jax import lax
from jax.sharding import PartitionSpec as P


def with_halo(cells, sides, width):
    for axis, dim in sides:
        count = lax.axis_size(axis)
        ends = count - 1
        head = lax.slice_in_dim(cells, 0, width, axis=dim)
        tail = lax.slice_in_dim(cells, cells.shape[dim] - width, cells.shape[dim], axis=dim)
        cells = jnp.concatenate(
            [
                lax.ppermute(tail, axis, [(i, (i + 1) % count) for i in range(ends)]),
                cells,
                lax.ppermute(head, axis, [((i + 1) % count, i) for i in range(ends)]),
            ],
            axis=dim,
        )
    return cells


def shards(innovation, perturbation, quality, neighbours, counts, spatial_blocks, chan_op):
    rows, width = innovation.shape
    block_rows = spatial_blocks.shape[2]
    slots = spatial_blocks.shape[1]
    nblk = rows // block_rows
    keep = quality.astype(jnp.bfloat16)[:, None]
    stacked = jnp.stack([innovation * keep, perturbation * keep])
    padded = with_halo(stacked, (("orbit", 1),), rows)
    tiles = padded.reshape(2, 3 * nblk, block_rows, width)
    first = lax.axis_index("orbit") * nblk - nblk
    local_ids = neighbours - first
    picked = jnp.take(tiles, local_ids.reshape(-1), axis=1).reshape(
        2, nblk, slots, block_rows, width
    )
    live = (jnp.arange(slots, dtype=jnp.int32)[None, :] < counts[:, None]).astype(jnp.bfloat16)
    weights = spatial_blocks * live[:, :, None, None]
    spatial = jnp.einsum(
        "bsij,vbsjc->vbic", weights, picked, preferred_element_type=jnp.float32
    ).astype(jnp.bfloat16)
    flat = spatial.reshape(2 * nblk, block_rows, width)
    by_rows = lax.all_to_all(flat, "chan", split_axis=0, concat_axis=2, tiled=True)
    mixed = jnp.einsum("nic,cd->nid", by_rows, chan_op, preferred_element_type=jnp.float32).astype(
        jnp.bfloat16
    )
    result = lax.all_to_all(mixed, "chan", split_axis=2, concat_axis=0, tiled=True)
    result = result.reshape(2, rows, width) * keep
    return (result[0], result[1])


def solution(mesh):
    placed = (
        P(("grp", "orbit"), "chan"),
        P(("grp", "orbit"), "chan"),
        P(("grp", "orbit")),
        P(("grp", "orbit"), None),
        P(("grp", "orbit")),
        P(("grp", "orbit"), None, None, None),
        P(),
    )
    return jax.shard_map(
        shards,
        mesh=mesh,
        in_specs=placed,
        out_specs=(P(("grp", "orbit"), "chan"), P(("grp", "orbit"), "chan")),
        check_vma=False,
    )
```

profile of v0, /device:TPU:11, one launch (start us, length us, event | category | flops | bytes accessed | tf_op | source)
XLA Modules:
  0.0 564.9 jit_solution(11867878666848216709)
XLA Ops:
  0.6 0.0 copy-start
  0.6 0.9 convert_element_type.19
  1.6 5.4 multiply_bitcast_fusion.1
  7.0 0.0 copy-done.2
  7.0 0.0 copy-start.5
  7.0 7.7 %pad_maximum_fusion.1 = bf16[2,8192,256]{2,1,0:T(8,128)(2,1)} fusion(bf16[1,8192,256]{2,1,0:T(8,128)(2,1)} %get-tuple-element.7, bf16[1,8192,256]{2,1,0:T(8,128)(2,1)S(1)} %get-tuple-element.6), kind=kLoop, calls=%fused_computation.9 | loop fusion | flops 4194304 | bytes 16777216 | tf_op jit(solution)/shard_map/stack | solution.py:30
  14.7 0.0 copy-done.1
  14.7 3.7 collective-permute-start
  18.4 3.8 collective-permute-start.1
  22.3 0.0 copy-done.4
  22.3 0.1 copy.25
  22.4 0.1 reshape.79
  22.5 0.1 copy.24
  22.7 0.0 copy-done.5
  22.7 0.1 fusion.11
  22.8 86.3 %collective-permute-done = bf16[2,8192,256]{2,1,0:T(8,128)(2,1)} collective-permute-done((bf16[2,8192,256]{2,1,0:T(8,128)(2,1)}, bf16[2,8192,256]{2,1,0:T(8,128)(2,1)}, u32[]{:S(2)}, u32[]{:S(2)}) %collective-permute-start) | collective-permute-done | bytes 8388640 | tf_op jit(solution)/shard_map/ppermute | solution.py:15
  109.1 4.4 collective-permute-done.1
  113.5 22.3 %pad_maximum_fusion = bf16[2,24576,256]{2,1,0:T(8,128)(2,1)} fusion(bf16[2,8192,256]{2,1,0:T(8,128)(2,1)} %collective-permute-done.1, bf16[1,8192,256]{2,1,0:T(8,128)(2,1)} %get-tuple-element.7, bf16[1,8192,256]{2,1,0:T(8,128)(2,1)} %copy-done.1, bf16[2,8192,256]{2,1,0:T(8,128)(2,1)} %collective-permute-done), kind=kLoop, calls=%fused_computation.4 | loop fusion | flops 100663296 | bytes 50331648 | tf_op jit(solution)/shard_map/concatenate | solution.py:13
  135.8 27.7 %gather_fusion = bf16[384,2,128,256]{3,2,1,0:T(8,128)(2,1)} fusion(bf16[2,192,128,256]{3,2,1,0:T(8,128)(2,1)} %bitcast.39, s32[1024]{0:T(1024)S(1)} %pad_clamp_fusion), kind=kCustom, calls=%fused_computation | custom fusion | bytes 100664832 | tf_op jit(solution)/shard_map/jit(_take)/gather | solution.py:35
  163.5 33.0 %copy.26 = bf16[2,384,128,256]{3,2,1,0:T(8,128)(2,1)} copy(bf16[2,384,128,256]{3,2,0,1:T(8,128)(2,1)} %bitcast.40) | data formatting | bytes 100663296 | tf_op jit(solution)/shard_map/jit(_take)/gather | solution.py:35
  196.5 28.3 %fusion.4 = bf16[2,64,128,256]{2,3,0,1:T(8,128)(2,1)} fusion(bf16[64,6,128,128]{3,2,1,0:T(8,128)(2,1)} %param.12, bf16[64,6]{1,0:T(8,128)(2,1)S(1)} %fusion.11, bf16[2,64,6,128,256]{4,3,2,1,0:T(8,128)(2,1)} %bitcast.41, pred[64,6]{1,0:T(8,128)(4,1)S(1)} %copy.24), kind=kOutput, calls=%fused_computation.8 | convolution fusion | flops 6478102528 | bytes 71304320 | tf_op jit(solution)/shard_map/bsij,vbsjc->vbic/dot_general | solution.py:40
  224.7 11.9 %copy.28 = bf16[2,64,128,256]{3,2,1,0:T(8,128)(2,1)} copy(bf16[2,64,128,256]{2,3,0,1:T(8,128)(2,1)} %fusion.4) | data formatting | bytes 16777216 | tf_op jit(solution)/shard_map/convert_element_type | solution.py:42
  236.7 112.0 %all_to_all.33 = bf16[128,128,256]{2,1,0:T(8,128)(2,1)} all-to-all(bf16[128,128,256]{2,1,0:T(8,128)(2,1)} %bitcast.43), channel_id=1, replica_groups=mesh['grp'=2,'orbit'=4,'chan'=4] {'chan'}, dimensions={0} | all-to-all | bytes 16777216 | tf_op jit(solution)/shard_map/all_to_all | solution.py:44
  348.6 7.7 %copy.36 = bf16[4,32,16,8,256]{4,3,0,2,1:T(8,128)(2,1)} copy(bf16[4,32,16,8,256]{4,3,2,1,0:T(8,128)(2,1)} %bitcast.44) | data formatting | bytes 16777216 | tf_op jit(solution)/shard_map/all_to_all | solution.py:44
  356.3 0.0 copy-done
  356.3 14.5 %convolution_convert_fusion = bf16[32,128,1024]{2,1,0:T(8,128)(2,1)} fusion(bf16[32,128,1024]{2,1,0:T(8,128)(2,1)} %bitcast.46, bf16[1024,1024]{1,0:T(8,128)(2,1)S(1)} %copy-done), kind=kOutput, calls=%fused_computation.10 | convolution fusion | flops 8594128896 | bytes 18874368 | tf_op jit(solution)/shard_map/nic,cd->nid/dot_general | solution.py:45
  370.9 12.5 %copy.30 = bf16[32,128,1024]{1,0,2:T(8,128)(2,1)} copy(bf16[32,128,1024]{2,1,0:T(8,128)(2,1)} %convolution_convert_fusion) | data formatting | bytes 16777216 | tf_op jit(solution)/shard_map/convert_element_type | solution.py:45
  383.4 159.5 %all_to_all.34 = bf16[32,128,1024]{1,0,2:T(8,128)(2,1)} all-to-all(bf16[32,128,1024]{1,0,2:T(8,128)(2,1)} %copy.30), channel_id=1, replica_groups=mesh['grp'=2,'orbit'=4,'chan'=4] {'chan'}, dimensions={2} | all-to-all | bytes 16777216 | tf_op jit(solution)/shard_map/all_to_all | solution.py:48
  542.9 13.7 %copy.31 = bf16[4,32,128,256]{3,2,1,0:T(8,128)(2,1)} copy(bf16[4,32,128,256]{2,1,3,0:T(8,128)(2,1)} %bitcast.45) | data formatting | bytes 16777216 | tf_op jit(solution)/shard_map/all_to_all | solution.py:48
  556.6 0.0 copy-done.3
  556.6 4.7 broadcast_multiply_fusion
  561.3 3.6 slice_bitcast_fusion
  (7 shorter events, 0.0 us)
Async XLA Ops:
  0.6 355.7 %copy-start = (bf16[1024,1024]{1,0:T(8,128)(2,1)S(1)}, bf16[1024,1024]{1,0:T(8,128)(2,1)}, u32[]{:S(2)}) copy-start(bf16[1024,1024]{1,0:T(8,128)(2,1)} %param.13) | copy-start | bytes 6291460
  1.6 5.4 copy-start.2
  7.0 7.7 %copy-start.1 = (bf16[1,8192,256]{2,1,0:T(8,128)(2,1)}, bf16[1,8192,256]{2,1,0:T(8,128)(2,1)S(1)}, u32[]{:S(2)}) copy-start(bf16[1,8192,256]{2,1,0:T(8,128)(2,1)S(1)} %get-tuple-element.6) | copy-start | bytes 12582916
  7.0 15.3 %copy-start.4 = (s32[64,6]{0,1:T(8,128)S(1)}, s32[64,6]{0,1:T(8,128)}, u32[]{:S(2)}) copy-start(s32[64,6]{0,1:T(8,128)} %param.10) | copy-start | bytes 4612
  7.0 15.7 %copy-start.5 = (s32[64]{0:T(128)S(1)}, s32[64]{0:T(128)}, u32[]{:S(2)}) copy-start(s32[64]{0:T(128)} %param.11) | copy-start | bytes 772
  14.7 94.4 %collective-permute-start = (bf16[2,8192,256]{2,1,0:T(8,128)(2,1)}, bf16[2,8192,256]{2,1,0:T(8,128)(2,1)}, u32[]{:S(2)}, u32[]{:S(2)}) collective-permute-start(bf16[2,8192,256]{2,1,0:T(8,128)(2,1)} %pad_maximum_fusion.1), channel_id=1, source_target_pairs={{0,4},{4,8},{8,12},{1,5},{5,9},{9,13},{2,6},{6,10},{10,14},{3,7},{... | collective-permute-start | bytes 25165832 | tf_op jit(solution)/shard_map/ppermute | solution.py:15
  18.4 95.1 %collective-permute-start.1 = (bf16[2,8192,256]{2,1,0:T(8,128)(2,1)}, bf16[2,8192,256]{2,1,0:T(8,128)(2,1)}, u32[]{:S(2)}, u32[]{:S(2)}) collective-permute-start(bf16[2,8192,256]{2,1,0:T(8,128)(2,1)} %pad_maximum_fusion.1), channel_id=1, source_target_pairs={{4,0},{8,4},{12,8},{5,1},{9,5},{13,9},{6,2},{10,6},{14,10},{7,3},{... | collective-permute-start | bytes 25165832 | tf_op jit(solution)/shard_map/ppermute | solution.py:17
  542.9 13.7 %copy-start.3 = (bf16[8192]{0:T(1024)(128)(2,1)S(1)}, bf16[8192]{0:T(1024)(128)(2,1)}, u32[]{:S(2)}) copy-start(bf16[8192]{0:T(1024)(128)(2,1)} %copy-done.2) | copy-start | bytes 49156
where the time goes:
time: 568 us; the launch traced here: 565 us
  blocking collectives  271 us (48%)
  local copies, waits for them, and re-layouts  111 us (20%)
  waiting for transfers between devices  90.7 us (16%)
  matrix products  42.8 us (8%)
  other arithmetic  41.1 us (7%)
  starting transfers between devices  7.54 us (1%)
    all_to_all x1, blocking collectives, shards(): lax.all_to_all(mixed, 'chan', split_axis=2, concat_axis=0, tiled=True)  160 us
    all_to_all x1, blocking collectives, shards(): lax.all_to_all(flat, 'chan', split_axis=0, concat_axis=2, tiled=True)  112 us
    ppermute x1, waiting for transfers between devices, with_halo(): lax.ppermute(tail, axis, [(i, (i + 1) % count) for i in range(ends)])  86.3 us
    gather x2, local copies, waits for them, and re-layouts, shards(): jnp.take(tiles, local_ids.reshape(-1), axis=1)  60.7 us
    dot_general x1, matrix products, shards(): jnp.einsum('bsij,vbsjc->vbic', weights, picked, preferred_element_type=jn...  28.3 us
    concatenate x1, other arithmetic, with_halo(): jnp.concatenate([lax.ppermute(tail, axis, [(i, (i + 1) % count) for i in...  22.3 us
    dot_general x1, matrix products, shards(): jnp.einsum('nic,cd->nid', by_rows, chan_op, preferred_element_type=jnp.fl...  14.5 us
    all_to_all x1, local copies, waits for them, and re-layouts, shards(): lax.all_to_all(mixed, 'chan', split_axis=2, concat_axis=0, tiled=True)  13.7 us
  transfers between devices with their start and end apart: 2, of which 2 were waited for; matrix products, arithmetic and copies ran while one was open for 0% of the time, Pallas kernels for 0%

commit v1 on v0

v1 whole, which is shorter than its diff:
```python
import functools

import jax
import jax.numpy as jnp
from jax import lax
from jax.experimental import pallas as pl
from jax.experimental.pallas import tpu as pltpu
from jax.sharding import PartitionSpec as P

VMEM_LIMIT = 48 * 1024 * 1024
ALIGN = 16
GROUP = 8


def params():
    return pltpu.CompilerParams(
        dimension_semantics=("arbitrary",), vmem_limit_bytes=VMEM_LIMIT
    )


def plan_kernel(quality_ref, pos_ref, offs_ref):
    blocks, rows = quality_ref.shape
    keep = quality_ref[...]
    ones = keep.astype(jnp.float32).astype(jnp.bfloat16)

    def tri(size, strict):
        a = lax.broadcasted_iota(jnp.int32, (size, size), 0)
        b = lax.broadcasted_iota(jnp.int32, (size, size), 1)
        return jnp.where(a < b if strict else a <= b, 1.0, 0.0).astype(jnp.bfloat16)

    within = jnp.dot(ones, tri(rows, True), preferred_element_type=jnp.float32)
    total = jnp.sum(keep.astype(jnp.float32), axis=1, keepdims=True)
    wide = jnp.broadcast_to(total, (blocks, rows)).astype(jnp.bfloat16)
    a = lax.broadcasted_iota(jnp.int32, (blocks, blocks), 0)
    b = lax.broadcasted_iota(jnp.int32, (blocks, blocks), 1)
    below = jnp.where(b < a, 1.0, 0.0).astype(jnp.bfloat16)
    before = jnp.dot(below, wide, preferred_element_type=jnp.float32)
    pos = (before + within).astype(jnp.int32)
    pos_ref[...] = jnp.where(keep > 0, pos, -1)
    offs_ref[...] = before.astype(jnp.int32)


def plan(quality, block_rows):
    nblk = quality.shape[0] // block_rows
    shape = jax.ShapeDtypeStruct((nblk, block_rows), jnp.int32)
    pos, offs = pl.pallas_call(plan_kernel, out_shape=(shape, shape))(
        quality.reshape(nblk, block_rows)
    )
    return pos, offs[:, 0]


def window(offs_ref, block):
    return pl.multiple_of((offs_ref[block] // ALIGN) * ALIGN, ALIGN)


def one_hot(pos, start, block_rows):
    span = block_rows + ALIGN
    at = lax.broadcasted_iota(jnp.int32, (span, block_rows), 0) + start
    return jnp.where(at == pos, 1.0, 0.0).astype(jnp.bfloat16)


def put_compact(packed, pos, start, tile):
    block_rows = tile.shape[0]
    part = jnp.dot(
        one_hot(pos, start, block_rows), tile, preferred_element_type=jnp.float32
    ).astype(jnp.bfloat16)
    packed[pl.ds(start, ALIGN), :] = packed[pl.ds(start, ALIGN), :] + part[:ALIGN]
    packed[pl.ds(pl.multiple_of(start + ALIGN, ALIGN), block_rows), :] = part[ALIGN:]


def clear(ref):
    rows = ref.shape[0]
    step = ALIGN

    def body(i, carry):
        ref[pl.ds(pl.multiple_of(i * step, step), step), :] = jnp.zeros(
            (step, ref.shape[1]), ref.dtype
        )
        return carry

    lax.fori_loop(0, rows // step, body, 0, unroll=8 if rows // step % 8 == 0 else 1)


def part_copies(packed, outs, sems, me, sizes, count, outward):
    copies = []
    base = 0
    at = 0
    for size in sizes:
        for shift in range(count):
            owner = lax.rem(me + (shift if outward else count - shift), count)
            where = packed.at[pl.ds(pl.multiple_of(base + owner * size, ALIGN), size), :]
            if outward:
                copies.append(pltpu.make_async_copy(where, outs[at], sems.at[at]))
            else:
                copies.append(pltpu.make_async_copy(outs[at], where, sems.at[at]))
            at += 1
        base += size * count
    return copies


def compact_kernel(sizes, count, me_ref, offs_ref, pos_ref, v_ref, *rest):
    outs, (packed, sems) = rest[:-2], rest[-2:]
    block_rows = pos_ref.shape[1]
    step = pl.program_id(0)

    @pl.when(step == 0)
    def _():
        clear(packed)

    for i in range(GROUP):
        put_compact(
            packed,
            pos_ref[i : i + 1, :],
            window(offs_ref, step * GROUP + i),
            v_ref[i * block_rows : (i + 1) * block_rows, :],
        )

    @pl.when(step == pl.num_programs(0) - 1)
    def _():
        copies = part_copies(packed, outs, sems, me_ref[0], sizes, count, True)
        for copy in copies:
            copy.start()
        for copy in copies:
            copy.wait()


def part_shapes(sizes, count, width):
    return tuple(
        jax.ShapeDtypeStruct((size, width), jnp.bfloat16) for size in sizes for _ in range(count)
    )


def compact(v, pos, offs, me, sizes, count):
    rows, width = v.shape
    nblk, block_rows = pos.shape
    shapes = part_shapes(sizes, count, width)
    return pl.pallas_call(
        functools.partial(compact_kernel, sizes, count),
        out_shape=shapes,
        grid_spec=pltpu.PrefetchScalarGridSpec(
            num_scalar_prefetch=2,
            grid=(nblk // GROUP,),
            in_specs=[
                pl.BlockSpec((GROUP, block_rows), lambda i, *_: (i, 0)),
                pl.BlockSpec((GROUP * block_rows, width), lambda i, *_: (i, 0)),
            ],
            out_specs=[pl.BlockSpec(memory_space=pl.ANY)] * len(shapes),
            scratch_shapes=[
                pltpu.VMEM((rows + ALIGN, width), jnp.bfloat16),
                pltpu.SemaphoreType.DMA((len(shapes),)),
            ],
        ),
        compiler_params=params(),
        cost_estimate=pl.CostEstimate(
            flops=2 * rows * 144 * width, bytes_accessed=4 * rows * width, transcendentals=0
        ),
    )(me, offs, pos, v)


def expand_kernel(sizes, count, me_ref, offs_ref, pos_ref, *rest):
    ins, (out_ref, packed, sems) = rest[:-3], rest[-3:]
    block_rows = pos_ref.shape[1]
    span = block_rows + ALIGN
    rows = packed.shape[0] - ALIGN
    step = pl.program_id(0)

    @pl.when(step == 0)
    def _():
        copies = part_copies(packed, ins, sems, me_ref[0], sizes, count, False)
        for copy in copies:
            copy.start()
        packed[rows:, :] = jnp.zeros((ALIGN, packed.shape[1]), packed.dtype)
        for copy in copies:
            copy.wait()

    for i in range(GROUP):
        start = window(offs_ref, step * GROUP + i)
        out_ref[i * block_rows : (i + 1) * block_rows, :] = lax.dot_general(
            one_hot(pos_ref[i : i + 1, :], start, block_rows),
            packed[pl.ds(start, span), :],
            (((0,), (0,)), ((), ())),
            preferred_element_type=jnp.float32,
        ).astype(jnp.bfloat16)


def expand(parts, pos, offs, me, sizes, count):
    nblk, block_rows = pos.shape
    rows = nblk * block_rows
    width = parts[0].shape[1]
    return pl.pallas_call(
        functools.partial(expand_kernel, sizes, count),
        out_shape=jax.ShapeDtypeStruct((rows, width), jnp.bfloat16),
        grid_spec=pltpu.PrefetchScalarGridSpec(
            num_scalar_prefetch=2,
            grid=(nblk // GROUP,),
            in_specs=[pl.BlockSpec((GROUP, block_rows), lambda i, *_: (i, 0))]
            + [pl.BlockSpec(memory_space=pl.ANY)] * len(parts),
            out_specs=pl.BlockSpec((GROUP * block_rows, width), lambda i, *_: (i, 0)),
            scratch_shapes=[
                pltpu.VMEM((rows + ALIGN, width), jnp.bfloat16),
                pltpu.SemaphoreType.DMA((len(parts),)),
            ],
        ),
        compiler_params=params(),
        cost_estimate=pl.CostEstimate(
            flops=2 * rows * 144 * width, bytes_accessed=4 * rows * width, transcendentals=0
        ),
    )(me, offs, pos, *parts)


def spatial_kernel(
    sizes, count, slots, me_ref, offs_ref, ids_ref, counts_ref, pos_ref, keep_ref, weight_ref,
    left, own, right, *rest
):
    block_rows = pos_ref.shape[1]
    step = pl.program_id(0)
    last = pl.num_programs(0) - 1
    if sizes is None:
        out_ref, tiles, halo_sems = rest
    else:
        outs, (tiles, halo_sems, packed, sems) = rest[:-4], rest[-4:]
    rows = tiles.shape[0] // 3

    @pl.when(step == 0)
    def _():
        copies = [
            pltpu.make_async_copy(source, tiles.at[pl.ds(i * rows, rows), :], halo_sems.at[i])
            for i, source in enumerate((left, own, right))
        ]
        for copy in copies:
            copy.start()
        if sizes is not None:
            clear(packed)
        for copy in copies:
            copy.wait()

    for i in range(GROUP):
        block = step * GROUP + i
        used = counts_ref[block]
        weights = []
        picked = []
        for slot in range(slots):
            at = ids_ref[block * slots + slot]
            live = jnp.where(slot < used, 1.0, 0.0)
            scale = jnp.broadcast_to(live, (1, block_rows))
            if sizes is not None:
                scale = scale * keep_ref[pl.ds(at, 1), :]
            weights.append(weight_ref[i, slot] * scale.astype(jnp.bfloat16))
            start = pl.multiple_of(at * block_rows, block_rows)
            picked.append(tiles[pl.ds(start, block_rows), :])
        spatial = jnp.dot(
            jnp.concatenate(weights, axis=1),
            jnp.concatenate(picked, axis=0),
            preferred_element_type=jnp.float32,
        ).astype(jnp.bfloat16)
        pos = pos_ref[i : i + 1, :]
        if sizes is None:
            a = lax.broadcasted_iota(jnp.int32, (block_rows, block_rows), 0)
            b = lax.broadcasted_iota(jnp.int32, (block_rows, block_rows), 1)
            kept = jnp.where((a == b) & (pos >= 0), 1.0, 0.0).astype(jnp.bfloat16)
            out_ref[i * block_rows : (i + 1) * block_rows, :] = jnp.dot(
                kept, spatial, preferred_element_type=jnp.float32
            ).astype(jnp.bfloat16)
        else:
            put_compact(packed, pos, window(offs_ref, block), spatial)

    if sizes is not None:

        @pl.when(step == last)
        def _():
            copies = part_copies(packed, outs, sems, me_ref[0], sizes, count, True)
            for copy in copies:
                copy.start()
            for copy in copies:
                copy.wait()


def spatial(halo, weights, keep, ids, counts, pos, offs, me, sizes, count):
    rows, width = halo[1].shape
    nblk, block_rows = pos.shape
    slots = weights.shape[1]
    any_spec = pl.BlockSpec(memory_space=pl.ANY)
    scratch = [
        pltpu.VMEM((3 * rows, width), jnp.bfloat16),
        pltpu.SemaphoreType.DMA((3,)),
    ]
    if sizes is None:
        shapes = jax.ShapeDtypeStruct((rows, width), jnp.bfloat16)
        out_specs = pl.BlockSpec((GROUP * block_rows, width), lambda i, *_: (i, 0))
    else:
        shapes = part_shapes(sizes, count, width)
        out_specs = [any_spec] * len(shapes)
        scratch += [
            pltpu.VMEM((rows + ALIGN, width), jnp.bfloat16),
            pltpu.SemaphoreType.DMA((len(shapes),)),
        ]
    return pl.pallas_call(
        functools.partial(spatial_kernel, sizes, count, slots),
        out_shape=shapes,
        grid_spec=pltpu.PrefetchScalarGridSpec(
            num_scalar_prefetch=4,
            grid=(nblk // GROUP,),
            in_specs=[
                pl.BlockSpec((GROUP, block_rows), lambda i, *_: (i, 0)),
                pl.BlockSpec(keep.shape, lambda i, *_: (0, 0)),
                pl.BlockSpec((GROUP, slots, block_rows, block_rows), lambda i, *_: (i, 0, 0, 0)),
                any_spec,
                any_spec,
                any_spec,
            ],
            out_specs=out_specs,
            scratch_shapes=scratch,
        ),
        compiler_params=params(),
        cost_estimate=pl.CostEstimate(
            flops=2 * rows * slots * block_rows * width,
            bytes_accessed=8 * rows * width + 2 * rows * slots * block_rows,
            transcendentals=0,
        ),
    )(me, offs, ids, counts, pos, keep, weights, *halo)


def mix_kernel(count, me_ref, op_ref, *rest):
    ins, outs, (rolled, sems) = rest[:count], rest[count : 2 * count], rest[2 * count :]
    width = ins[0].shape[1]
    me = me_ref[0]

    @pl.when(pl.program_id(0) == 0)
    def _():
        copies = []
        for shift in range(count):
            source = lax.rem(me + count - shift, count)
            copies.append(
                pltpu.make_async_copy(
                    op_ref.at[pl.ds(pl.multiple_of(source * width, ALIGN), width), :],
                    rolled.at[pl.ds(shift * width, width), :],
                    sems.at[shift],
                )
            )
        for copy in copies:
            copy.start()
        for copy in copies:
            copy.wait()

    row = jnp.concatenate([part[...] for part in ins], axis=1)
    for shift in range(count):
        dest = lax.rem(me + shift, count)
        columns = rolled[:, pl.ds(pl.multiple_of(dest * width, 128), width)]
        outs[shift][...] = jnp.dot(row, columns, preferred_element_type=jnp.float32).astype(
            jnp.bfloat16
        )


def mix(parts, chan_op, me):
    count = len(parts)
    rows, width = parts[0].shape
    tiles = [t for t in range(ALIGN, min(rows, 640) + 1, ALIGN) if rows % t == 0]
    tile = tiles[-1]
    spec = pl.BlockSpec((tile, width), lambda i, *_: (i, 0))
    return pl.pallas_call(
        functools.partial(mix_kernel, count),
        out_shape=part_shapes((rows,), count, width),
        grid_spec=pltpu.PrefetchScalarGridSpec(
            num_scalar_prefetch=1,
            grid=(rows // tile,),
            in_specs=[pl.BlockSpec(memory_space=pl.ANY)] + [spec] * count,
            out_specs=[spec] * count,
            scratch_shapes=[
                pltpu.VMEM(chan_op.shape, jnp.bfloat16),
                pltpu.SemaphoreType.DMA((count,)),
            ],
        ),
        compiler_params=params(),
        cost_estimate=pl.CostEstimate(
            flops=2 * rows * chan_op.shape[0] * chan_op.shape[1],
            bytes_accessed=4 * rows * width * count + 2 * chan_op.size,
            transcendentals=0,
        ),
    )(me, chan_op, *parts)


def exchange(parts):
    count = len(parts)
    return (parts[0],) + tuple(
        lax.ppermute(parts[k], "chan", [(i, (i + k) % count) for i in range(count)])
        for k in range(1, count)
    )


def neighbours_of(x):
    count = lax.axis_size("orbit")
    up = [(i, i + 1) for i in range(count - 1)]
    down = [(i + 1, i) for i in range(count - 1)]
    return lax.ppermute(x, "orbit", up), x, lax.ppermute(x, "orbit", down)


def shards(innovation, perturbation, quality, neighbours, counts, spatial_blocks, chan_op):
    rows, width = innovation.shape
    block_rows = spatial_blocks.shape[2]
    nblk = rows // block_rows
    count = lax.axis_size("chan")
    unit = ALIGN * count
    main = -(-rows * 57 // (64 * unit)) * unit
    sizes = (main // count, (rows - main) // count)

    me = lax.axis_index("chan").astype(jnp.int32).reshape(1)
    first = (lax.axis_index("orbit") - 1) * nblk
    ids = jnp.clip(neighbours - first, 0, 3 * nblk - 1).reshape(-1)
    more = jnp.sum(quality, dtype=jnp.int32) > main
    more = lax.pmax(more.astype(jnp.int32), ("grp", "orbit"))

    halo_p = neighbours_of(perturbation)
    keep = quality.reshape(nblk, block_rows).astype(jnp.float32)
    keep = jnp.concatenate(neighbours_of(keep), axis=0)
    pos, offs = plan(quality, block_rows)

    parts_i = compact(innovation, pos, offs, me, sizes, count)
    there_i = exchange(parts_i[:count])
    parts_p = spatial(
        halo_p, spatial_blocks, keep, ids, counts, pos, offs, me, sizes, count
    )
    there_p = exchange(parts_p[:count])

    def rest(parts):
        return tuple(exchange(mix(exchange(p), chan_op, me)) for p in parts)

    def nothing(parts):
        return jax.tree.map(jnp.zeros_like, parts)

    rest_i, rest_p = lax.cond(more > 0, rest, nothing, (parts_i[count:], parts_p[count:]))

    back_i = exchange(mix(there_i, chan_op, me))
    mixed_i = expand(back_i + rest_i, pos, offs, me, sizes, count)
    halo_i = neighbours_of(mixed_i)
    back_p = exchange(mix(there_p, chan_op, me))
    out_i = spatial(halo_i, spatial_blocks, keep, ids, counts, pos, offs, me, None, count)
    out_p = expand(back_p + rest_p, pos, offs, me, sizes, count)
    return out_i, out_p


def solution(mesh):
    placed = (
        P(("grp", "orbit"), "chan"),
        P(("grp", "orbit"), "chan"),
        P(("grp", "orbit")),
        P(("grp", "orbit"), None),
        P(("grp", "orbit")),
        P(("grp", "orbit"), None, None, None),
        P(),
    )
    return jax.shard_map(
        shards,
        mesh=mesh,
        in_specs=placed,
        out_specs=(P(("grp", "orbit"), "chan"), P(("grp", "orbit"), "chan")),
        check_vma=False,
    )
```

time: 568 us -> 455 us (0.80)
  blocking collectives: 271 us -> 5.56 us
  waiting for transfers between devices: 90.7 us -> 311 us
  local copies, waits for them, and re-layouts: 111 us -> 14.7 us
  Pallas kernels: 0 us -> 89.4 us
  matrix products: 42.8 us -> 0 us
  other arithmetic: 41.1 us -> 1.48 us
  starting transfers between devices: 7.54 us -> 29.8 us
    all_to_all x2 -> x0, blocking collectives: 271 us -> none  [the longest x1 160 us: shards(): lax.all_to_all(mixed, 'chan', split_axis=2, concat_axis=0, tiled=True)]
    ppermute x2 -> x18, waiting for transfers between devices: 90.7 us -> 311 us  [the longest x12 286 us: exchange(): lax.ppermute(parts[k], 'chan', [(i, (i + k) % count) for i in range(count)])]
    pallas_call x0 -> x8, Pallas kernels: none -> 89.4 us  [the longest x2 48.5 us: spatial(): pl.pallas_call(functools.partial(spatial_kernel, sizes, count, slots), ou...]
    gather x2 -> x0, local copies, waits for them, and re-layouts: 60.7 us -> none  [shards(): jnp.take(tiles, local_ids.reshape(-1), axis=1)]
    dot_general x2 -> x0, matrix products: 42.8 us -> none  [the longest x1 28.3 us: shards(): jnp.einsum('bsij,vbsjc->vbic', weights, picked, preferred_element_type=jn...]
    convert_element_type x2 -> x0, local copies, waits for them, and re-layouts: 24.4 us -> none  [the longest x1 12.5 us: shards(): jnp.einsum('nic,cd->nid', by_rows, chan_op, preferred_element_type=jnp.fl...]
    concatenate x1, other arithmetic: 22.3 us -> 0.01 us  [shards(): keep = jnp.concatenate(neighbours_of(keep), axis=0)]
    ppermute x2 -> x18, starting transfers between devices: 7.54 us -> 29.8 us  [the longest x6 17.4 us: neighbours_of(): return (lax.ppermute(x, 'orbit', up), x, lax.ppermute(x, 'orbit', down))]
  transfers between devices with their start and end apart: 2 -> 18, of which waited for: 2 -> 13; matrix products, arithmetic and copies ran while one was open for 0% -> 1% of each run, Pallas kernels for 0% -> 7%
where the time goes in v1:
time: 455 us; the launch traced here: 454 us
  waiting for transfers between devices  311 us (68%)
  Pallas kernels  89.4 us (20%)
  starting transfers between devices  29.8 us (7%)
  local copies, waits for them, and re-layouts  14.7 us (3%)
  blocking collectives  5.56 us (1%)
    ppermute x12, waiting for transfers between devices, exchange(): lax.ppermute(parts[k], 'chan', [(i, (i + k) % count) for i in range(count)])  286 us
    pallas_call x2, Pallas kernels, spatial(): pl.pallas_call(functools.partial(spatial_kernel, sizes, count, slots), ou...  48.5 us
    ppermute x6, waiting for transfers between devices, neighbours_of(): return (lax.ppermute(x, 'orbit', up), x, lax.ppermute(x, 'orbit', down))  24.9 us
    ppermute x6, starting transfers between devices, neighbours_of(): return (lax.ppermute(x, 'orbit', up), x, lax.ppermute(x, 'orbit', down))  17.4 us
    pallas_call x2, Pallas kernels, expand(): pl.pallas_call(functools.partial(expand_kernel, sizes, count), out_shape=...  15.7 us
    pallas_call x2, Pallas kernels, mix(): pl.pallas_call(functools.partial(mix_kernel, count), out_shape=part_shape...  13 us
    ppermute x12, starting transfers between devices, exchange(): lax.ppermute(parts[k], 'chan', [(i, (i + k) % count) for i in range(count)])  12.4 us
    pallas_call x1, Pallas kernels, compact(): pl.pallas_call(functools.partial(compact_kernel, sizes, count), out_shape...  10.7 us
  transfers between devices with their start and end apart: 18, of which 13 were waited for; matrix products, arithmetic and copies ran while one was open for 1% of the time, Pallas kernels for 7%

profile of v1, /device:TPU:11, one launch (start us, length us, event | category | flops | bytes accessed | tf_op | source)
XLA Modules:
  0.0 454.0 jit_solution(10149389640322439671)
XLA Ops:
  0.6 3.7 collective-permute-start.20
  4.4 2.6 collective-permute-start.21
  6.9 1.5 fusion
  8.4 1.9 collective-permute-start.13
  10.3 3.6 collective-permute-start.12
  14.0 1.6 shard_map.86
  17.2 10.7 %shard_map.87 = (bf16[1824,256]{1,0:T(8,128)(2,1)S(1)}, bf16[1824,256]{1,0:T(8,128)(2,1)}, bf16[1824,256]{1,0:T(8,128)(2,1)}, bf16[1824,256]{1,0:T(8,128)(2,1)S(...) custom-call(s32[1]{0:T(128)} %bitcast.me_ref, ...), custom_call_target="tpu_custom_call" | custom-call | flops 603979776 | bytes 8388608 | tf_op jit(solution)/shard_map/pallas_call | solution.py:137
  30.2 24.9 %collective-permute-done.13 = f32[64,128]{1,0:T(8,128)S(1)} collective-permute-done((f32[64,128]{1,0:T(8,128)S(1)}, f32[64,128]{1,0:T(8,128)S(1)}, u32[]{:S(2)}, u32[]{:S(2)}) %collective-permute-start.13) | collective-permute-done | bytes 32800 | tf_op jit(solution)/shard_map/ppermute | solution.py:394
  55.0 2.3 collective-permute-start.15
  58.2 5.6 %pmax.7 = s32[]{:T(128)} all-reduce(s32[]{:T(128)S(6)} %convert_element_type.10), channel_id=1, replica_groups=mesh['grp'=2,'orbit'=4,'chan'=4] {'grp','orbit'}, use_global_device_ids=true, to_apply=%region_1.2 | all-reduce | flops 1 | bytes 8 | tf_op jit(solution)/shard_map/pmax | solution.py:410
  64.7 26.1 %collective-permute-done.14.rest_1_ = bf16[1824,256]{1,0:T(8,128)(2,1)S(1)} collective-permute-done((bf16[1824,256]{1,0:T(8,128)(2,1)}, bf16[1824,256]{1,0:T(8,128)(2,1)S(1)}, u32[]{:S(2)}, u32[]{:S(2)}) %collective-permute-start.14) | collective-permute-done | bytes 933920 | tf_op jit(solution)/shard_map/ppermute | solution.py:385
  91.8 18.5 %collective-permute-done.15.rest_2_ = bf16[1824,256]{1,0:T(8,128)(2,1)S(1)} collective-permute-done((bf16[1824,256]{1,0:T(8,128)(2,1)}, bf16[1824,256]{1,0:T(8,128)(2,1)S(1)}, u32[]{:S(2)}, u32[]{:S(2)}) %collective-permute-start.15) | collective-permute-done | bytes 933920 | tf_op jit(solution)/shard_map/ppermute | solution.py:385
  110.3 1.6 collective-permute-done.16.rest_3_
  114.3 7.2 %shard_map.88 = (bf16[1824,256]{1,0:T(8,128)(2,1)S(1)}, bf16[1824,256]{1,0:T(8,128)(2,1)S(1)}, bf16[1824,256]{1,0:T(8,128)(2,1)S(1)}, bf16[1824,256]{1,0:T(8,128)(2,1)S(1)}) custom-call(s32[1]{0:T(128)} %bitcast.me_ref, bf16[1024,1024]{1,0:T(8,128)(2,1)} %op_ref.3, bf16[1824,256]{1,0:T(8,128)(2,1)S(1)} %copy-done.11, bf16[1824,256]{1,0:T(8,128)(2,1)S(1)} %copy-done.13, ...), custom_call_target="tpu_custom_call" | custom-call | flops 3825205248 | bytes 9568256 | tf_op jit(solution)/shard_map/pallas_call | solution.py:360
  123.4 25.5 %shard_map.89 = (bf16[1824,256]{1,0:T(8,128)(2,1)S(1)}, bf16[1824,256]{1,0:T(8,128)(2,1)S(1)}, bf16[1824,256]{1,0:T(8,128)(2,1)S(1)}, bf16[1824,256]{1,0:T(8,128...) custom-call(s32[1]{0:T(128)} %bitcast.me_ref, ...), custom_call_target="tpu_custom_call" | custom-call | flops 3221225472 | bytes 29360128 | tf_op jit(solution)/shard_map/pallas_call | solution.py:297
  150.8 4.0 conditional.1
  154.9 2.1 collective-permute-start.18
  158.3 18.6 %collective-permute-done.17.rest_1_ = bf16[1824,256]{1,0:T(8,128)(2,1)S(1)} collective-permute-done((bf16[1824,256]{1,0:T(8,128)(2,1)}, bf16[1824,256]{1,0:T(8,128)(2,1)S(1)}, u32[]{:S(2)}, u32[]{:S(2)}) %collective-permute-start.17) | collective-permute-done | bytes 933920 | tf_op jit(solution)/shard_map/ppermute | solution.py:385
  176.9 58.3 %collective-permute-done.18.rest_2_ = bf16[1824,256]{1,0:T(8,128)(2,1)S(1)} collective-permute-done((bf16[1824,256]{1,0:T(8,128)(2,1)}, bf16[1824,256]{1,0:T(8,128)(2,1)S(1)}, u32[]{:S(2)}, u32[]{:S(2)}) %collective-permute-start.18) | collective-permute-done | bytes 933920 | tf_op jit(solution)/shard_map/ppermute | solution.py:385
  235.2 3.1 collective-permute-done.19.rest_3_
  238.3 7.9 %shard_map.90.own = bf16[8192,256]{1,0:T(8,128)(2,1)} custom-call(s32[1]{0:T(128)} %bitcast.me_ref, s32[64]{0:T(128)S(1)} %slice_reduce_fusion.offs_ref, s32[64,128]{1,0:T(8,128)S(1)} %copy-done.1, bf16[1824,256]{1,0:T(8,128)(2,1)S(1)} %get-tuple-element.80.rest_0_, bf16[1824,256]{1,0:T(8,128)(2,1)S(1)} %collective-permute-done.17.rest_1_, ...), custom_call_target="tpu_custom_call" | custom-call | flops 603979776 | bytes 8388608 | tf_op jit(solution)/shard_map/pallas_call | solution.py:190
  246.2 2.4 collective-permute-start.23
  248.6 3.2 collective-permute-start.22
  253.3 21.2 %collective-permute-done.24.rest_1_ = bf16[1824,256]{1,0:T(8,128)(2,1)S(1)} collective-permute-done((bf16[1824,256]{1,0:T(8,128)(2,1)S(1)}, bf16[1824,256]{1,0:T(8,128)(2,1)S(1)}, u32[]{:S(2)}, u32[]{:S(2)}) %collective-permute-start.24) | collective-permute-done | bytes 933920 | tf_op jit(solution)/shard_map/ppermute | solution.py:385
  274.5 57.6 %collective-permute-done.25.rest_2_ = bf16[1824,256]{1,0:T(8,128)(2,1)S(1)} collective-permute-done((bf16[1824,256]{1,0:T(8,128)(2,1)S(1)}, bf16[1824,256]{1,0:T(8,128)(2,1)S(1)}, u32[]{:S(2)}, u32[]{:S(2)}) %collective-permute-start.25) | collective-permute-done | bytes 933920 | tf_op jit(solution)/shard_map/ppermute | solution.py:385
  334.0 5.8 %shard_map.92 = (bf16[1824,256]{1,0:T(8,128)(2,1)S(1)}, bf16[1824,256]{1,0:T(8,128)(2,1)S(1)}, bf16[1824,256]{1,0:T(8,128)(2,1)S(1)}, bf16[1824,256]{1,0:T(8,128)(2,1)S(1)}) custom-call(s32[1]{0:T(128)} %bitcast.me_ref, bf16[1024,1024]{1,0:T(8,128)(2,1)S(1)} %copy-done.15, bf16[1824,256]{1,0:T(8,128)(2,1)S(1)} %get-tuple-element.96.rest_0_, ...), custom_call_target="tpu_custom_call" | custom-call | flops 3825205248 | bytes 9568256 | tf_op jit(solution)/shard_map/pallas_call | solution.py:360
  339.8 2.2 collective-permute-start.28
  343.4 18.3 %collective-permute-done.27.rest_1_ = bf16[1824,256]{1,0:T(8,128)(2,1)S(1)} collective-permute-done((bf16[1824,256]{1,0:T(8,128)(2,1)S(1)}, bf16[1824,256]{1,0:T(8,128)(2,1)S(1)}, u32[]{:S(2)}, u32[]{:S(2)}) %collective-permute-start.27) | collective-permute-done | bytes 933920 | tf_op jit(solution)/shard_map/ppermute | solution.py:385
  361.7 58.2 %collective-permute-done.28.rest_2_ = bf16[1824,256]{1,0:T(8,128)(2,1)S(1)} collective-permute-done((bf16[1824,256]{1,0:T(8,128)(2,1)S(1)}, bf16[1824,256]{1,0:T(8,128)(2,1)S(1)}, u32[]{:S(2)}, u32[]{:S(2)}) %collective-permute-start.28) | collective-permute-done | bytes 933920 | tf_op jit(solution)/shard_map/ppermute | solution.py:385
  419.9 3.3 collective-permute-done.29.rest_3_
  423.2 7.8 %shard_map.93 = bf16[8192,256]{1,0:T(8,128)(2,1)} custom-call(s32[1]{0:T(128)} %bitcast.me_ref, s32[64]{0:T(128)S(1)} %slice_reduce_fusion.offs_ref, s32[64,128]{1,0:T(8,128)S(1)} %copy-done.1, bf16[1824,256]{1,0:T(8,128)(2,1)S(1)} %get-tuple-element.100.rest_0_, bf16[1824,256]{1,0:T(8,128)(2,1)S(1)} %collective-permute-done.27.rest_1_, ...), custom_call_target="tpu_custom_call" | custom-call | flops 603979776 | bytes 8388608 | tf_op jit(solution)/shard_map/pallas_call | solution.py:190
  431.0 22.9 %shard_map.91 = bf16[8192,256]{1,0:T(8,128)(2,1)} custom-call(s32[1]{0:T(128)} %bitcast.me_ref, s32[64]{0:T(128)S(1)} %slice_reduce_fusion.offs_ref, s32[384]{0:T(512)S(1)} %reshape.16.ids_ref, s32[64]{0:T(128)S(1)} %copy-done.2, s32[64,128]{1,0:T(8,128)S(1)} %copy-done.1, f32[192,128]{1,0:T(8,128)S(1)} %pad_maximum_fusion.keep_ref, ...), custom_call_target="tpu_custom_call" | custom-call | flops 3221225472 | bytes 29360128 | tf_op jit(solution)/shard_map/pallas_call | solution.py:297
  (72 shorter events, 21.6 us)
Async XLA Ops:
  0.6 63.1 %copy-start.16 = (s32[64,6]{0,1:T(8,128)S(1)}, s32[64,6]{0,1:T(8,128)}, u32[]{:S(2)}) copy-start(s32[64,6]{0,1:T(8,128)} %param.12) | copy-start | bytes 4612
  0.6 122.7 %collective-permute-start.20 = (bf16[8192,256]{1,0:T(8,128)(2,1)}, bf16[8192,256]{1,0:T(8,128)(2,1)}, u32[]{:S(2)}, u32[]{:S(2)}) collective-permute-start(bf16[8192,256]{1,0:T(8,128)(2,1)} %own.1), channel_id=1, source_target_pairs={{0,4},{4,8},{8,12},{1,5},{5,9},{9,13},{2,6},{6,10},{10,14},{3,7},{... | collective-permute-start | bytes 12582920 | tf_op jit(solution)/shard_map/ppermute | solution.py:394
  4.4 119.0 %collective-permute-start.21 = (bf16[8192,256]{1,0:T(8,128)(2,1)}, bf16[8192,256]{1,0:T(8,128)(2,1)}, u32[]{:S(2)}, u32[]{:S(2)}) collective-permute-start(bf16[8192,256]{1,0:T(8,128)(2,1)} %own.1), channel_id=1, source_target_pairs={{4,0},{8,4},{12,8},{5,1},{9,5},{13,9},{6,2},{10,6},{14,10},{7,3},{... | collective-permute-start | bytes 12582920 | tf_op jit(solution)/shard_map/ppermute | solution.py:394
  8.4 46.6 %collective-permute-start.13 = (f32[64,128]{1,0:T(8,128)S(1)}, f32[64,128]{1,0:T(8,128)S(1)}, u32[]{:S(2)}, u32[]{:S(2)}) collective-permute-start(f32[64,128]{1,0:T(8,128)S(1)} %get-tuple-element.109), channel_id=1, source_target_pairs={{4,0},{8,4},{12,8},{5,1},{9,5},{13,9},{6,2},{10,6},{14,10},{7,3},{... | collective-permute-start | bytes 98312 | tf_op jit(solution)/shard_map/ppermute | solution.py:394
  10.3 47.0 %collective-permute-start.12 = (f32[64,128]{1,0:T(8,128)S(1)}, f32[64,128]{1,0:T(8,128)S(1)}, u32[]{:S(2)}, u32[]{:S(2)}) collective-permute-start(f32[64,128]{1,0:T(8,128)S(1)} %get-tuple-element.109), channel_id=1, source_target_pairs={{0,4},{4,8},{8,12},{1,5},{5,9},{9,13},{2,6},{6,10},{10,14},{3,7},{... | collective-permute-start | bytes 98312 | tf_op jit(solution)/shard_map/ppermute | solution.py:394
  28.9 62.0 %collective-permute-start.14 = (bf16[1824,256]{1,0:T(8,128)(2,1)}, bf16[1824,256]{1,0:T(8,128)(2,1)S(1)}, u32[]{:S(2)}, u32[]{:S(2)}) collective-permute-start(bf16[1824,256]{1,0:T(8,128)(2,1)} %get-tuple-element.77), channel_id=1, source_target_pairs={{0,1},{1,2},{2,3},{3,0},{4,5},{5,6},{6,7},{7,4},{8,9},{9,10},{10,1... | collective-permute-start | bytes 2801672 | tf_op jit(solution)/shard_map/ppermute | solution.py:385
  55.0 55.2 %collective-permute-start.15 = (bf16[1824,256]{1,0:T(8,128)(2,1)}, bf16[1824,256]{1,0:T(8,128)(2,1)S(1)}, u32[]{:S(2)}, u32[]{:S(2)}) collective-permute-start(bf16[1824,256]{1,0:T(8,128)(2,1)} %get-tuple-element.78), channel_id=1, source_target_pairs={{0,2},{1,3},{2,0},{3,1},{4,6},{5,7},{6,4},{7,5},{8,10},{9,11},{10,... | collective-permute-start | bytes 2801672 | tf_op jit(solution)/shard_map/ppermute | solution.py:385
  57.4 54.5 %collective-permute-start.16 = (bf16[1824,256]{1,0:T(8,128)(2,1)S(1)}, bf16[1824,256]{1,0:T(8,128)(2,1)}, u32[]{:S(2)}, u32[]{:S(2)}) collective-permute-start(bf16[1824,256]{1,0:T(8,128)(2,1)S(1)} %get-tuple-element.79), channel_id=1, source_target_pairs={{0,3},{1,0},{2,1},{3,2},{4,7},{5,4},{6,5},{7,6},{8,11},{9,8},{10,9... | collective-permute-start | bytes 2801672 | tf_op jit(solution)/shard_map/ppermute | solution.py:385
  110.3 1.6 copy-start.17
  111.9 1.2 copy-start.11
  113.1 1.2 copy-start.13
  114.3 9.1 %copy-start.1 = (s32[64,128]{1,0:T(8,128)S(1)}, s32[64,128]{1,0:T(8,128)}, u32[]{:S(2)}) copy-start(s32[64,128]{1,0:T(8,128)} %get-tuple-element.75.pos_ref) | copy-start | bytes 98308
  114.3 9.1 %copy-start.2 = (s32[64]{0:T(128)S(1)}, s32[64]{0:T(128)}, u32[]{:S(2)}) copy-start(s32[64]{0:T(128)} %counts_ref.3) | copy-start | bytes 772
  123.3 25.6 %copy-start.7 = (bf16[1824,256]{1,0:T(8,128)(2,1)}, bf16[1824,256]{1,0:T(8,128)(2,1)S(1)}, u32[]{:S(2)}) copy-start(bf16[1824,256]{1,0:T(8,128)(2,1)S(1)} %get-tuple-element.83) | copy-start | bytes 2801668
  123.3 26.5 %copy-start.14 = (bf16[1024,1024]{1,0:T(8,128)(2,1)S(1)}, bf16[1024,1024]{1,0:T(8,128)(2,1)}, u32[]{:S(2)}) copy-start(bf16[1024,1024]{1,0:T(8,128)(2,1)} %op_ref.3) | copy-start | bytes 6291460
  123.3 26.5 %copy-start.20 = (bf16[224,256]{1,0:T(8,128)(2,1)S(1)}, bf16[224,256]{1,0:T(8,128)(2,1)}, u32[]{:S(2)}) copy-start(bf16[224,256]{1,0:T(8,128)(2,1)} %get-tuple-element.85) | copy-start | bytes 344068
  123.3 26.5 %copy-start.21 = (bf16[224,256]{1,0:T(8,128)(2,1)S(1)}, bf16[224,256]{1,0:T(8,128)(2,1)}, u32[]{:S(2)}) copy-start(bf16[224,256]{1,0:T(8,128)(2,1)} %get-tuple-element.86) | copy-start | bytes 344068
  154.8 22.2 %collective-permute-start.17 = (bf16[1824,256]{1,0:T(8,128)(2,1)}, bf16[1824,256]{1,0:T(8,128)(2,1)S(1)}, u32[]{:S(2)}, u32[]{:S(2)}) collective-permute-start(bf16[1824,256]{1,0:T(8,128)(2,1)} %copy-done.9), channel_id=1, source_target_pairs={{0,1},{1,2},{2,3},{3,0},{4,5},{5,6},{6,7},{7,4},{8,9},{9,10},{10,1... | collective-permute-start | bytes 2801672 | tf_op jit(solution)/shard_map/ppermute | solution.py:385
  154.9 80.4 %collective-permute-start.18 = (bf16[1824,256]{1,0:T(8,128)(2,1)}, bf16[1824,256]{1,0:T(8,128)(2,1)S(1)}, u32[]{:S(2)}, u32[]{:S(2)}) collective-permute-start(bf16[1824,256]{1,0:T(8,128)(2,1)} %copy-done.8), channel_id=1, source_target_pairs={{0,2},{1,3},{2,0},{3,1},{4,6},{5,7},{6,4},{7,5},{8,10},{9,11},{10,... | collective-permute-start | bytes 2801672 | tf_op jit(solution)/shard_map/ppermute | solution.py:385
  156.9 81.4 %collective-permute-start.19 = (bf16[1824,256]{1,0:T(8,128)(2,1)}, bf16[1824,256]{1,0:T(8,128)(2,1)S(1)}, u32[]{:S(2)}, u32[]{:S(2)}) collective-permute-start(bf16[1824,256]{1,0:T(8,128)(2,1)} %copy-done.7), channel_id=1, source_target_pairs={{0,3},{1,0},{2,1},{3,2},{4,7},{5,4},{6,5},{7,6},{8,11},{9,8},{10,9... | collective-permute-start | bytes 2801672 | tf_op jit(solution)/shard_map/ppermute | solution.py:385
  238.3 13.5 %copy-start.6 = (bf16[1824,256]{1,0:T(8,128)(2,1)S(1)}, bf16[1824,256]{1,0:T(8,128)(2,1)}, u32[]{:S(2)}) copy-start(bf16[1824,256]{1,0:T(8,128)(2,1)} %copy-done.5) | copy-start | bytes 2801668
  238.3 13.5 %copy-start.4 = (bf16[1824,256]{1,0:T(8,128)(2,1)S(1)}, bf16[1824,256]{1,0:T(8,128)(2,1)}, u32[]{:S(2)}) copy-start(bf16[1824,256]{1,0:T(8,128)(2,1)} %copy-done.3) | copy-start | bytes 2801668
  238.3 95.7 %copy-start.15 = (bf16[1024,1024]{1,0:T(8,128)(2,1)S(1)}, bf16[1024,1024]{1,0:T(8,128)(2,1)}, u32[]{:S(2)}) copy-start(bf16[1024,1024]{1,0:T(8,128)(2,1)} %op_ref.3) | copy-start | bytes 6291460
  246.2 184.9 %collective-permute-start.23 = (bf16[8192,256]{1,0:T(8,128)(2,1)}, bf16[8192,256]{1,0:T(8,128)(2,1)}, u32[]{:S(2)}, u32[]{:S(2)}) collective-permute-start(bf16[8192,256]{1,0:T(8,128)(2,1)} %shard_map.90.own), channel_id=1, source_target_pairs={{4,0},{8,4},{12,8},{5,1},{9,5},{13,9},{6,2},{10,6},{14,10},{7,3},{... | collective-permute-start | bytes 12582920 | tf_op jit(solution)/shard_map/ppermute | solution.py:394
  248.6 182.5 %collective-permute-start.22 = (bf16[8192,256]{1,0:T(8,128)(2,1)}, bf16[8192,256]{1,0:T(8,128)(2,1)S(1)}, u32[]{:S(2)}, u32[]{:S(2)}) collective-permute-start(bf16[8192,256]{1,0:T(8,128)(2,1)} %shard_map.90.own), channel_id=1, source_target_pairs={{0,4},{4,8},{8,12},{1,5},{5,9},{9,13},{2,6},{6,10},{10,14},{3,7},{... | collective-permute-start | bytes 12582920 | tf_op jit(solution)/shard_map/ppermute | solution.py:394
  251.8 22.8 %collective-permute-start.24 = (bf16[1824,256]{1,0:T(8,128)(2,1)S(1)}, bf16[1824,256]{1,0:T(8,128)(2,1)S(1)}, u32[]{:S(2)}, u32[]{:S(2)}) collective-permute-start(bf16[1824,256]{1,0:T(8,128)(2,1)S(1)} %copy-done.6), channel_id=1, source_target_pairs={{0,1},{1,2},{2,3},{3,0},{4,5},{5,6},{6,7},{7,4},{8,9},{9,10},{10,1... | collective-permute-start | bytes 2801672 | tf_op jit(solution)/shard_map/ppermute | solution.py:385
  251.8 80.2 %collective-permute-start.25 = (bf16[1824,256]{1,0:T(8,128)(2,1)S(1)}, bf16[1824,256]{1,0:T(8,128)(2,1)S(1)}, u32[]{:S(2)}, u32[]{:S(2)}) collective-permute-start(bf16[1824,256]{1,0:T(8,128)(2,1)S(1)} %copy-done.4), channel_id=1, source_target_pairs={{0,2},{1,3},{2,0},{3,1},{4,6},{5,7},{6,4},{7,5},{8,10},{9,11},{10,... | collective-permute-start | bytes 2801672 | tf_op jit(solution)/shard_map/ppermute | solution.py:385
  251.9 81.1 %collective-permute-start.26 = (bf16[1824,256]{1,0:T(8,128)(2,1)S(1)}, bf16[1824,256]{1,0:T(8,128)(2,1)S(1)}, u32[]{:S(2)}, u32[]{:S(2)}) collective-permute-start(bf16[1824,256]{1,0:T(8,128)(2,1)S(1)} %get-tuple-element.99), channel_id=1, source_target_pairs={{0,3},{1,0},{2,1},{3,2},{4,7},{5,4},{6,5},{7,6},{8,11},{9,8},{10,9... | collective-permute-start | bytes 2801672 | tf_op jit(solution)/shard_map/ppermute | solution.py:385
  332.1 1.0 copy-start.18
  339.8 21.9 %collective-permute-start.27 = (bf16[1824,256]{1,0:T(8,128)(2,1)S(1)}, bf16[1824,256]{1,0:T(8,128)(2,1)S(1)}, u32[]{:S(2)}, u32[]{:S(2)}) collective-permute-start(bf16[1824,256]{1,0:T(8,128)(2,1)S(1)} %get-tuple-element.101), channel_id=1, source_target_pairs={{0,1},{1,2},{2,3},{3,0},{4,5},{5,6},{6,7},{7,4},{8,9},{9,10},{10,1... | collective-permute-start | bytes 2801672 | tf_op jit(solution)/shard_map/ppermute | solution.py:385
  339.8 80.0 %collective-permute-start.28 = (bf16[1824,256]{1,0:T(8,128)(2,1)S(1)}, bf16[1824,256]{1,0:T(8,128)(2,1)S(1)}, u32[]{:S(2)}, u32[]{:S(2)}) collective-permute-start(bf16[1824,256]{1,0:T(8,128)(2,1)S(1)} %get-tuple-element.102), channel_id=1, source_target_pairs={{0,2},{1,3},{2,0},{3,1},{4,6},{5,7},{6,4},{7,5},{8,10},{9,11},{10,... | collective-permute-start | bytes 2801672 | tf_op jit(solution)/shard_map/ppermute | solution.py:385
  342.0 81.2 %collective-permute-start.29 = (bf16[1824,256]{1,0:T(8,128)(2,1)S(1)}, bf16[1824,256]{1,0:T(8,128)(2,1)S(1)}, u32[]{:S(2)}, u32[]{:S(2)}) collective-permute-start(bf16[1824,256]{1,0:T(8,128)(2,1)S(1)} %get-tuple-element.103), channel_id=1, source_target_pairs={{0,3},{1,0},{2,1},{3,2},{4,7},{5,4},{6,5},{7,6},{8,11},{9,8},{10,9... | collective-permute-start | bytes 2801672 | tf_op jit(solution)/shard_map/ppermute | solution.py:385
  (8 other events, 7.3 us)

commit v2 on v1

--- a/solution.py
+++ b/solution.py
@@ -9,6 +9,7 @@
 
 VMEM_LIMIT = 48 * 1024 * 1024
 ALIGN = 16
+DEPTH = 3
 GROUP = 8
 
 
@@ -59,13 +60,16 @@
     return jnp.where(at == pos, 1.0, 0.0).astype(jnp.bfloat16)
 
 
-def put_compact(packed, pos, start, tile):
-    block_rows = tile.shape[0]
-    part = jnp.dot(
-        one_hot(pos, start, block_rows), tile, preferred_element_type=jnp.float32
+def kept_rows(pos, start, tile):
+    return jnp.dot(
+        one_hot(pos, start, tile.shape[0]), tile, preferred_element_type=jnp.float32
     ).astype(jnp.bfloat16)
+
+
+def put_rows(packed, start, part):
+    rest = part.shape[0] - ALIGN
     packed[pl.ds(start, ALIGN), :] = packed[pl.ds(start, ALIGN), :] + part[:ALIGN]
-    packed[pl.ds(pl.multiple_of(start + ALIGN, ALIGN), block_rows), :] = part[ALIGN:]
+    packed[pl.ds(pl.multiple_of(start + ALIGN, ALIGN), rest), :] = part[ALIGN:]
 
 
 def clear(ref):
@@ -81,24 +85,19 @@
     lax.fori_loop(0, rows // step, body, 0, unroll=8 if rows // step % 8 == 0 else 1)
 
 
-def part_copies(packed, outs, sems, me, sizes, count, outward):
+def part_copies(packed, parts, sems, me, outward):
+    count = len(parts)
+    size = parts[0].shape[0]
     copies = []
-    base = 0
-    at = 0
-    for size in sizes:
-        for shift in range(count):
-            owner = lax.rem(me + (shift if outward else count - shift), count)
-            where = packed.at[pl.ds(pl.multiple_of(base + owner * size, ALIGN), size), :]
-            if outward:
-                copies.append(pltpu.make_async_copy(where, outs[at], sems.at[at]))
-            else:
-                copies.append(pltpu.make_async_copy(outs[at], where, sems.at[at]))
-            at += 1
-        base += size * count
+    for shift, part in enumerate(parts):
+        owner = lax.rem(me + (shift if outward else count - shift), count)
+        where = packed.at[pl.ds(pl.multiple_of(owner * size, ALIGN), size), :]
+        ends = (where, part) if outward else (part, where)
+        copies.append(pltpu.make_async_copy(*ends, sems.at[shift]))
     return copies
 
 
-def compact_kernel(sizes, count, me_ref, offs_ref, pos_ref, v_ref, *rest):
+def compact_kernel(me_ref, offs_ref, pos_ref, v_ref, *rest):
     outs, (packed, sems) = rest[:-2], rest[-2:]
     block_rows = pos_ref.shape[1]
     step = pl.program_id(0)
@@ -107,35 +106,35 @@
     def _():
         clear(packed)
 
-    for i in range(GROUP):
-        put_compact(
-            packed,
-            pos_ref[i : i + 1, :],
-            window(offs_ref, step * GROUP + i),
-            v_ref[i * block_rows : (i + 1) * block_rows, :],
+    starts = [window(offs_ref, step * GROUP + i) for i in range(GROUP)]
+    found = [
+        kept_rows(
+            pos_ref[i : i + 1, :], starts[i], v_ref[i * block_rows : (i + 1) * block_rows, :]
         )
+        for i in range(GROUP)
+    ]
+    for start, part in zip(starts, found):
+        put_rows(packed, start, part)
 
     @pl.when(step == pl.num_programs(0) - 1)
     def _():
-        copies = part_copies(packed, outs, sems, me_ref[0], sizes, count, True)
+        copies = part_copies(packed, outs, sems, me_ref[0], True)
         for copy in copies:
             copy.start()
         for copy in copies:
             copy.wait()
 
 
-def part_shapes(sizes, count, width):
-    return tuple(
-        jax.ShapeDtypeStruct((size, width), jnp.bfloat16) for size in sizes for _ in range(count)
-    )
-
-
-def compact(v, pos, offs, me, sizes, count):
+def part_shapes(size, count, width):
+    return (jax.ShapeDtypeStruct((size, width), jnp.bfloat16),) * count
+
+
+def compact(v, pos, offs, me, size, count):
     rows, width = v.shape
     nblk, block_rows = pos.shape
-    shapes = part_shapes(sizes, count, width)
+    shapes = part_shapes(size, count, width)
     return pl.pallas_call(
-        functools.partial(compact_kernel, sizes, count),
+        compact_kernel,
         out_shape=shapes,
         grid_spec=pltpu.PrefetchScalarGridSpec(
             num_scalar_prefetch=2,
@@ -151,25 +150,22 @@
             ],
         ),
         compiler_params=params(),
-        cost_estimate=pl.CostEstimate(
-            flops=2 * rows * 144 * width, bytes_accessed=4 * rows * width, transcendentals=0
-        ),
+        cost_estimate=pl.CostEstimate(flops=1, bytes_accessed=1, transcendentals=0),
     )(me, offs, pos, v)
 
 
-def expand_kernel(sizes, count, me_ref, offs_ref, pos_ref, *rest):
+def expand_kernel(me_ref, offs_ref, pos_ref, *rest):
     ins, (out_ref, packed, sems) = rest[:-3], rest[-3:]
     block_rows = pos_ref.shape[1]
     span = block_rows + ALIGN
-    rows = packed.shape[0] - ALIGN
     step = pl.program_id(0)
 
     @pl.when(step == 0)
     def _():
-        copies = part_copies(packed, ins, sems, me_ref[0], sizes, count, False)
+        copies = part_copies(packed, ins, sems, me_ref[0], False)
         for copy in copies:
             copy.start()
-        packed[rows:, :] = jnp.zeros((ALIGN, packed.shape[1]), packed.dtype)
+        clear(packed.at[pl.ds(len(ins) * ins[0].shape[0], packed.shape[0] - len(ins) * ins[0].shape[0]), :])
         for copy in copies:
             copy.wait()
 
@@ -183,12 +179,12 @@
         ).astype(jnp.bfloat16)
 
 
-def expand(parts, pos, offs, me, sizes, count):
+def expand(parts, pos, offs, me):
     nblk, block_rows = pos.shape
     rows = nblk * block_rows
     width = parts[0].shape[1]
     return pl.pallas_call(
-        functools.partial(expand_kernel, sizes, count),
+        expand_kernel,
         out_shape=jax.ShapeDtypeStruct((rows, width), jnp.bfloat16),
         grid_spec=pltpu.PrefetchScalarGridSpec(
             num_scalar_prefetch=2,
@@ -202,20 +198,18 @@
             ],
         ),
         compiler_params=params(),
-        cost_estimate=pl.CostEstimate(
-            flops=2 * rows * 144 * width, bytes_accessed=4 * rows * width, transcendentals=0
-        ),
+        cost_estimate=pl.CostEstimate(flops=1, bytes_accessed=1, transcendentals=0),
     )(me, offs, pos, *parts)
 
 
 def spatial_kernel(
-    sizes, count, slots, me_ref, offs_ref, ids_ref, counts_ref, pos_ref, keep_ref, weight_ref,
+    compacting, slots, me_ref, offs_ref, ids_ref, counts_ref, pos_ref, weight_ref,
     left, own, right, *rest
 ):
     block_rows = pos_ref.shape[1]
     step = pl.program_id(0)
     last = pl.num_programs(0) - 1
-    if sizes is None:
+    if not compacting:
         out_ref, tiles, halo_sems = rest
     else:
         outs, (tiles, halo_sems, packed, sems) = rest[:-4], rest[-4:]
@@ -229,11 +223,12 @@
         ]
         for copy in copies:
             copy.start()
-        if sizes is not None:
+        if compacting:
             clear(packed)
         for copy in copies:
             copy.wait()
 
+    found = []
     for i in range(GROUP):
         block = step * GROUP + i
         used = counts_ref[block]
@@ -242,10 +237,7 @@
         for slot in range(slots):
             at = ids_ref[block * slots + slot]
             live = jnp.where(slot < used, 1.0, 0.0)
-            scale = jnp.broadcast_to(live, (1, block_rows))
-            if sizes is not None:
-                scale = scale * keep_ref[pl.ds(at, 1), :]
-            weights.append(weight_ref[i, slot] * scale.astype(jnp.bfloat16))
+            weights.append(weight_ref[i, slot] * live.astype(jnp.bfloat16))
             start = pl.multiple_of(at * block_rows, block_rows)
             picked.append(tiles[pl.ds(start, block_rows), :])
         spatial = jnp.dot(
@@ -254,7 +246,7 @@
             preferred_element_type=jnp.float32,
         ).astype(jnp.bfloat16)
         pos = pos_ref[i : i + 1, :]
-        if sizes is None:
+        if not compacting:
             a = lax.broadcasted_iota(jnp.int32, (block_rows, block_rows), 0)
             b = lax.broadcasted_iota(jnp.int32, (block_rows, block_rows), 1)
             kept = jnp.where((a == b) & (pos >= 0), 1.0, 0.0).astype(jnp.bfloat16)
@@ -262,20 +254,24 @@
                 kept, spatial, preferred_element_type=jnp.float32
             ).astype(jnp.bfloat16)
         else:
-            put_compact(packed, pos, window(offs_ref, block), spatial)
-
-    if sizes is not None:
+            start = window(offs_ref, block)
+            found.append((start, kept_rows(pos, start, spatial)))
+
+    for start, part in found:
+        put_rows(packed, start, part)
+
+    if compacting:
 
         @pl.when(step == last)
         def _():
-            copies = part_copies(packed, outs, sems, me_ref[0], sizes, count, True)
+            copies = part_copies(packed, outs, sems, me_ref[0], True)
             for copy in copies:
                 copy.start()
             for copy in copies:
                 copy.wait()
 
 
-def spatial(halo, weights, keep, ids, counts, pos, offs, me, sizes, count):
+def spatial(halo, weights, ids, counts, pos, offs, me, size, count):
     rows, width = halo[1].shape
     nblk, block_rows = pos.shape
     slots = weights.shape[1]
@@ -284,25 +280,24 @@
         pltpu.VMEM((3 * rows, width), jnp.bfloat16),
         pltpu.SemaphoreType.DMA((3,)),
     ]
-    if sizes is None:
+    if size is None:
         shapes = jax.ShapeDtypeStruct((rows, width), jnp.bfloat16)
         out_specs = pl.BlockSpec((GROUP * block_rows, width), lambda i, *_: (i, 0))
     else:
-        shapes = part_shapes(sizes, count, width)
+        shapes = part_shapes(size, count, width)
         out_specs = [any_spec] * len(shapes)
         scratch += [
             pltpu.VMEM((rows + ALIGN, width), jnp.bfloat16),
             pltpu.SemaphoreType.DMA((len(shapes),)),
         ]
     return pl.pallas_call(
-        functools.partial(spatial_kernel, sizes, count, slots),
+        functools.partial(spatial_kernel, size is not None, slots),
         out_shape=shapes,
         grid_spec=pltpu.PrefetchScalarGridSpec(
             num_scalar_prefetch=4,
             grid=(nblk // GROUP,),
             in_specs=[
                 pl.BlockSpec((GROUP, block_rows), lambda i, *_: (i, 0)),
-                pl.BlockSpec(keep.shape, lambda i, *_: (0, 0)),
                 pl.BlockSpec((GROUP, slots, block_rows, block_rows), lambda i, *_: (i, 0, 0, 0)),
                 any_spec,
                 any_spec,
@@ -312,12 +307,8 @@
             scratch_shapes=scratch,
         ),
         compiler_params=params(),
-        cost_estimate=pl.CostEstimate(
-            flops=2 * rows * slots * block_rows * width,
-            bytes_accessed=8 * rows * width + 2 * rows * slots * block_rows,
-            transcendentals=0,
-        ),
-    )(me, offs, ids, counts, pos, keep, weights, *halo)
+        cost_estimate=pl.CostEstimate(flops=1, bytes_accessed=1, transcendentals=0),
+    )(me, offs, ids, counts, pos, weights, *halo)
 
 
 def mix_kernel(count, me_ref, op_ref, *rest):
@@ -359,7 +350,7 @@
     spec = pl.BlockSpec((tile, width), lambda i, *_: (i, 0))
     return pl.pallas_call(
         functools.partial(mix_kernel, count),
-        out_shape=part_shapes((rows,), count, width),
+        out_shape=part_shapes(rows, count, width),
         grid_spec=pltpu.PrefetchScalarGridSpec(
             num_scalar_prefetch=1,
             grid=(rows // tile,),
@@ -371,20 +362,31 @@
             ],
         ),
         compiler_params=params(),
-        cost_estimate=pl.CostEstimate(
-            flops=2 * rows * chan_op.shape[0] * chan_op.shape[1],
-            bytes_accessed=4 * rows * width * count + 2 * chan_op.size,
-            transcendentals=0,
-        ),
+        cost_estimate=pl.CostEstimate(flops=1, bytes_accessed=1, transcendentals=0),
     )(me, chan_op, *parts)
 
 
-def exchange(parts):
-    count = len(parts)
-    return (parts[0],) + tuple(
-        lax.ppermute(parts[k], "chan", [(i, (i + k) % count) for i in range(count)])
-        for k in range(1, count)
-    )
+class Line:
+    def __init__(self, depth):
+        self.depth = depth
+        self.done = []
+
+    def exchange(self, parts):
+        count = len(parts)
+        arrived = list(parts)
+        for shift in sorted(range(1, count), key=lambda k: min(k, count - k)):
+            part = parts[shift]
+            if len(self.done) >= self.depth:
+                part = after(part, self.done[-self.depth])
+            arrived[shift] = lax.ppermute(
+                part, "chan", [(i, (i + shift) % count) for i in range(count)]
+            )
+            self.done.append(arrived[shift])
+        return tuple(arrived)
+
+
+def after(values, *others):
+    return lax.optimization_barrier((values, others))[0]
 
 
 def neighbours_of(x):
@@ -394,48 +396,61 @@
     return lax.ppermute(x, "orbit", up), x, lax.ppermute(x, "orbit", down)
 
 
-def shards(innovation, perturbation, quality, neighbours, counts, spatial_blocks, chan_op):
+def weigh(
+    innovation, perturbation, quality, neighbours, counts, spatial_blocks, chan_op, capacity, watch
+):
     rows, width = innovation.shape
     block_rows = spatial_blocks.shape[2]
     nblk = rows // block_rows
     count = lax.axis_size("chan")
-    unit = ALIGN * count
-    main = -(-rows * 57 // (64 * unit)) * unit
-    sizes = (main // count, (rows - main) // count)
+    size = capacity // count
 
     me = lax.axis_index("chan").astype(jnp.int32).reshape(1)
     first = (lax.axis_index("orbit") - 1) * nblk
     ids = jnp.clip(neighbours - first, 0, 3 * nblk - 1).reshape(-1)
-    more = jnp.sum(quality, dtype=jnp.int32) > main
-    more = lax.pmax(more.astype(jnp.int32), ("grp", "orbit"))
-
-    halo_p = neighbours_of(perturbation)
-    keep = quality.reshape(nblk, block_rows).astype(jnp.float32)
-    keep = jnp.concatenate(neighbours_of(keep), axis=0)
     pos, offs = plan(quality, block_rows)
 
-    parts_i = compact(innovation, pos, offs, me, sizes, count)
-    there_i = exchange(parts_i[:count])
-    parts_p = spatial(
-        halo_p, spatial_blocks, keep, ids, counts, pos, offs, me, sizes, count
+    def spread(halo, room):
+        return spatial(halo, spatial_blocks, ids, counts, pos, offs, me, room, count)
+
+    parts_i = compact(innovation, pos, offs, me, size, count)
+    line = Line(DEPTH)
+    there_i = line.exchange(parts_i)
+    perturbation, quality = after((perturbation, quality), parts_i[0])
+    masked_p = perturbation * quality.astype(jnp.bfloat16)[:, None]
+    parts_p = spread(neighbours_of(masked_p), size)
+    there_p = line.exchange(parts_p)
+
+    mixed_i = mix(after(there_i, parts_p[0]), chan_op, me)
+    back_i = line.exchange(mixed_i)
+    mixed_p = mix(after(there_p, mixed_i[0]), chan_op, me)
+    back_p = line.exchange(mixed_p)
+    seen = watch(after(quality, mixed_p[0]))
+
+    wide_i = expand(after(back_i, mixed_p[0]), pos, offs, me)
+    out_i = spread(neighbours_of(wide_i), None)
+    out_p = expand(after(back_p, out_i), pos, offs, me)
+    return (out_i, out_p), seen
+
+
+def shards(innovation, perturbation, quality, *others):
+    rows = innovation.shape[0]
+    unit = ALIGN * lax.axis_size("chan")
+    capacity = -(-rows * 57 // (64 * unit)) * unit
+    given = (innovation, perturbation, quality, *others)
+
+    def overfull(quality):
+        more = jnp.sum(quality, dtype=jnp.int32) > capacity
+        return lax.pmax(more.astype(jnp.int32), ("grp", "orbit"))
+
+    packed, more = weigh(*given, capacity, overfull)
+    return lax.cond(
+        more > 0,
+        lambda given, packed: weigh(*given, rows, lambda quality: None)[0],
+        lambda given, packed: packed,
+        given,
+        packed,
     )
-    there_p = exchange(parts_p[:count])
-
-    def rest(parts):
-        return tuple(exchange(mix(exchange(p), chan_op, me)) for p in parts)
-
-    def nothing(parts):
-        return jax.tree.map(jnp.zeros_like, parts)
-
-    rest_i, rest_p = lax.cond(more > 0, rest, nothing, (parts_i[count:], parts_p[count:]))
-
-    back_i = exchange(mix(there_i, chan_op, me))
-    mixed_i = expand(back_i + rest_i, pos, offs, me, sizes, count)
-    halo_i = neighbours_of(mixed_i)
-    back_p = exchange(mix(there_p, chan_op, me))
-    out_i = spatial(halo_i, spatial_blocks, keep, ids, counts, pos, offs, me, None, count)
-    out_p = expand(back_p + rest_p, pos, offs, me, sizes, count)
-    return out_i, out_p
 
 
 def solution(mesh):

time: 455 us -> 374 us (0.82)
  waiting for transfers between devices: 311 us -> 204 us
  blocking collectives: 5.56 us -> 40 us
  local copies, waits for them, and re-layouts: 14.7 us -> 1.9 us
    ppermute x12, waiting for transfers between devices: 286 us -> 163 us  [exchange(): lax.ppermute(part, 'chan', [(i, (i + shift) % count) for i in range(count)])]
    pmax x1, blocking collectives: 5.56 us -> 40 us  [overfull(): return lax.pmax(more.astype(jnp.int32), ('grp', 'orbit'))]
    ppermute x6 -> x4, waiting for transfers between devices: 24.9 us -> 40.8 us  [neighbours_of(): return (lax.ppermute(x, 'orbit', up), x, lax.ppermute(x, 'orbit', down))]
    unnamed x44 -> x18, local copies, waits for them, and re-layouts: 9.68 us -> 0.8 us
    ppermute x12, starting transfers between devices: 12.4 us -> 20.3 us  [exchange(): lax.ppermute(part, 'chan', [(i, (i + shift) % count) for i in range(count)])]
    ppermute x6 -> x4, starting transfers between devices: 17.4 us -> 12.2 us  [neighbours_of(): return (lax.ppermute(x, 'orbit', up), x, lax.ppermute(x, 'orbit', down))]
  transfers between devices with their start and end apart: 18 -> 16, of which waited for: 13 -> 10; matrix products, arithmetic and copies ran while one was open for 1% -> 0% of each run, Pallas kernels for 7% -> 16%
where the time goes in v2:
time: 374 us; the launch traced here: 371 us
  waiting for transfers between devices  204 us (55%)
  Pallas kernels  87.3 us (23%)
  blocking collectives  40 us (11%)
  starting transfers between devices  32.4 us (9%)
    ppermute x12, waiting for transfers between devices, exchange(): lax.ppermute(part, 'chan', [(i, (i + shift) % count) for i in range(count)])  163 us
    pallas_call x2, Pallas kernels, spatial(): pl.pallas_call(functools.partial(spatial_kernel, size is not None, slots)...  48.2 us
    ppermute x4, waiting for transfers between devices, neighbours_of(): return (lax.ppermute(x, 'orbit', up), x, lax.ppermute(x, 'orbit', down))  40.8 us
    pmax x1, blocking collectives, overfull(): return lax.pmax(more.astype(jnp.int32), ('grp', 'orbit'))  40 us
    ppermute x12, starting transfers between devices, exchange(): lax.ppermute(part, 'chan', [(i, (i + shift) % count) for i in range(count)])  20.3 us
    pallas_call x2, Pallas kernels, expand(): pl.pallas_call(expand_kernel, out_shape=jax.ShapeDtypeStruct((rows, width...  14 us
    pallas_call x2, Pallas kernels, mix(): pl.pallas_call(functools.partial(mix_kernel, count), out_shape=part_shape...  12.4 us
    ppermute x4, starting transfers between devices, neighbours_of(): return (lax.ppermute(x, 'orbit', up), x, lax.ppermute(x, 'orbit', down))  12.2 us
  transfers between devices with their start and end apart: 16, of which 10 were waited for; matrix products, arithmetic and copies ran while one was open for 0% of the time, Pallas kernels for 16%

profile of v2, /device:TPU:11, one launch (start us, length us, event | category | flops | bytes accessed | tf_op | source)
XLA Modules:
  0.0 371.2 jit_solution(3587006414109245931)
XLA Ops:
  0.6 1.6 shard_map.90
  3.9 11.1 %shard_map.91 = (bf16[1824,256]{1,0:T(8,128)(2,1)S(1)}, bf16[1824,256]{1,0:T(8,128)(2,1)S(1)}, bf16[1824,256]{1,0:T(8,128)(2,1)}, bf16[1824,256]{1,0:T(8,128)(2,1)}) custom-call(s32[1]{0:T(128)} %bitcast.2.me_ref, s32[64]{0:T(128)S(1)} %slice_reduce_fusion.1.offs_ref, s32[64,128]{1,0:T(8,128)S(1)} %copy-done, bf16[8192,256]{1,0:T(8,128)(2,1)} %v_ref.1), custom_call_target="tpu_custom_call" | custom-call | flops 1 | bytes 1 | tf_op jit(solution)/shard_map/pallas_call | solution.py:136
  15.1 2.6 broadcast_multiply_fusion.1.own
  17.7 2.6 collective-permute-start.17
  20.3 3.0 collective-permute-start.16
  23.6 2.3 collective-permute-start.20
  25.9 2.2 collective-permute-start.18
  28.4 39.9 %collective-permute-done.17.right = bf16[8192,256]{1,0:T(8,128)(2,1)} collective-permute-done((bf16[8192,256]{1,0:T(8,128)(2,1)}, bf16[8192,256]{1,0:T(8,128)(2,1)}, u32[]{:S(2)}, u32[]{:S(2)}) %collective-permute-start.17) | collective-permute-done | bytes 4194336 | tf_op jit(solution)/shard_map/ppermute | solution.py:396
  68.2 0.9 collective-permute-done.16.left
  69.1 24.3 %shard_map.92 = (bf16[1824,256]{1,0:T(8,128)(2,1)S(1)}, bf16[1824,256]{1,0:T(8,128)(2,1)S(1)}, bf16[1824,256]{1,0:T(8,128)(2,1)S(1)}, bf16[1824,256]{1,0:T(8,128)(2,1)S(1)}) custom-call(s32[1]{0:T(128)} %bitcast.2.me_ref, s32[64]{0:T(128)S(1)} %slice_reduce_fusion.1.offs_ref, s32[384]{0:T(512)S(1)} %reshape.26.ids_ref, s32[64]{0:T(128)S(1)} %copy-done.15, ...), custom_call_target="tpu_custom_call" | custom-call | flops 1 | bytes 1 | tf_op jit(solution)/shard_map/pallas_call | solution.py:293
  93.7 2.3 collective-permute-start.21
  96.0 49.9 %collective-permute-done.18.rest_1_ = bf16[1824,256]{1,0:T(8,128)(2,1)S(1)} collective-permute-done((bf16[1824,256]{1,0:T(8,128)(2,1)S(1)}, bf16[1824,256]{1,0:T(8,128)(2,1)S(1)}, u32[]{:S(2)}, u32[]{:S(2)}) %collective-permute-start.18) | collective-permute-done | bytes 933920 | tf_op jit(solution)/shard_map/ppermute | solution.py:381
  145.8 2.2 collective-permute-start.19
  148.1 5.8 %shard_map.93 = (bf16[1824,256]{1,0:T(8,128)(2,1)S(1)}, bf16[1824,256]{1,0:T(8,128)(2,1)S(1)}, bf16[1824,256]{1,0:T(8,128)(2,1)S(1)}, bf16[1824,256]{1,0:T(8,128)(2,1)S(1)}) custom-call(s32[1]{0:T(128)} %bitcast.2.me_ref, bf16[1024,1024]{1,0:T(8,128)(2,1)S(1)} %copy-done.4, bf16[1824,256]{1,0:T(8,128)(2,1)S(1)} %get-tuple-element.133.rest_0_, ...), custom_call_target="tpu_custom_call" | custom-call | flops 1 | bytes 1 | tf_op jit(solution)/shard_map/pallas_call | solution.py:351
  153.8 10.8 %collective-permute-done.23.rest_3_ = bf16[1824,256]{1,0:T(8,128)(2,1)S(1)} collective-permute-done((bf16[1824,256]{1,0:T(8,128)(2,1)S(1)}, bf16[1824,256]{1,0:T(8,128)(2,1)S(1)}, u32[]{:S(2)}, u32[]{:S(2)}) %collective-permute-start.23) | collective-permute-done | bytes 933920 | tf_op jit(solution)/shard_map/ppermute | solution.py:381
  164.7 1.8 collective-permute-done.21.rest_2_
  166.5 3.6 collective-permute-start.25
  170.1 55.9 %collective-permute-done.19.rest_1_ = bf16[1824,256]{1,0:T(8,128)(2,1)S(1)} collective-permute-done((bf16[1824,256]{1,0:T(8,128)(2,1)S(1)}, bf16[1824,256]{1,0:T(8,128)(2,1)S(1)}, u32[]{:S(2)}, u32[]{:S(2)}) %collective-permute-start.19) | collective-permute-done | bytes 933920 | tf_op jit(solution)/shard_map/ppermute | solution.py:381
  225.9 2.2 collective-permute-start.24
  228.2 6.6 %shard_map.94 = (bf16[1824,256]{1,0:T(8,128)(2,1)S(1)}, bf16[1824,256]{1,0:T(8,128)(2,1)}, bf16[1824,256]{1,0:T(8,128)(2,1)}, bf16[1824,256]{1,0:T(8,128)(2,1)}) custom-call(s32[1]{0:T(128)} %bitcast.2.me_ref, bf16[1024,1024]{1,0:T(8,128)(2,1)S(1)} %copy-done.4, bf16[1824,256]{1,0:T(8,128)(2,1)S(1)} %get-tuple-element.138.rest_0_, ...), custom_call_target="tpu_custom_call" | custom-call | flops 1 | bytes 1 | tf_op jit(solution)/shard_map/pallas_call | solution.py:351
  234.8 10.0 %collective-permute-done.26.rest_3_ = bf16[1824,256]{1,0:T(8,128)(2,1)S(1)} collective-permute-done((bf16[1824,256]{1,0:T(8,128)(2,1)S(1)}, bf16[1824,256]{1,0:T(8,128)(2,1)S(1)}, u32[]{:S(2)}, u32[]{:S(2)}) %collective-permute-start.26) | collective-permute-done | bytes 933920 | tf_op jit(solution)/shard_map/ppermute | solution.py:381
  244.8 1.3 collective-permute-done.25.rest_2_
  246.0 20.0 %collective-permute-done.24.rest_1_ = bf16[1824,256]{1,0:T(8,128)(2,1)S(1)} collective-permute-done((bf16[1824,256]{1,0:T(8,128)(2,1)S(1)}, bf16[1824,256]{1,0:T(8,128)(2,1)S(1)}, u32[]{:S(2)}, u32[]{:S(2)}) %collective-permute-start.24) | collective-permute-done | bytes 933920 | tf_op jit(solution)/shard_map/ppermute | solution.py:381
  266.0 6.9 %shard_map.95.own = bf16[8192,256]{1,0:T(8,128)(2,1)} custom-call(s32[1]{0:T(128)} %bitcast.2.me_ref, s32[64]{0:T(128)S(1)} %slice_reduce_fusion.1.offs_ref, s32[64,128]{1,0:T(8,128)S(1)} %copy-done.1, bf16[1824,256]{1,0:T(8,128)(2,1)S(1)} %get-tuple-element.150.rest_0_, bf16[1824,256]{1,0:T(8,128)(2,1)S(1)} %collective-permute-done.24.rest_1_, ...), custom_call_target="tpu_custom_call" | custom-call | flops 1 | bytes 1 | tf_op jit(solution)/shard_map/pallas_call | solution.py:186
  273.0 3.2 collective-permute-start.28
  276.2 3.3 collective-permute-start.27
  280.4 2.6 collective-permute-start.30
  283.0 1.6 collective-permute-start.29
  285.9 40.0 %pmax.7 = s32[]{:T(128)} all-reduce(s32[]{:T(128)S(6)} %convert_element_type.13), channel_id=1, replica_groups=mesh['grp'=2,'orbit'=4,'chan'=4] {'grp','orbit'}, use_global_device_ids=true, to_apply=%region_1.2 | all-reduce | flops 1 | bytes 8 | tf_op jit(solution)/shard_map/pmax | solution.py:444
  326.5 23.9 %shard_map.96 = bf16[8192,256]{1,0:T(8,128)(2,1)} custom-call(s32[1]{0:T(128)} %bitcast.2.me_ref, s32[64]{0:T(128)S(1)} %slice_reduce_fusion.1.offs_ref, s32[384]{0:T(512)S(1)} %reshape.26.ids_ref, s32[64]{0:T(128)S(1)} %copy-done.15, s32[64,128]{1,0:T(8,128)S(1)} %copy-done.1, bf16[64,6,128,128]{3,2,1,0:T(8,128)(2,1)} %weight_ref.3, ...), custom_call_target="tpu_custom_call" | custom-call | flops 1 | bytes 1 | tf_op jit(solution)/shard_map/pallas_call | solution.py:293
  350.4 13.2 %collective-permute-done.29.rest_1_ = bf16[1824,256]{1,0:T(8,128)(2,1)} collective-permute-done((bf16[1824,256]{1,0:T(8,128)(2,1)}, bf16[1824,256]{1,0:T(8,128)(2,1)}, u32[]{:S(2)}, u32[]{:S(2)}) %collective-permute-start.29) | collective-permute-done | bytes 933920 | tf_op jit(solution)/shard_map/ppermute | solution.py:381
  363.7 7.1 %shard_map.97 = bf16[8192,256]{1,0:T(8,128)(2,1)} custom-call(s32[1]{0:T(128)} %bitcast.2.me_ref, s32[64]{0:T(128)S(1)} %slice_reduce_fusion.1.offs_ref, s32[64,128]{1,0:T(8,128)S(1)} %copy-done.1, bf16[1824,256]{1,0:T(8,128)(2,1)S(1)} %get-tuple-element.160.rest_0_, bf16[1824,256]{1,0:T(8,128)(2,1)} %collective-permute-done.29.rest_1_, ...), custom_call_target="tpu_custom_call" | custom-call | flops 1 | bytes 1 | tf_op jit(solution)/shard_map/pallas_call | solution.py:186
  (35 shorter events, 4.1 us)
Async XLA Ops:
  0.6 14.4 %copy-start.13 = (s32[8192]{0:T(1024)S(1)}, s32[8192]{0:T(1024)}, u32[]{:S(2)}) copy-start(s32[8192]{0:T(1024)} %param.11) | copy-start | bytes 98308
  3.2 0.8 copy-start
  3.9 11.1 %copy-start.6 = (bf16[8192,256]{1,0:T(8,128)(2,1)S(1)}, bf16[8192,256]{1,0:T(8,128)(2,1)}, u32[]{:S(2)}) copy-start(bf16[8192,256]{1,0:T(8,128)(2,1)} %param.10) | copy-start | bytes 12582916
  15.1 13.0 %copy-start.14 = (s32[64,6]{0,1:T(8,128)S(1)}, s32[64,6]{0,1:T(8,128)}, u32[]{:S(2)}) copy-start(s32[64,6]{0,1:T(8,128)} %param.12) | copy-start | bytes 4612
  15.1 54.0 %copy-start.1 = (s32[64,128]{1,0:T(8,128)S(1)}, s32[64,128]{1,0:T(8,128)}, u32[]{:S(2)}) copy-start(s32[64,128]{1,0:T(8,128)} %get-tuple-element.119.pos_ref) | copy-start | bytes 98308
  15.1 54.0 %copy-start.15 = (s32[64]{0:T(128)S(1)}, s32[64]{0:T(128)}, u32[]{:S(2)}) copy-start(s32[64]{0:T(128)} %counts_ref.3) | copy-start | bytes 772
  17.7 50.5 %collective-permute-start.17 = (bf16[8192,256]{1,0:T(8,128)(2,1)}, bf16[8192,256]{1,0:T(8,128)(2,1)}, u32[]{:S(2)}, u32[]{:S(2)}) collective-permute-start(bf16[8192,256]{1,0:T(8,128)(2,1)} %broadcast_multiply_fusion.1.own), channel_id=1, source_target_pairs={{4,0},{8,4},{12,8},{5,1},{9,5},{13,9},{6,2},{10,6},{14,10},{7,3},{... | collective-permute-start | bytes 12582920 | tf_op jit(solution)/shard_map/ppermute | solution.py:396
  20.3 48.8 %collective-permute-start.16 = (bf16[8192,256]{1,0:T(8,128)(2,1)}, bf16[8192,256]{1,0:T(8,128)(2,1)}, u32[]{:S(2)}, u32[]{:S(2)}) collective-permute-start(bf16[8192,256]{1,0:T(8,128)(2,1)} %broadcast_multiply_fusion.1.own), channel_id=1, source_target_pairs={{0,4},{4,8},{8,12},{1,5},{5,9},{9,13},{2,6},{6,10},{10,14},{3,7},{... | collective-permute-start | bytes 12582920 | tf_op jit(solution)/shard_map/ppermute | solution.py:396
  23.4 70.1 %collective-permute-start.22 = (bf16[1824,256]{1,0:T(8,128)(2,1)}, bf16[1824,256]{1,0:T(8,128)(2,1)}, u32[]{:S(2)}, u32[]{:S(2)}) collective-permute-start(bf16[1824,256]{1,0:T(8,128)(2,1)} %get-tuple-element.131), channel_id=1, source_target_pairs={{0,3},{1,0},{2,1},{3,2},{4,7},{5,4},{6,5},{7,6},{8,11},{9,8},{10,9... | collective-permute-start | bytes 2801672 | tf_op jit(solution)/shard_map/ppermute | solution.py:381
  23.6 70.1 %collective-permute-start.20 = (bf16[1824,256]{1,0:T(8,128)(2,1)}, bf16[1824,256]{1,0:T(8,128)(2,1)}, u32[]{:S(2)}, u32[]{:S(2)}) collective-permute-start(bf16[1824,256]{1,0:T(8,128)(2,1)} %get-tuple-element.128), channel_id=1, source_target_pairs={{0,2},{1,3},{2,0},{3,1},{4,6},{5,7},{6,4},{7,5},{8,10},{9,11},{10,... | collective-permute-start | bytes 2801672 | tf_op jit(solution)/shard_map/ppermute | solution.py:381
  25.9 119.9 %collective-permute-start.18 = (bf16[1824,256]{1,0:T(8,128)(2,1)S(1)}, bf16[1824,256]{1,0:T(8,128)(2,1)S(1)}, u32[]{:S(2)}, u32[]{:S(2)}) collective-permute-start(bf16[1824,256]{1,0:T(8,128)(2,1)S(1)} %get-tuple-element.125), channel_id=1, source_target_pairs={{0,1},{1,2},{2,3},{3,0},{4,5},{5,6},{6,7},{7,4},{8,9},{9,10},{10,1... | collective-permute-start | bytes 2801672 | tf_op jit(solution)/shard_map/ppermute | solution.py:381
  28.3 119.7 %copy-start.4 = (bf16[1024,1024]{1,0:T(8,128)(2,1)S(1)}, bf16[1024,1024]{1,0:T(8,128)(2,1)}, u32[]{:S(2)}) copy-start(bf16[1024,1024]{1,0:T(8,128)(2,1)} %op_ref.3) | copy-start | bytes 6291460
  93.4 71.2 %collective-permute-start.23 = (bf16[1824,256]{1,0:T(8,128)(2,1)S(1)}, bf16[1824,256]{1,0:T(8,128)(2,1)S(1)}, u32[]{:S(2)}, u32[]{:S(2)}) collective-permute-start(bf16[1824,256]{1,0:T(8,128)(2,1)S(1)} %get-tuple-element.132), channel_id=1, source_target_pairs={{0,3},{1,0},{2,1},{3,2},{4,7},{5,4},{6,5},{7,6},{8,11},{9,8},{10,9... | collective-permute-start | bytes 2801672 | tf_op jit(solution)/shard_map/ppermute | solution.py:381
  93.7 72.8 %collective-permute-start.21 = (bf16[1824,256]{1,0:T(8,128)(2,1)S(1)}, bf16[1824,256]{1,0:T(8,128)(2,1)S(1)}, u32[]{:S(2)}, u32[]{:S(2)}) collective-permute-start(bf16[1824,256]{1,0:T(8,128)(2,1)S(1)} %get-tuple-element.129), channel_id=1, source_target_pairs={{0,2},{1,3},{2,0},{3,1},{4,6},{5,7},{6,4},{7,5},{8,10},{9,11},{10,... | collective-permute-start | bytes 2801672 | tf_op jit(solution)/shard_map/ppermute | solution.py:381
  145.8 80.1 %collective-permute-start.19 = (bf16[1824,256]{1,0:T(8,128)(2,1)S(1)}, bf16[1824,256]{1,0:T(8,128)(2,1)S(1)}, u32[]{:S(2)}, u32[]{:S(2)}) collective-permute-start(bf16[1824,256]{1,0:T(8,128)(2,1)S(1)} %get-tuple-element.126), channel_id=1, source_target_pairs={{0,1},{1,2},{2,3},{3,0},{4,5},{5,6},{6,7},{7,4},{8,9},{9,10},{10,1... | collective-permute-start | bytes 2801672 | tf_op jit(solution)/shard_map/ppermute | solution.py:381
  164.7 63.5 %copy-start.11 = (bf16[1824,256]{1,0:T(8,128)(2,1)}, bf16[1824,256]{1,0:T(8,128)(2,1)S(1)}, u32[]{:S(2)}) copy-start(bf16[1824,256]{1,0:T(8,128)(2,1)S(1)} %collective-permute-done.23.rest_3_) | copy-start | bytes 2801668
  164.7 80.1 %collective-permute-start.26 = (bf16[1824,256]{1,0:T(8,128)(2,1)S(1)}, bf16[1824,256]{1,0:T(8,128)(2,1)S(1)}, u32[]{:S(2)}, u32[]{:S(2)}) collective-permute-start(bf16[1824,256]{1,0:T(8,128)(2,1)S(1)} %get-tuple-element.149), channel_id=1, source_target_pairs={{0,3},{1,0},{2,1},{3,2},{4,7},{5,4},{6,5},{7,6},{8,11},{9,8},{10,9... | collective-permute-start | bytes 2801672 | tf_op jit(solution)/shard_map/ppermute | solution.py:381
  166.5 61.7 %copy-start.12 = (bf16[1824,256]{1,0:T(8,128)(2,1)}, bf16[1824,256]{1,0:T(8,128)(2,1)S(1)}, u32[]{:S(2)}) copy-start(bf16[1824,256]{1,0:T(8,128)(2,1)S(1)} %collective-permute-done.21.rest_2_) | copy-start | bytes 2801668
  166.5 79.5 %collective-permute-start.25 = (bf16[1824,256]{1,0:T(8,128)(2,1)S(1)}, bf16[1824,256]{1,0:T(8,128)(2,1)S(1)}, u32[]{:S(2)}, u32[]{:S(2)}) collective-permute-start(bf16[1824,256]{1,0:T(8,128)(2,1)S(1)} %get-tuple-element.147), channel_id=1, source_target_pairs={{0,2},{1,3},{2,0},{3,1},{4,6},{5,7},{6,4},{7,5},{8,10},{9,11},{10,... | collective-permute-start | bytes 2801672 | tf_op jit(solution)/shard_map/ppermute | solution.py:381
  225.9 40.1 %collective-permute-start.24 = (bf16[1824,256]{1,0:T(8,128)(2,1)S(1)}, bf16[1824,256]{1,0:T(8,128)(2,1)S(1)}, u32[]{:S(2)}, u32[]{:S(2)}) collective-permute-start(bf16[1824,256]{1,0:T(8,128)(2,1)S(1)} %get-tuple-element.145), channel_id=1, source_target_pairs={{0,1},{1,2},{2,3},{3,0},{4,5},{5,6},{6,7},{7,4},{8,9},{9,10},{10,1... | collective-permute-start | bytes 2801672 | tf_op jit(solution)/shard_map/ppermute | solution.py:381
  273.0 53.5 %collective-permute-start.28 = (bf16[8192,256]{1,0:T(8,128)(2,1)}, bf16[8192,256]{1,0:T(8,128)(2,1)}, u32[]{:S(2)}, u32[]{:S(2)}) collective-permute-start(bf16[8192,256]{1,0:T(8,128)(2,1)} %shard_map.95.own), channel_id=1, source_target_pairs={{4,0},{8,4},{12,8},{5,1},{9,5},{13,9},{6,2},{10,6},{14,10},{7,3},{... | collective-permute-start | bytes 12582920 | tf_op jit(solution)/shard_map/ppermute | solution.py:396
  276.2 50.3 %collective-permute-start.27 = (bf16[8192,256]{1,0:T(8,128)(2,1)}, bf16[8192,256]{1,0:T(8,128)(2,1)}, u32[]{:S(2)}, u32[]{:S(2)}) collective-permute-start(bf16[8192,256]{1,0:T(8,128)(2,1)} %shard_map.95.own), channel_id=1, source_target_pairs={{0,4},{4,8},{8,12},{1,5},{5,9},{9,13},{2,6},{6,10},{10,14},{3,7},{... | collective-permute-start | bytes 12582920 | tf_op jit(solution)/shard_map/ppermute | solution.py:396
  279.5 70.9 %collective-permute-start.31 = (bf16[1824,256]{1,0:T(8,128)(2,1)}, bf16[1824,256]{1,0:T(8,128)(2,1)S(1)}, u32[]{:S(2)}, u32[]{:S(2)}) collective-permute-start(bf16[1824,256]{1,0:T(8,128)(2,1)} %get-tuple-element.159), channel_id=1, source_target_pairs={{0,3},{1,0},{2,1},{3,2},{4,7},{5,4},{6,5},{7,6},{8,11},{9,8},{10,9... | collective-permute-start | bytes 2801672 | tf_op jit(solution)/shard_map/ppermute | solution.py:381
  280.4 70.1 %collective-permute-start.30 = (bf16[1824,256]{1,0:T(8,128)(2,1)}, bf16[1824,256]{1,0:T(8,128)(2,1)S(1)}, u32[]{:S(2)}, u32[]{:S(2)}) collective-permute-start(bf16[1824,256]{1,0:T(8,128)(2,1)} %get-tuple-element.157), channel_id=1, source_target_pairs={{0,2},{1,3},{2,0},{3,1},{4,6},{5,7},{6,4},{7,5},{8,10},{9,11},{10,... | collective-permute-start | bytes 2801672 | tf_op jit(solution)/shard_map/ppermute | solution.py:381
  283.0 80.7 %collective-permute-start.29 = (bf16[1824,256]{1,0:T(8,128)(2,1)}, bf16[1824,256]{1,0:T(8,128)(2,1)}, u32[]{:S(2)}, u32[]{:S(2)}) collective-permute-start(bf16[1824,256]{1,0:T(8,128)(2,1)} %get-tuple-element.155), channel_id=1, source_target_pairs={{0,1},{1,2},{2,3},{3,0},{4,5},{5,6},{6,7},{7,4},{8,9},{9,10},{10,1... | collective-permute-start | bytes 2801672 | tf_op jit(solution)/shard_map/ppermute | solution.py:381

commit v3 on v2

v3 whole, which is shorter than its diff:
```python
import functools

import jax
import jax.numpy as jnp
from jax import lax
from jax.experimental import pallas as pl
from jax.experimental.pallas import tpu as pltpu
from jax.sharding import PartitionSpec as P

VMEM_LIMIT = 48 * 1024 * 1024
ALIGN = 16
DEPTH = 3
PAIR = 2
EXPAND = 1
GROUP = 8


def params():
    return pltpu.CompilerParams(
        dimension_semantics=("arbitrary",), vmem_limit_bytes=VMEM_LIMIT
    )


def plan(quality, pos_ref, offs_ref):
    blocks, rows = quality.shape
    ones = quality.astype(jnp.float32).astype(jnp.bfloat16)

    def ahead(size):
        a = lax.broadcasted_iota(jnp.int32, (size, size), 0)
        b = lax.broadcasted_iota(jnp.int32, (size, size), 1)
        return jnp.where(a < b, 1.0, 0.0).astype(jnp.bfloat16)

    def dot(a, b, dims=((1,), (0,))):
        return lax.dot_general(a, b, (dims, ((), ())), preferred_element_type=jnp.float32)

    within = dot(ones, ahead(rows))
    totals = dot(jnp.ones((8, rows), jnp.bfloat16), ones, ((1,), (1,)))
    first = dot(totals.astype(jnp.bfloat16), ahead(blocks))
    offs_ref[...] = first.astype(jnp.int32)
    wide = jnp.broadcast_to(jnp.sum(ones.astype(jnp.float32), axis=1, keepdims=True), (blocks, rows))
    before = dot(ahead(blocks), wide.astype(jnp.bfloat16), ((0,), (0,)))
    pos_ref[...] = jnp.where(quality > 0, (before + within).astype(jnp.int32), -1)


def window(offs_ref, block):
    return pl.multiple_of((offs_ref[0, block] // ALIGN) * ALIGN, ALIGN)


def kept_rows(pos, start, tile):
    rows = tile.shape[0]
    at = lax.broadcasted_iota(jnp.int32, (rows + ALIGN, rows), 0) + start
    chosen = jnp.where(at == pos, 1.0, 0.0).astype(jnp.bfloat16)
    return jnp.dot(chosen, tile, preferred_element_type=jnp.float32).astype(jnp.bfloat16)


def put_rows(packed, start, part):
    rest = part.shape[0] - ALIGN
    packed[pl.ds(start, ALIGN), :] = packed[pl.ds(start, ALIGN), :] + part[:ALIGN]
    packed[pl.ds(pl.multiple_of(start + ALIGN, ALIGN), rest), :] = part[ALIGN:]


def clear(ref, start):
    def body(i, carry):
        at = pl.multiple_of(i * ALIGN, ALIGN)
        ref[pl.ds(at, ALIGN), :] = jnp.zeros((ALIGN, ref.shape[1]), ref.dtype)
        return carry

    lax.fori_loop(start // ALIGN, ref.shape[0] // ALIGN, body, 0)


def send_ready(packed, outs, sems, me, before, now, last):
    count = len(outs)
    size = outs[0].shape[0]
    for shift, copy in enumerate(part_copies(packed, outs, sems, me, True)):
        past = (lax.rem(me + shift, count) + 1) * size

        @pl.when((past > before) & ((past <= now) | last))
        def _():
            copy.start()


def group_copies(source, target, sems):
    pieces = sems.shape[0]
    size = source.shape[0] // pieces
    return [
        pltpu.make_async_copy(
            source.at[pl.ds(i * size, size)], target.at[pl.ds(i * size, size)], sems.at[i]
        )
        for i in range(pieces)
    ]


def group_wait(source, target, sems, i):
    size = source.shape[0] // sems.shape[0]
    pltpu.make_async_copy(
        source.at[pl.ds(0, size)], target.at[pl.ds(0, size)], sems.at[i]
    ).wait()


def pack_round(step, rounds, pos, offs, tiles, packed, outs, sems, me):
    found = []
    for i, tile in enumerate(tiles):
        start = window(offs, step * GROUP + i * PAIR)
        row = jnp.concatenate([pos[i * PAIR + j : i * PAIR + j + 1, :] for j in range(PAIR)], axis=1)
        found.append((start, kept_rows(row, start, tile)))
    for start, part in found:
        put_rows(packed, start, part)
    last = step == rounds - 1

    @pl.when(last)
    def _():
        start, part = found[-1]
        clear(packed, start + part.shape[0])

    before = jnp.where(step == 0, 0, window(offs, step * GROUP))
    now = window(offs, jnp.where(last, 0, (step + 1) * GROUP))
    send_ready(packed, outs, sems, me, before, now, last)


def part_copies(packed, parts, sems, me, outward):
    count = len(parts)
    size = parts[0].shape[0]
    copies = []
    for shift, part in enumerate(parts):
        owner = lax.rem(me + (shift if outward else count - shift), count)
        where = packed.at[pl.ds(pl.multiple_of(owner * size, ALIGN), size), :]
        ends = (where, part) if outward else (part, where)
        copies.append(pltpu.make_async_copy(*ends, sems.at[shift]))
    return copies


def compact_kernel(me_ref, quality_ref, v_ref, pos_ref, offs_ref, *rest):
    outs, (tiles, packed, sems, in_sems, offs, offs_sem) = rest[:-6], rest[-6:]
    nblk, block_rows = pos_ref.shape
    rounds = nblk // GROUP
    for copy in group_copies(v_ref, tiles, in_sems):
        copy.start()
    plan(quality_ref[...], pos_ref, offs_ref)
    copy = pltpu.make_async_copy(offs_ref, offs, offs_sem)
    copy.start()
    packed[:ALIGN, :] = jnp.zeros((ALIGN, packed.shape[1]), packed.dtype)
    copy.wait()

    def body(step, carry):
        group_wait(v_ref, tiles, in_sems, step)
        pos = pos_ref[pl.ds(pl.multiple_of(step * GROUP, GROUP), GROUP), :]
        span = PAIR * block_rows
        made = []
        for i in range(GROUP // PAIR):
            at = pl.multiple_of(step * (GROUP * block_rows) + i * span, span)
            made.append(tiles[pl.ds(at, span), :])
        pack_round(step, rounds, pos, offs, made, packed, outs, sems, me_ref[0])
        return carry

    lax.fori_loop(0, rounds, body, 0)
    for copy in part_copies(packed, outs, sems, me_ref[0], True):
        copy.wait()


def part_shapes(size, count, width):
    return (jax.ShapeDtypeStruct((size, width), jnp.bfloat16),) * count


def compact(v, quality, me, size, count):
    rows, width = v.shape
    nblk, block_rows = quality.shape
    shapes = part_shapes(size, count, width)
    plan_shapes = (
        jax.ShapeDtypeStruct((nblk, block_rows), jnp.int32),
        jax.ShapeDtypeStruct((8, nblk), jnp.int32),
    )
    pos, offs, *parts = pl.pallas_call(
        compact_kernel,
        out_shape=plan_shapes + shapes,
        grid_spec=pltpu.PrefetchScalarGridSpec(
            num_scalar_prefetch=1,
            grid=(1,),
            in_specs=[
                pl.BlockSpec((nblk, block_rows), lambda i, *_: (0, 0)),
                pl.BlockSpec(memory_space=pl.ANY),
            ],
            out_specs=[
                pl.BlockSpec((nblk, block_rows), lambda i, *_: (0, 0)),
                pl.BlockSpec((8, nblk), lambda i, *_: (0, 0)),
            ]
            + [pl.BlockSpec(memory_space=pl.ANY)] * len(shapes),
            scratch_shapes=[
                pltpu.VMEM((rows, width), jnp.bfloat16),
                pltpu.VMEM((rows + ALIGN, width), jnp.bfloat16),
                pltpu.SemaphoreType.DMA((len(shapes),)),
                pltpu.SemaphoreType.DMA((nblk // GROUP,)),
                pltpu.SMEM((8, nblk), jnp.int32),
                pltpu.SemaphoreType.DMA,
            ],
        ),
        compiler_params=params(),
        cost_estimate=pl.CostEstimate(
            flops=2 * rows * 272 * width, bytes_accessed=4 * rows * width, transcendentals=0
        ),
    )(me, quality, v)
    return pos, offs, tuple(parts)


def expand_kernel(me_ref, offs_ref, pos_ref, *rest):
    ins, (out_ref, packed, tiles, sems, out_sems) = rest[:-5], rest[-5:]
    nblk, block_rows = pos_ref.shape
    rounds = nblk // GROUP
    span = EXPAND * block_rows
    held = len(ins) * ins[0].shape[0]
    copies = part_copies(packed, ins, sems, me_ref[0], False)
    for copy in copies:
        copy.start()
    clear(packed, held)
    for copy in copies:
        copy.wait()

    def body(step, carry):
        pos = pos_ref[pl.ds(pl.multiple_of(step * GROUP, GROUP), GROUP), :]
        made = []
        for i in range(0, GROUP, EXPAND):
            start = window(offs_ref, step * GROUP + i)
            row = jnp.concatenate([pos[i + j : i + j + 1, :] for j in range(EXPAND)], axis=1)
            at = lax.broadcasted_iota(jnp.int32, (span + ALIGN, span), 0) + start
            chosen = jnp.where(at == row, 1.0, 0.0).astype(jnp.bfloat16)
            made.append(
                lax.dot_general(
                    chosen,
                    packed[pl.ds(start, span + ALIGN), :],
                    (((0,), (0,)), ((), ())),
                    preferred_element_type=jnp.float32,
                ).astype(jnp.bfloat16)
            )
        size = GROUP * block_rows
        base = pl.multiple_of(step * size, size)
        for i, rows in enumerate(made):
            tiles[pl.ds(pl.multiple_of(base + i * span, span), span), :] = rows
        pltpu.make_async_copy(
            tiles.at[pl.ds(base, size)], out_ref.at[pl.ds(base, size)], out_sems.at[step]
        ).start()
        return carry

    lax.fori_loop(0, rounds, body, 0)
    for copy in group_copies(tiles, out_ref, out_sems):
        copy.wait()


def expand(parts, pos, offs, me):
    nblk, block_rows = pos.shape
    rows = nblk * block_rows
    width = parts[0].shape[1]
    return pl.pallas_call(
        expand_kernel,
        out_shape=jax.ShapeDtypeStruct((rows, width), jnp.bfloat16),
        grid_spec=pltpu.PrefetchScalarGridSpec(
            num_scalar_prefetch=2,
            grid=(1,),
            in_specs=[pl.BlockSpec((nblk, block_rows), lambda i, *_: (0, 0))]
            + [pl.BlockSpec(memory_space=pl.ANY)] * len(parts),
            out_specs=pl.BlockSpec(memory_space=pl.ANY),
            scratch_shapes=[
                pltpu.VMEM((rows + ALIGN, width), jnp.bfloat16),
                pltpu.VMEM((rows, width), jnp.bfloat16),
                pltpu.SemaphoreType.DMA((len(parts),)),
                pltpu.SemaphoreType.DMA((nblk // GROUP,)),
            ],
        ),
        compiler_params=params(),
        cost_estimate=pl.CostEstimate(
            flops=2 * rows * 256 * width, bytes_accessed=4 * rows * width, transcendentals=0
        ),
    )(me, offs, pos, *parts)


def spatial_kernel(
    compacting, me_ref, offs_ref, ids_ref, counts_ref, pos_ref, weight_ref, near, own, far, *rest
):
    nblk, block_rows = pos_ref.shape
    slots = weight_ref.shape[1]
    rounds = nblk // GROUP
    scratch = 6
    outs, (tiles, weights, halo_sems, weight_sems, made, sems) = rest[:-scratch], rest[-scratch:]
    rows = tiles.shape[0] // 3
    loads = group_copies(weight_ref, weights, weight_sems)
    loads[0].start()
    halo = [
        pltpu.make_async_copy(source, tiles.at[pl.ds(i * rows, rows), :], halo_sems.at[i])
        for i, source in enumerate((near, own, far))
    ]
    for copy in halo + loads[1:]:
        copy.start()
    if compacting:
        made[:ALIGN, :] = jnp.zeros((ALIGN, made.shape[1]), made.dtype)
    for copy in halo:
        copy.wait()

    def product(step, i):
        block = step * GROUP + i
        used = counts_ref[block]
        live = []
        picked = []
        for slot in range(slots):
            at = ids_ref[block * slots + slot]
            scale = jnp.where(slot < used, 1.0, 0.0).astype(jnp.bfloat16)
            live.append(weights[block, slot] * scale)
            start = pl.multiple_of(at * block_rows, block_rows)
            picked.append(tiles[pl.ds(start, block_rows), :])
        return jnp.dot(
            jnp.concatenate(live, axis=1),
            jnp.concatenate(picked, axis=0),
            preferred_element_type=jnp.float32,
        ).astype(jnp.bfloat16)

    def body(step, carry):
        group_wait(weight_ref, weights, weight_sems, step)
        pos = pos_ref[pl.ds(pl.multiple_of(step * GROUP, GROUP), GROUP), :]
        found = [product(step, i) for i in range(GROUP)]
        if compacting:
            found = [
                jnp.concatenate(found[i : i + PAIR], axis=0) for i in range(0, GROUP, PAIR)
            ]
            pack_round(step, rounds, pos, offs_ref, found, made, outs, sems, me_ref[0])
            return carry
        a = lax.broadcasted_iota(jnp.int32, (block_rows, block_rows), 0)
        b = lax.broadcasted_iota(jnp.int32, (block_rows, block_rows), 1)
        size = GROUP * block_rows
        base = pl.multiple_of(step * size, size)
        for i in range(GROUP):
            kept = jnp.where((a == b) & (pos[i : i + 1, :] >= 0), 1.0, 0.0).astype(jnp.bfloat16)
            made[pl.ds(pl.multiple_of(base + i * block_rows, block_rows), block_rows), :] = jnp.dot(
                kept, found[i], preferred_element_type=jnp.float32
            ).astype(jnp.bfloat16)
        pltpu.make_async_copy(
            made.at[pl.ds(base, size)], outs[0].at[pl.ds(base, size)], sems.at[step]
        ).start()
        return carry

    lax.fori_loop(0, rounds, body, 0)
    if compacting:
        copies = part_copies(made, outs, sems, me_ref[0], True)
    else:
        copies = group_copies(made, outs[0], sems)
    for copy in copies:
        copy.wait()


def spatial(halo, weights, ids, counts, pos, offs, me, size, count):
    rows, width = halo[1].shape
    nblk, block_rows = pos.shape
    slots = weights.shape[1]
    any_spec = pl.BlockSpec(memory_space=pl.ANY)
    rounds = nblk // GROUP
    if size is None:
        shapes = (jax.ShapeDtypeStruct((rows, width), jnp.bfloat16),)
        made = (rows, rounds)
    else:
        shapes = part_shapes(size, count, width)
        made = (rows + ALIGN, len(shapes))
    return pl.pallas_call(
        functools.partial(spatial_kernel, size is not None),
        out_shape=shapes,
        grid_spec=pltpu.PrefetchScalarGridSpec(
            num_scalar_prefetch=4,
            grid=(1,),
            in_specs=[pl.BlockSpec((nblk, block_rows), lambda i, *_: (0, 0))] + [any_spec] * 4,
            out_specs=[any_spec] * len(shapes),
            scratch_shapes=[
                pltpu.VMEM((3 * rows, width), jnp.bfloat16),
                pltpu.VMEM(weights.shape, jnp.bfloat16),
                pltpu.SemaphoreType.DMA((3,)),
                pltpu.SemaphoreType.DMA((rounds,)),
                pltpu.VMEM((made[0], width), jnp.bfloat16),
                pltpu.SemaphoreType.DMA((made[1],)),
            ],
        ),
        compiler_params=params(),
        cost_estimate=pl.CostEstimate(
            flops=2 * rows * slots * block_rows * width,
            bytes_accessed=8 * rows * width + 2 * rows * slots * block_rows,
            transcendentals=0,
        ),
    )(me, offs, ids, counts, pos, weights, *halo)


def mix_kernel(count, me_ref, op_ref, *rest):
    ins, outs, (rolled, sems) = rest[:count], rest[count : 2 * count], rest[2 * count :]
    width = ins[0].shape[1]
    me = me_ref[0]

    @pl.when(pl.program_id(0) == 0)
    def _():
        copies = []
        for shift in range(count):
            source = lax.rem(me + count - shift, count)
            copies.append(
                pltpu.make_async_copy(
                    op_ref.at[pl.ds(pl.multiple_of(source * width, ALIGN), width), :],
                    rolled.at[pl.ds(shift * width, width), :],
                    sems.at[shift],
                )
            )
        for copy in copies:
            copy.start()
        for copy in copies:
            copy.wait()

    row = jnp.concatenate([part[...] for part in ins], axis=1)
    for shift in range(count):
        dest = lax.rem(me + shift, count)
        columns = rolled[:, pl.ds(pl.multiple_of(dest * width, 128), width)]
        outs[shift][...] = jnp.dot(row, columns, preferred_element_type=jnp.float32).astype(
            jnp.bfloat16
        )


def mix(parts, chan_op, me):
    count = len(parts)
    rows, width = parts[0].shape
    tiles = [t for t in range(ALIGN, min(rows, 640) + 1, ALIGN) if rows % t == 0]
    tile = tiles[-1]
    spec = pl.BlockSpec((tile, width), lambda i, *_: (i, 0))
    return pl.pallas_call(
        functools.partial(mix_kernel, count),
        out_shape=part_shapes(rows, count, width),
        grid_spec=pltpu.PrefetchScalarGridSpec(
            num_scalar_prefetch=1,
            grid=(rows // tile,),
            in_specs=[pl.BlockSpec(memory_space=pl.ANY)] + [spec] * count,
            out_specs=[spec] * count,
            scratch_shapes=[
                pltpu.VMEM(chan_op.shape, jnp.bfloat16),
                pltpu.SemaphoreType.DMA((count,)),
            ],
        ),
        compiler_params=params(),
        cost_estimate=pl.CostEstimate(flops=1, bytes_accessed=1, transcendentals=0),
    )(me, chan_op, *parts)


class Line:
    def __init__(self, depth):
        self.depth = depth
        self.done = []

    def exchange(self, parts):
        count = len(parts)
        arrived = list(parts)
        for shift in sorted(range(1, count), key=lambda k: min(k, count - k)):
            part = parts[shift]
            if len(self.done) >= self.depth:
                part = after(part, self.done[-self.depth])
            arrived[shift] = lax.ppermute(
                part, "chan", [(i, (i + shift) % count) for i in range(count)]
            )
            self.done.append(arrived[shift])
        return tuple(arrived)


def after(values, *others):
    return lax.optimization_barrier((values, others))[0]


def halo_of(x):
    count = lax.axis_size("orbit")
    far = [(i, i + 1) for i in range(1, count - 1, 2)]
    far = lax.ppermute(x, "orbit", far + [(b, a) for a, b in far])
    near = [(i, i + 1) for i in range(0, count - 1, 2)]
    near = lax.ppermute(x, "orbit", near + [(b, a) for a, b in near])
    return near, x, far


def halo_ids(neighbours, nblk):
    mine = lax.axis_index("orbit")
    local = jnp.clip(neighbours - (mine - 1) * nblk, 0, 3 * nblk - 1)
    side = local // nblk
    side = jnp.where(mine % 2 == 0, 2 - side, side)
    return (side * nblk + local % nblk).reshape(-1)


def weigh(
    innovation, perturbation, quality, neighbours, counts, spatial_blocks, chan_op, capacity, watch
):
    rows, width = innovation.shape
    block_rows = spatial_blocks.shape[2]
    nblk = rows // block_rows
    count = lax.axis_size("chan")
    size = capacity // count

    me = lax.axis_index("chan").astype(jnp.int32).reshape(1)
    ids = halo_ids(neighbours, nblk)

    def spread(halo, room):
        return spatial(halo, spatial_blocks, ids, counts, pos, offs, me, room, count)

    kept = quality.reshape(nblk, block_rows)
    pos, offs, parts_i = compact(innovation, kept, me, size, count)
    line = Line(DEPTH)
    there_i = line.exchange(parts_i)
    perturbation, quality = after((perturbation, quality), parts_i[0])
    masked_p = perturbation * quality.astype(jnp.bfloat16)[:, None]
    parts_p = spread(halo_of(masked_p), size)
    there_p = line.exchange(parts_p)

    mixed_i = mix(after(there_i, parts_p[0]), chan_op, me)
    back_i = line.exchange(mixed_i)
    mixed_p = mix(after(there_p, mixed_i[0]), chan_op, me)
    back_p = line.exchange(mixed_p)
    seen = watch(after(quality, mixed_p[0]))

    wide_i = expand(after(back_i, mixed_p[0]), pos, offs, me)
    (out_i,) = spread(halo_of(wide_i), None)
    out_p = expand(after(back_p, out_i), pos, offs, me)
    return (out_i, out_p), seen


def shards(innovation, perturbation, quality, *others):
    rows = innovation.shape[0]
    unit = ALIGN * lax.axis_size("chan")
    capacity = -(-rows * 57 // (64 * unit)) * unit
    given = (innovation, perturbation, quality, *others)

    def overfull(quality):
        more = jnp.sum(quality, dtype=jnp.int32) > capacity
        return lax.pmax(more.astype(jnp.int32), ("grp", "orbit"))

    packed, more = weigh(*given, capacity, overfull)
    return lax.cond(
        more > 0,
        lambda given, packed: weigh(*given, rows, lambda quality: None)[0],
        lambda given, packed: packed,
        given,
        packed,
    )


def solution(mesh):
    placed = (
        P(("grp", "orbit"), "chan"),
        P(("grp", "orbit"), "chan"),
        P(("grp", "orbit")),
        P(("grp", "orbit"), None),
        P(("grp", "orbit")),
        P(("grp", "orbit"), None, None, None),
        P(),
    )
    return jax.shard_map(
        shards,
        mesh=mesh,
        in_specs=placed,
        out_specs=(P(("grp", "orbit"), "chan"), P(("grp", "orbit"), "chan")),
        check_vma=False,
    )
```

time: 374 us -> 358 us (0.957)
  Pallas kernels: 87.3 us -> 63.2 us
  waiting for transfers between devices: 204 us -> 221 us
  starting transfers between devices: 32.4 us -> 26.2 us
    pallas_call x4 -> x3, Pallas kernels: 60.9 us -> 39 us  [the longest x2 32.1 us: spatial(): pl.pallas_call(functools.partial(spatial_kernel, size is not None), out_s...]
    ppermute x12, waiting for transfers between devices: 163 us -> 178 us  [exchange(): lax.ppermute(part, 'chan', [(i, (i + shift) % count) for i in range(count)])]
    ppermute x4, starting transfers between devices: 12.2 us -> 7.7 us  [the longest x2 6.89 us: halo_of(): far = lax.ppermute(x, 'orbit', far + [(b, a) for a, b in far])]
  transfers between devices with their start and end apart: 16 -> 16, of which waited for: 10 -> 9; matrix products, arithmetic and copies ran while one was open for 0% -> 0% of each run, Pallas kernels for 16% -> 13%
where the time goes in v3:
time: 358 us; the launch traced here: 356 us
  waiting for transfers between devices  221 us (62%)
  Pallas kernels  63.2 us (18%)
  blocking collectives  38.9 us (11%)
  starting transfers between devices  26.2 us (7%)
    ppermute x12, waiting for transfers between devices, exchange(): lax.ppermute(part, 'chan', [(i, (i + shift) % count) for i in range(count)])  178 us
    ppermute x2, waiting for transfers between devices, halo_of(): far = lax.ppermute(x, 'orbit', far + [(b, a) for a, b in far])  43 us
    pmax x1, blocking collectives, overfull(): return lax.pmax(more.astype(jnp.int32), ('grp', 'orbit'))  38.9 us
    pallas_call x2, Pallas kernels, spatial(): pl.pallas_call(functools.partial(spatial_kernel, size is not None), out_s...  32.1 us
    ppermute x12, starting transfers between devices, exchange(): lax.ppermute(part, 'chan', [(i, (i + shift) % count) for i in range(count)])  18.5 us
    pallas_call x2, Pallas kernels, mix(): pl.pallas_call(functools.partial(mix_kernel, count), out_shape=part_shape...  12.4 us
    pallas_call x2, Pallas kernels, expand(): pl.pallas_call(expand_kernel, out_shape=jax.ShapeDtypeStruct((rows, width...  11.7 us
  transfers between devices with their start and end apart: 16, of which 9 were waited for; matrix products, arithmetic and copies ran while one was open for 0% of the time, Pallas kernels for 13%

profile of v3, /device:TPU:11, one launch (start us, length us, event | category | flops | bytes accessed | tf_op | source)
XLA Modules:
  0.0 355.7 jit_solution(8209710812082744318)
XLA Ops:
  0.7 7.0 %shard_map.90 = (s32[64,128]{1,0:T(8,128)S(1)}, s32[8,64]{1,0:T(8,128)S(1)}, bf16[1824,256]{1,0:T(8,128)(2,1)S(1)}, bf16[1824,256]{1,0:T(8,128)(2,1)S(1)}, bf16[...) custom-call(s32[1]{0:T(128)} %bitcast.2.me_ref, s32[64,128]{1,0:T(8,128)} %bitcast.4, bf16[8192,256]{1,0:T(8,128)(2,1)} %v_ref.1), custom_call_target="tpu_custom_call" | custom-call | flops 1140850688 | bytes 8388608 | tf_op jit(solution)/shard_map/pallas_call | solution.py:172
  7.7 2.6 broadcast_multiply_fusion.1.own
  10.3 3.7 %collective-permute-start.17 = (bf16[8192,256]{1,0:T(8,128)(2,1)}, bf16[8192,256]{1,0:T(8,128)(2,1)}, u32[]{:S(2)}, u32[]{:S(2)}) collective-permute-start(bf16[8192,256]{1,0:T(8,128)(2,1)} %broadcast_multiply_fusion.1.own), channel_id=1, source_target_pairs={{4,8},{8,4},{5,9},{9,5},{6,10},{10,6},{7,11},{11,7},{20,24},{24,20... | collective-permute-start | bytes 12582920 | tf_op jit(solution)/shard_map/ppermute | solution.py:465
  14.3 1.4 collective-permute-start.20
  15.7 2.2 collective-permute-start.18
  18.2 42.6 %collective-permute-done.17.far = bf16[8192,256]{1,0:T(8,128)(2,1)} collective-permute-done((bf16[8192,256]{1,0:T(8,128)(2,1)}, bf16[8192,256]{1,0:T(8,128)(2,1)}, u32[]{:S(2)}, u32[]{:S(2)}) %collective-permute-start.17) | collective-permute-done | bytes 4194336 | tf_op jit(solution)/shard_map/ppermute | solution.py:465
  60.8 16.7 %shard_map.91 = (bf16[1824,256]{1,0:T(8,128)(2,1)S(1)}, bf16[1824,256]{1,0:T(8,128)(2,1)S(1)}, bf16[1824,256]{1,0:T(8,128)(2,1)S(1)}, bf16[1824,256]{1,0:T(8,128)(2,1)S(1)}) custom-call(s32[1]{0:T(128)} %bitcast.2.me_ref, s32[8,64]{1,0:T(8,128)S(1)} %get-tuple-element.120.offs_ref, s32[384]{0:T(512)S(1)} %reshape.26.ids_ref, s32[64]{0:T(128)S(1)} %copy-done.11, ...), custom_call_target="tpu_custom_call" | custom-call | flops 3221225472 | bytes 29360128 | tf_op jit(solution)/shard_map/pallas_call | solution.py:358
  77.6 1.4 collective-permute-start.21
  79.0 56.7 %collective-permute-done.18.rest_1_ = bf16[1824,256]{1,0:T(8,128)(2,1)S(1)} collective-permute-done((bf16[1824,256]{1,0:T(8,128)(2,1)S(1)}, bf16[1824,256]{1,0:T(8,128)(2,1)S(1)}, u32[]{:S(2)}, u32[]{:S(2)}) %collective-permute-start.18) | collective-permute-done | bytes 933920 | tf_op jit(solution)/shard_map/ppermute | solution.py:451
  135.7 2.2 collective-permute-start.19
  137.9 5.8 %shard_map.92 = (bf16[1824,256]{1,0:T(8,128)(2,1)S(1)}, bf16[1824,256]{1,0:T(8,128)(2,1)S(1)}, bf16[1824,256]{1,0:T(8,128)(2,1)S(1)}, bf16[1824,256]{1,0:T(8,128)(2,1)S(1)}) custom-call(s32[1]{0:T(128)} %bitcast.2.me_ref, bf16[1024,1024]{1,0:T(8,128)(2,1)S(1)} %copy-done, bf16[1824,256]{1,0:T(8,128)(2,1)S(1)} %get-tuple-element.133.rest_0_, ...), custom_call_target="tpu_custom_call" | custom-call | flops 1 | bytes 1 | tf_op jit(solution)/shard_map/pallas_call | solution.py:421
  143.7 12.6 %collective-permute-done.23.rest_3_ = bf16[1824,256]{1,0:T(8,128)(2,1)S(1)} collective-permute-done((bf16[1824,256]{1,0:T(8,128)(2,1)S(1)}, bf16[1824,256]{1,0:T(8,128)(2,1)S(1)}, u32[]{:S(2)}, u32[]{:S(2)}) %collective-permute-start.23) | collective-permute-done | bytes 933920 | tf_op jit(solution)/shard_map/ppermute | solution.py:451
  156.3 3.5 collective-permute-start.25
  159.8 56.0 %collective-permute-done.19.rest_1_ = bf16[1824,256]{1,0:T(8,128)(2,1)S(1)} collective-permute-done((bf16[1824,256]{1,0:T(8,128)(2,1)S(1)}, bf16[1824,256]{1,0:T(8,128)(2,1)S(1)}, u32[]{:S(2)}, u32[]{:S(2)}) %collective-permute-start.19) | collective-permute-done | bytes 933920 | tf_op jit(solution)/shard_map/ppermute | solution.py:451
  215.8 2.2 collective-permute-start.24
  218.0 6.6 %shard_map.93 = (bf16[1824,256]{1,0:T(8,128)(2,1)S(1)}, bf16[1824,256]{1,0:T(8,128)(2,1)}, bf16[1824,256]{1,0:T(8,128)(2,1)}, bf16[1824,256]{1,0:T(8,128)(2,1)}) custom-call(s32[1]{0:T(128)} %bitcast.2.me_ref, bf16[1024,1024]{1,0:T(8,128)(2,1)S(1)} %copy-done, bf16[1824,256]{1,0:T(8,128)(2,1)S(1)} %get-tuple-element.138.rest_0_, ...), custom_call_target="tpu_custom_call" | custom-call | flops 1 | bytes 1 | tf_op jit(solution)/shard_map/pallas_call | solution.py:421
  224.6 11.8 %collective-permute-done.26.rest_3_ = bf16[1824,256]{1,0:T(8,128)(2,1)S(1)} collective-permute-done((bf16[1824,256]{1,0:T(8,128)(2,1)S(1)}, bf16[1824,256]{1,0:T(8,128)(2,1)S(1)}, u32[]{:S(2)}, u32[]{:S(2)}) %collective-permute-start.26) | collective-permute-done | bytes 933920 | tf_op jit(solution)/shard_map/ppermute | solution.py:451
  236.4 19.5 %collective-permute-done.24.rest_1_ = bf16[1824,256]{1,0:T(8,128)(2,1)S(1)} collective-permute-done((bf16[1824,256]{1,0:T(8,128)(2,1)S(1)}, bf16[1824,256]{1,0:T(8,128)(2,1)S(1)}, u32[]{:S(2)}, u32[]{:S(2)}) %collective-permute-start.24) | collective-permute-done | bytes 933920 | tf_op jit(solution)/shard_map/ppermute | solution.py:451
  255.9 5.8 %shard_map.94.own = bf16[8192,256]{1,0:T(8,128)(2,1)} custom-call(s32[1]{0:T(128)} %bitcast.2.me_ref, s32[8,64]{1,0:T(8,128)S(1)} %get-tuple-element.120.offs_ref, s32[64,128]{1,0:T(8,128)S(1)} %get-tuple-element.121.pos_ref, bf16[1824,256]{1,0:T(8,128)(2,1)S(1)} %get-tuple-element.150.rest_0_, bf16[1824,256]{1,0:T(8,128)(2,1)S(1)} %collective-permute-done.24.rest_1_, ...), custom_call_target="tpu_custom_call" | custom-call | flops 1073741824 | bytes 8388608 | tf_op jit(solution)/shard_map/pallas_call | solution.py:251
  261.7 3.2 collective-permute-start.28
  264.9 0.7 collective-permute-start.27
  265.6 1.8 collective-permute-start.31
  267.4 1.6 collective-permute-start.30
  269.0 1.9 collective-permute-start.29
  271.0 0.6 reduce_sum.9
  272.2 38.9 %pmax.7 = s32[]{:T(128)} all-reduce(s32[]{:T(128)S(6)} %convert_element_type.13), channel_id=1, replica_groups=mesh['grp'=2,'orbit'=4,'chan'=4] {'grp','orbit'}, use_global_device_ids=true, to_apply=%region_1.2 | all-reduce | flops 1 | bytes 8 | tf_op jit(solution)/shard_map/pmax | solution.py:523
  311.8 0.3 collective-permute-done.28.far
  312.2 15.4 %shard_map.95 = bf16[8192,256]{1,0:T(8,128)(2,1)} custom-call(s32[1]{0:T(128)} %bitcast.2.me_ref, s32[8,64]{1,0:T(8,128)S(1)} %get-tuple-element.120.offs_ref, s32[384]{0:T(512)S(1)} %reshape.26.ids_ref, s32[64]{0:T(128)S(1)} %copy-done.11, s32[64,128]{1,0:T(8,128)S(1)} %get-tuple-element.121.pos_ref, bf16[64,6,128,128]{3,2,1,0:T(8,128)(2,1)} %weight_ref.3, ...), custom_call_target="tpu_custom_call" | custom-call | flops 3221225472 | bytes 29360128 | tf_op jit(solution)/shard_map/pallas_call | solution.py:358
  327.6 1.8 collective-permute-done.30.rest_2_
  329.4 20.0 %collective-permute-done.29.rest_1_ = bf16[1824,256]{1,0:T(8,128)(2,1)} collective-permute-done((bf16[1824,256]{1,0:T(8,128)(2,1)}, bf16[1824,256]{1,0:T(8,128)(2,1)}, u32[]{:S(2)}, u32[]{:S(2)}) %collective-permute-start.29) | collective-permute-done | bytes 933920 | tf_op jit(solution)/shard_map/ppermute | solution.py:451
  349.4 5.9 %shard_map.96 = bf16[8192,256]{1,0:T(8,128)(2,1)} custom-call(s32[1]{0:T(128)} %bitcast.2.me_ref, s32[8,64]{1,0:T(8,128)S(1)} %get-tuple-element.120.offs_ref, s32[64,128]{1,0:T(8,128)S(1)} %get-tuple-element.121.pos_ref, bf16[1824,256]{1,0:T(8,128)(2,1)S(1)} %get-tuple-element.160.rest_0_, bf16[1824,256]{1,0:T(8,128)(2,1)} %collective-permute-done.29.rest_1_, ...), custom_call_target="tpu_custom_call" | custom-call | flops 1073741824 | bytes 8388608 | tf_op jit(solution)/shard_map/pallas_call | solution.py:251
  355.3 0.2 conditional.1
  (29 shorter events, 0.7 us)
Async XLA Ops:
  0.6 7.0 %copy-start.9 = (s32[8192]{0:T(1024)S(1)}, s32[8192]{0:T(1024)}, u32[]{:S(2)}) copy-start(s32[8192]{0:T(1024)} %param.11) | copy-start | bytes 98308
  0.6 7.0 %copy-start.2 = (bf16[8192,256]{1,0:T(8,128)(2,1)S(1)}, bf16[8192,256]{1,0:T(8,128)(2,1)}, u32[]{:S(2)}) copy-start(bf16[8192,256]{1,0:T(8,128)(2,1)} %param.10) | copy-start | bytes 12582916
  7.6 10.3 %copy-start.10 = (s32[64,6]{0,1:T(8,128)S(1)}, s32[64,6]{0,1:T(8,128)}, u32[]{:S(2)}) copy-start(s32[64,6]{0,1:T(8,128)} %param.12) | copy-start | bytes 4612
  7.7 53.1 %copy-start.11 = (s32[64]{0:T(128)S(1)}, s32[64]{0:T(128)}, u32[]{:S(2)}) copy-start(s32[64]{0:T(128)} %counts_ref.3) | copy-start | bytes 772
  10.3 50.5 %collective-permute-start.17 = (bf16[8192,256]{1,0:T(8,128)(2,1)}, bf16[8192,256]{1,0:T(8,128)(2,1)}, u32[]{:S(2)}, u32[]{:S(2)}) collective-permute-start(bf16[8192,256]{1,0:T(8,128)(2,1)} %broadcast_multiply_fusion.1.own), channel_id=1, source_target_pairs={{4,8},{8,4},{5,9},{9,5},{6,10},{10,6},{7,11},{11,7},{20,24},{24,20... | collective-permute-start | bytes 12582920 | tf_op jit(solution)/shard_map/ppermute | solution.py:465
  14.0 46.8 %collective-permute-start.16 = (bf16[8192,256]{1,0:T(8,128)(2,1)}, bf16[8192,256]{1,0:T(8,128)(2,1)}, u32[]{:S(2)}, u32[]{:S(2)}) collective-permute-start(bf16[8192,256]{1,0:T(8,128)(2,1)} %broadcast_multiply_fusion.1.own), channel_id=1, source_target_pairs={{0,4},{8,12},{4,0},{12,8},{1,5},{9,13},{5,1},{13,9},{2,6},{10,14},... | collective-permute-start | bytes 12582920 | tf_op jit(solution)/shard_map/ppermute | solution.py:467
  14.1 63.4 %collective-permute-start.22 = (bf16[1824,256]{1,0:T(8,128)(2,1)}, bf16[1824,256]{1,0:T(8,128)(2,1)}, u32[]{:S(2)}, u32[]{:S(2)}) collective-permute-start(bf16[1824,256]{1,0:T(8,128)(2,1)} %get-tuple-element.131), channel_id=1, source_target_pairs={{0,3},{1,0},{2,1},{3,2},{4,7},{5,4},{6,5},{7,6},{8,11},{9,8},{10,9... | collective-permute-start | bytes 2801672 | tf_op jit(solution)/shard_map/ppermute | solution.py:451
  14.3 63.3 %collective-permute-start.20 = (bf16[1824,256]{1,0:T(8,128)(2,1)}, bf16[1824,256]{1,0:T(8,128)(2,1)}, u32[]{:S(2)}, u32[]{:S(2)}) collective-permute-start(bf16[1824,256]{1,0:T(8,128)(2,1)} %get-tuple-element.128), channel_id=1, source_target_pairs={{0,2},{1,3},{2,0},{3,1},{4,6},{5,7},{6,4},{7,5},{8,10},{9,11},{10,... | collective-permute-start | bytes 2801672 | tf_op jit(solution)/shard_map/ppermute | solution.py:451
  15.7 120.0 %collective-permute-start.18 = (bf16[1824,256]{1,0:T(8,128)(2,1)S(1)}, bf16[1824,256]{1,0:T(8,128)(2,1)S(1)}, u32[]{:S(2)}, u32[]{:S(2)}) collective-permute-start(bf16[1824,256]{1,0:T(8,128)(2,1)S(1)} %get-tuple-element.125), channel_id=1, source_target_pairs={{0,1},{1,2},{2,3},{3,0},{4,5},{5,6},{6,7},{7,4},{8,9},{9,10},{10,1... | collective-permute-start | bytes 2801672 | tf_op jit(solution)/shard_map/ppermute | solution.py:451
  60.8 77.1 %copy-start = (bf16[1024,1024]{1,0:T(8,128)(2,1)S(1)}, bf16[1024,1024]{1,0:T(8,128)(2,1)}, u32[]{:S(2)}) copy-start(bf16[1024,1024]{1,0:T(8,128)(2,1)} %op_ref.3) | copy-start | bytes 6291460
  77.5 78.8 %collective-permute-start.23 = (bf16[1824,256]{1,0:T(8,128)(2,1)S(1)}, bf16[1824,256]{1,0:T(8,128)(2,1)S(1)}, u32[]{:S(2)}, u32[]{:S(2)}) collective-permute-start(bf16[1824,256]{1,0:T(8,128)(2,1)S(1)} %get-tuple-element.132), channel_id=1, source_target_pairs={{0,3},{1,0},{2,1},{3,2},{4,7},{5,4},{6,5},{7,6},{8,11},{9,8},{10,9... | collective-permute-start | bytes 2801672 | tf_op jit(solution)/shard_map/ppermute | solution.py:451
  77.6 78.7 %collective-permute-start.21 = (bf16[1824,256]{1,0:T(8,128)(2,1)S(1)}, bf16[1824,256]{1,0:T(8,128)(2,1)S(1)}, u32[]{:S(2)}, u32[]{:S(2)}) collective-permute-start(bf16[1824,256]{1,0:T(8,128)(2,1)S(1)} %get-tuple-element.129), channel_id=1, source_target_pairs={{0,2},{1,3},{2,0},{3,1},{4,6},{5,7},{6,4},{7,5},{8,10},{9,11},{10,... | collective-permute-start | bytes 2801672 | tf_op jit(solution)/shard_map/ppermute | solution.py:451
  135.7 80.1 %collective-permute-start.19 = (bf16[1824,256]{1,0:T(8,128)(2,1)S(1)}, bf16[1824,256]{1,0:T(8,128)(2,1)S(1)}, u32[]{:S(2)}, u32[]{:S(2)}) collective-permute-start(bf16[1824,256]{1,0:T(8,128)(2,1)S(1)} %get-tuple-element.126), channel_id=1, source_target_pairs={{0,1},{1,2},{2,3},{3,0},{4,5},{5,6},{6,7},{7,4},{8,9},{9,10},{10,1... | collective-permute-start | bytes 2801672 | tf_op jit(solution)/shard_map/ppermute | solution.py:451
  156.3 61.7 %copy-start.7 = (bf16[1824,256]{1,0:T(8,128)(2,1)}, bf16[1824,256]{1,0:T(8,128)(2,1)S(1)}, u32[]{:S(2)}) copy-start(bf16[1824,256]{1,0:T(8,128)(2,1)S(1)} %collective-permute-done.23.rest_3_) | copy-start | bytes 2801668
  156.3 80.1 %collective-permute-start.26 = (bf16[1824,256]{1,0:T(8,128)(2,1)S(1)}, bf16[1824,256]{1,0:T(8,128)(2,1)S(1)}, u32[]{:S(2)}, u32[]{:S(2)}) collective-permute-start(bf16[1824,256]{1,0:T(8,128)(2,1)S(1)} %get-tuple-element.149), channel_id=1, source_target_pairs={{0,3},{1,0},{2,1},{3,2},{4,7},{5,4},{6,5},{7,6},{8,11},{9,8},{10,9... | collective-permute-start | bytes 2801672 | tf_op jit(solution)/shard_map/ppermute | solution.py:451
  156.3 61.7 %copy-start.8 = (bf16[1824,256]{1,0:T(8,128)(2,1)}, bf16[1824,256]{1,0:T(8,128)(2,1)S(1)}, u32[]{:S(2)}) copy-start(bf16[1824,256]{1,0:T(8,128)(2,1)S(1)} %collective-permute-done.21.rest_2_) | copy-start | bytes 2801668
  156.3 80.1 %collective-permute-start.25 = (bf16[1824,256]{1,0:T(8,128)(2,1)S(1)}, bf16[1824,256]{1,0:T(8,128)(2,1)S(1)}, u32[]{:S(2)}, u32[]{:S(2)}) collective-permute-start(bf16[1824,256]{1,0:T(8,128)(2,1)S(1)} %get-tuple-element.147), channel_id=1, source_target_pairs={{0,2},{1,3},{2,0},{3,1},{4,6},{5,7},{6,4},{7,5},{8,10},{9,11},{10,... | collective-permute-start | bytes 2801672 | tf_op jit(solution)/shard_map/ppermute | solution.py:451
  215.8 40.1 %collective-permute-start.24 = (bf16[1824,256]{1,0:T(8,128)(2,1)S(1)}, bf16[1824,256]{1,0:T(8,128)(2,1)S(1)}, u32[]{:S(2)}, u32[]{:S(2)}) collective-permute-start(bf16[1824,256]{1,0:T(8,128)(2,1)S(1)} %get-tuple-element.145), channel_id=1, source_target_pairs={{0,1},{1,2},{2,3},{3,0},{4,5},{5,6},{6,7},{7,4},{8,9},{9,10},{10,1... | collective-permute-start | bytes 2801672 | tf_op jit(solution)/shard_map/ppermute | solution.py:451
  261.7 50.5 %collective-permute-start.28 = (bf16[8192,256]{1,0:T(8,128)(2,1)}, bf16[8192,256]{1,0:T(8,128)(2,1)}, u32[]{:S(2)}, u32[]{:S(2)}) collective-permute-start(bf16[8192,256]{1,0:T(8,128)(2,1)} %shard_map.94.own), channel_id=1, source_target_pairs={{4,8},{8,4},{5,9},{9,5},{6,10},{10,6},{7,11},{11,7},{20,24},{24,20... | collective-permute-start | bytes 12582920 | tf_op jit(solution)/shard_map/ppermute | solution.py:465
  264.9 47.3 %collective-permute-start.27 = (bf16[8192,256]{1,0:T(8,128)(2,1)}, bf16[8192,256]{1,0:T(8,128)(2,1)}, u32[]{:S(2)}, u32[]{:S(2)}) collective-permute-start(bf16[8192,256]{1,0:T(8,128)(2,1)} %shard_map.94.own), channel_id=1, source_target_pairs={{0,4},{8,12},{4,0},{12,8},{1,5},{9,13},{5,1},{13,9},{2,6},{10,14},... | collective-permute-start | bytes 12582920 | tf_op jit(solution)/shard_map/ppermute | solution.py:467
  265.6 61.9 %collective-permute-start.31 = (bf16[1824,256]{1,0:T(8,128)(2,1)}, bf16[1824,256]{1,0:T(8,128)(2,1)S(1)}, u32[]{:S(2)}, u32[]{:S(2)}) collective-permute-start(bf16[1824,256]{1,0:T(8,128)(2,1)} %get-tuple-element.159), channel_id=1, source_target_pairs={{0,3},{1,0},{2,1},{3,2},{4,7},{5,4},{6,5},{7,6},{8,11},{9,8},{10,9... | collective-permute-start | bytes 2801672 | tf_op jit(solution)/shard_map/ppermute | solution.py:451
  267.4 62.0 %collective-permute-start.30 = (bf16[1824,256]{1,0:T(8,128)(2,1)}, bf16[1824,256]{1,0:T(8,128)(2,1)S(1)}, u32[]{:S(2)}, u32[]{:S(2)}) collective-permute-start(bf16[1824,256]{1,0:T(8,128)(2,1)} %get-tuple-element.157), channel_id=1, source_target_pairs={{0,2},{1,3},{2,0},{3,1},{4,6},{5,7},{6,4},{7,5},{8,10},{9,11},{10,... | collective-permute-start | bytes 2801672 | tf_op jit(solution)/shard_map/ppermute | solution.py:451
  269.0 80.4 %collective-permute-start.29 = (bf16[1824,256]{1,0:T(8,128)(2,1)}, bf16[1824,256]{1,0:T(8,128)(2,1)}, u32[]{:S(2)}, u32[]{:S(2)}) collective-permute-start(bf16[1824,256]{1,0:T(8,128)(2,1)} %get-tuple-element.155), channel_id=1, source_target_pairs={{0,1},{1,2},{2,3},{3,0},{4,5},{5,6},{6,7},{7,4},{8,9},{9,10},{10,1... | collective-permute-start | bytes 2801672 | tf_op jit(solution)/shard_map/ppermute | solution.py:451

commit v4 on v3

--- a/solution.py
+++ b/solution.py
@@ -7,7 +7,7 @@
 from jax.experimental.pallas import tpu as pltpu
 from jax.sharding import PartitionSpec as P
 
-VMEM_LIMIT = 48 * 1024 * 1024
+MIB = 1024 * 1024
 ALIGN = 16
 DEPTH = 3
 PAIR = 2
@@ -15,9 +15,9 @@
 GROUP = 8
 
 
-def params():
+def params(mib):
     return pltpu.CompilerParams(
-        dimension_semantics=("arbitrary",), vmem_limit_bytes=VMEM_LIMIT
+        dimension_semantics=("arbitrary",), vmem_limit_bytes=mib * MIB
     )
 
 
@@ -193,7 +193,7 @@
                 pltpu.SemaphoreType.DMA,
             ],
         ),
-        compiler_params=params(),
+        compiler_params=params(16),
         cost_estimate=pl.CostEstimate(
             flops=2 * rows * 272 * width, bytes_accessed=4 * rows * width, transcendentals=0
         ),
@@ -264,7 +264,7 @@
                 pltpu.SemaphoreType.DMA((nblk // GROUP,)),
             ],
         ),
-        compiler_params=params(),
+        compiler_params=params(16),
         cost_estimate=pl.CostEstimate(
             flops=2 * rows * 256 * width, bytes_accessed=4 * rows * width, transcendentals=0
         ),
@@ -272,7 +272,7 @@
 
 
 def spatial_kernel(
-    compacting, me_ref, offs_ref, ids_ref, counts_ref, pos_ref, weight_ref, near, own, far, *rest
+    compacting, me_ref, offs_ref, ids_ref, counts_ref, pos_ref, weight_ref, near, own, far, _, *rest
 ):
     nblk, block_rows = pos_ref.shape
     slots = weight_ref.shape[1]
@@ -361,7 +361,7 @@
         grid_spec=pltpu.PrefetchScalarGridSpec(
             num_scalar_prefetch=4,
             grid=(1,),
-            in_specs=[pl.BlockSpec((nblk, block_rows), lambda i, *_: (0, 0))] + [any_spec] * 4,
+            in_specs=[pl.BlockSpec((nblk, block_rows), lambda i, *_: (0, 0))] + [any_spec] * 5,
             out_specs=[any_spec] * len(shapes),
             scratch_shapes=[
                 pltpu.VMEM((3 * rows, width), jnp.bfloat16),
@@ -372,7 +372,7 @@
                 pltpu.SemaphoreType.DMA((made[1],)),
             ],
         ),
-        compiler_params=params(),
+        compiler_params=params(34),
         cost_estimate=pl.CostEstimate(
             flops=2 * rows * slots * block_rows * width,
             bytes_accessed=8 * rows * width + 2 * rows * slots * block_rows,
@@ -431,7 +431,7 @@
                 pltpu.SemaphoreType.DMA((count,)),
             ],
         ),
-        compiler_params=params(),
+        compiler_params=params(16),
         cost_estimate=pl.CostEstimate(flops=1, bytes_accessed=1, transcendentals=0),
     )(me, chan_op, *parts)
 
@@ -459,6 +459,23 @@
     return lax.optimization_barrier((values, others))[0]
 
 
+def gate_kernel(x_ref, out_ref):
+    out_ref[...] = x_ref[...]
+
+
+def gate(x):
+    shape = (ALIGN, x.shape[1])
+    spec = pl.BlockSpec(shape, lambda i: (0, 0))
+    return pl.pallas_call(
+        gate_kernel,
+        out_shape=jax.ShapeDtypeStruct(shape, x.dtype),
+        grid=(1,),
+        in_specs=[spec],
+        out_specs=spec,
+        cost_estimate=pl.CostEstimate(flops=10**11, bytes_accessed=1, transcendentals=0),
+    )(x)
+
+
 def halo_of(x):
     count = lax.axis_size("orbit")
     far = [(i, i + 1) for i in range(1, count - 1, 2)]
@@ -497,17 +514,17 @@
     there_i = line.exchange(parts_i)
     perturbation, quality = after((perturbation, quality), parts_i[0])
     masked_p = perturbation * quality.astype(jnp.bfloat16)[:, None]
-    parts_p = spread(halo_of(masked_p), size)
+    parts_p = spread((*halo_of(masked_p), gate(there_i[1 % count])), size)
     there_p = line.exchange(parts_p)
 
     mixed_i = mix(after(there_i, parts_p[0]), chan_op, me)
     back_i = line.exchange(mixed_i)
-    mixed_p = mix(after(there_p, mixed_i[0]), chan_op, me)
-    back_p = line.exchange(mixed_p)
-    seen = watch(after(quality, mixed_p[0]))
+    seen = watch(after(quality, parts_p[0]))
+    mixed_p = mix(after(there_p, (mixed_i[0], seen)), chan_op, me)
+    back_p = line.exchange(after(mixed_p, back_i))
 
     wide_i = expand(after(back_i, mixed_p[0]), pos, offs, me)
-    (out_i,) = spread(halo_of(wide_i), None)
+    (out_i,) = spread((*halo_of(wide_i), gate(back_p[count // 2])), None)
     out_p = expand(after(back_p, out_i), pos, offs, me)
     return (out_i, out_p), seen
 

time: 358 us -> 344 us (0.961)
  blocking collectives: 38.9 us -> 11 us
  local copies, waits for them, and re-layouts: 0.27 us -> 13.2 us
  Pallas kernels: 63.2 us -> 67.4 us
    pmax x1, blocking collectives: 38.9 us -> 11 us  [overfull(): return lax.pmax(more.astype(jnp.int32), ('grp', 'orbit'))]
    unnamed x14 -> x40, local copies, waits for them, and re-layouts: 0.04 us -> 13 us
    ppermute x2, waiting for transfers between devices: 43 us -> 30.5 us  [halo_of(): far = lax.ppermute(x, 'orbit', far + [(b, a) for a, b in far])]
    ppermute x12, waiting for transfers between devices: 178 us -> 189 us  [exchange(): lax.ppermute(part, 'chan', [(i, (i + shift) % count) for i in range(count)])]
  transfers between devices with their start and end apart: 16 -> 16, of which waited for: 9 -> 9; matrix products, arithmetic and copies ran while one was open for 0% -> 1% of each run, Pallas kernels for 13% -> 16%
where the time goes in v4:
time: 344 us; the launch traced here: 343 us
  waiting for transfers between devices  220 us (64%)
  Pallas kernels  67.4 us (20%)
  starting transfers between devices  25.5 us (7%)
  local copies, waits for them, and re-layouts  13.2 us (4%)
  blocking collectives  11 us (3%)
    ppermute x12, waiting for transfers between devices, exchange(): lax.ppermute(part, 'chan', [(i, (i + shift) % count) for i in range(count)])  189 us
    pallas_call x2, Pallas kernels, spatial(): pl.pallas_call(functools.partial(spatial_kernel, size is not None), out_s...  32.3 us
    ppermute x2, waiting for transfers between devices, halo_of(): far = lax.ppermute(x, 'orbit', far + [(b, a) for a, b in far])  30.5 us
    ppermute x12, starting transfers between devices, exchange(): lax.ppermute(part, 'chan', [(i, (i + shift) % count) for i in range(count)])  16.8 us
    pallas_call x2, Pallas kernels, mix(): pl.pallas_call(functools.partial(mix_kernel, count), out_shape=part_shape...  13.4 us
    unnamed x40, local copies, waits for them, and re-layouts  13 us
    pallas_call x2, Pallas kernels, expand(): pl.pallas_call(expand_kernel, out_shape=jax.ShapeDtypeStruct((rows, width...  12.4 us
    pmax x1, blocking collectives, overfull(): return lax.pmax(more.astype(jnp.int32), ('grp', 'orbit'))  11 us
  transfers between devices with their start and end apart: 16, of which 9 were waited for; matrix products, arithmetic and copies ran while one was open for 1% of the time, Pallas kernels for 16%

profile of v4, /device:TPU:11, one launch (start us, length us, event | category | flops | bytes accessed | tf_op | source)
XLA Modules:
  0.0 342.7 jit_solution(11555738567371217256)
XLA Ops:
  0.7 6.7 %shard_map.90 = (s32[64,128]{1,0:T(8,128)S(1)}, s32[8,64]{1,0:T(8,128)S(1)}, bf16[1824,256]{1,0:T(8,128)(2,1)S(1)}, bf16[1824,256]{1,0:T(8,128)(2,1)}, bf16[1824...) custom-call(s32[1]{0:T(128)} %bitcast.2.me_ref, s32[64,128]{1,0:T(8,128)} %bitcast.4, bf16[8192,256]{1,0:T(8,128)(2,1)} %v_ref.1), custom_call_target="tpu_custom_call" | custom-call | flops 1140850688 | bytes 8388608 | tf_op jit(solution)/shard_map/pallas_call | solution.py:172
  7.3 1.4 collective-permute-start.18
  8.7 2.6 broadcast_multiply_fusion.1.own
  11.3 4.0 %collective-permute-start.17 = (bf16[8192,256]{1,0:T(8,128)(2,1)}, bf16[8192,256]{1,0:T(8,128)(2,1)}, u32[]{:S(2)}, u32[]{:S(2)}) collective-permute-start(bf16[8192,256]{1,0:T(8,128)(2,1)} %broadcast_multiply_fusion.1.own), channel_id=1, source_target_pairs={{4,8},{8,4},{5,9},{9,5},{6,10},{10,6},{7,11},{11,7},{20,24},{24,20... | collective-permute-start | bytes 12582920 | tf_op jit(solution)/shard_map/ppermute | solution.py:482
  17.3 11.8 %collective-permute-done.18.x_ref.rest_1_ = bf16[1824,256]{1,0:T(8,128)(2,1)S(1)} collective-permute-done((bf16[1824,256]{1,0:T(8,128)(2,1)}, bf16[1824,256]{1,0:T(8,128)(2,1)S(1)}, u32[]{:S(2)}, u32[]{:S(2)}) %collective-permute-start.18) | collective-permute-done | bytes 933920 | tf_op jit(solution)/shard_map/ppermute | solution.py:451
  30.1 1.3 shard_map.91._
  31.4 30.5 %collective-permute-done.17.far = bf16[8192,256]{1,0:T(8,128)(2,1)} collective-permute-done((bf16[8192,256]{1,0:T(8,128)(2,1)}, bf16[8192,256]{1,0:T(8,128)(2,1)}, u32[]{:S(2)}, u32[]{:S(2)}) %collective-permute-start.17) | collective-permute-done | bytes 4194336 | tf_op jit(solution)/shard_map/ppermute | solution.py:482
  62.5 16.9 %shard_map.92 = (bf16[1824,256]{1,0:T(8,128)(2,1)S(1)}, bf16[1824,256]{1,0:T(8,128)(2,1)S(1)}, bf16[1824,256]{1,0:T(8,128)(2,1)S(1)}, bf16[1824,256]{1,0:T(8,128)(2,1)S(1)}) custom-call(s32[1]{0:T(128)} %bitcast.2.me_ref, s32[8,64]{1,0:T(8,128)S(1)} %get-tuple-element.128.offs_ref, s32[384]{0:T(512)S(1)} %reshape.26.ids_ref, s32[64]{0:T(128)S(1)} %copy-done.27, ...), custom_call_target="tpu_custom_call" | custom-call | flops 3221225472 | bytes 29360128 | tf_op jit(solution)/shard_map/pallas_call | solution.py:358
  80.4 10.8 %collective-permute-done.20.rest_3_ = bf16[1824,256]{1,0:T(8,128)(2,1)} collective-permute-done((bf16[1824,256]{1,0:T(8,128)(2,1)}, bf16[1824,256]{1,0:T(8,128)(2,1)}, u32[]{:S(2)}, u32[]{:S(2)}) %collective-permute-start.20) | collective-permute-done | bytes 933920 | tf_op jit(solution)/shard_map/ppermute | solution.py:451
  91.2 37.2 %collective-permute-done.19.rest_2_ = bf16[1824,256]{1,0:T(8,128)(2,1)S(1)} collective-permute-done((bf16[1824,256]{1,0:T(8,128)(2,1)}, bf16[1824,256]{1,0:T(8,128)(2,1)S(1)}, u32[]{:S(2)}, u32[]{:S(2)}) %collective-permute-start.19) | collective-permute-done | bytes 933920 | tf_op jit(solution)/shard_map/ppermute | solution.py:451
  129.3 3.0 collective-permute-start.23
  133.5 6.5 %shard_map.93 = (bf16[1824,256]{1,0:T(8,128)(2,1)S(1)}, bf16[1824,256]{1,0:T(8,128)(2,1)}, bf16[1824,256]{1,0:T(8,128)(2,1)}, bf16[1824,256]{1,0:T(8,128)(2,1)}) custom-call(s32[1]{0:T(128)} %bitcast.2.me_ref, bf16[1024,1024]{1,0:T(8,128)(2,1)S(1)} %copy-done.20, bf16[1824,256]{1,0:T(8,128)(2,1)S(1)} %get-tuple-element.136.rest_0_, ...), custom_call_target="tpu_custom_call" | custom-call | flops 1 | bytes 1 | tf_op jit(solution)/shard_map/pallas_call | solution.py:421
  141.0 1.5 collective-permute-start.26
  142.4 9.4 %collective-permute-done.23.rest_2_ = bf16[1824,256]{1,0:T(8,128)(2,1)S(1)} collective-permute-done((bf16[1824,256]{1,0:T(8,128)(2,1)S(1)}, bf16[1824,256]{1,0:T(8,128)(2,1)S(1)}, u32[]{:S(2)}, u32[]{:S(2)}) %collective-permute-start.23) | collective-permute-done | bytes 933920 | tf_op jit(solution)/shard_map/ppermute | solution.py:451
  152.9 2.1 collective-permute-start.24
  154.9 56.0 %collective-permute-done.21.rest_1_ = bf16[1824,256]{1,0:T(8,128)(2,1)S(1)} collective-permute-done((bf16[1824,256]{1,0:T(8,128)(2,1)S(1)}, bf16[1824,256]{1,0:T(8,128)(2,1)S(1)}, u32[]{:S(2)}, u32[]{:S(2)}) %collective-permute-start.21) | collective-permute-done | bytes 933920 | tf_op jit(solution)/shard_map/ppermute | solution.py:451
  211.9 2.2 collective-permute-start.22
  215.5 11.0 %pmax.7 = s32[]{:T(128)} all-reduce(s32[]{:T(128)S(6)} %convert_element_type.13), channel_id=1, replica_groups=mesh['grp'=2,'orbit'=4,'chan'=4] {'grp','orbit'}, use_global_device_ids=true, to_apply=%region_1.2 | all-reduce | flops 1 | bytes 8 | tf_op jit(solution)/shard_map/pmax | solution.py:540
  226.5 1.2 copy-done.9
  227.6 1.2 copy-done.11
  228.8 1.2 copy-done.13
  230.0 1.2 copy-done.15
  231.2 6.9 %shard_map.94 = (bf16[1824,256]{1,0:T(8,128)(2,1)S(1)}, bf16[1824,256]{1,0:T(8,128)(2,1)}, bf16[1824,256]{1,0:T(8,128)(2,1)}, bf16[1824,256]{1,0:T(8,128)(2,1)}) custom-call(s32[1]{0:T(128)} %bitcast.2.me_ref, bf16[1024,1024]{1,0:T(8,128)(2,1)} %op_ref.3, bf16[1824,256]{1,0:T(8,128)(2,1)S(1)} %copy-done.9, bf16[1824,256]{1,0:T(8,128)(2,1)S(1)} %copy-done.15, ...), custom_call_target="tpu_custom_call" | custom-call | flops 1 | bytes 1 | tf_op jit(solution)/shard_map/pallas_call | solution.py:421
  238.1 12.9 %collective-permute-done.22.rest_1_ = bf16[1824,256]{1,0:T(8,128)(2,1)} collective-permute-done((bf16[1824,256]{1,0:T(8,128)(2,1)}, bf16[1824,256]{1,0:T(8,128)(2,1)}, u32[]{:S(2)}, u32[]{:S(2)}) %collective-permute-start.22) | collective-permute-done | bytes 933920 | tf_op jit(solution)/shard_map/ppermute | solution.py:451
  251.1 3.5 %collective-permute-start.29 = (bf16[1824,256]{1,0:T(8,128)(2,1)}, bf16[1824,256]{1,0:T(8,128)(2,1)}, u32[]{:S(2)}, u32[]{:S(2)}) collective-permute-start(bf16[1824,256]{1,0:T(8,128)(2,1)} %get-tuple-element.166), channel_id=1, source_target_pairs={{0,2},{1,3},{2,0},{3,1},{4,6},{5,7},{6,4},{7,5},{8,10},{9,11},{10,... | collective-permute-start | bytes 2801672 | tf_op jit(solution)/shard_map/ppermute | solution.py:451
  255.3 6.2 %shard_map.95.own = bf16[8192,256]{1,0:T(8,128)(2,1)} custom-call(s32[1]{0:T(128)} %bitcast.2.me_ref, s32[8,64]{1,0:T(8,128)S(1)} %get-tuple-element.128.offs_ref, s32[64,128]{1,0:T(8,128)S(1)} %get-tuple-element.129.pos_ref, bf16[1824,256]{1,0:T(8,128)(2,1)S(1)} %get-tuple-element.158.rest_0_, bf16[1824,256]{1,0:T(8,128)(2,1)} %collective-permute-done.22.rest_1_, ...), custom_call_target="tpu_custom_call" | custom-call | flops 1073741824 | bytes 8388608 | tf_op jit(solution)/shard_map/pallas_call | solution.py:251
  261.5 4.6 %collective-permute-start.28 = (bf16[8192,256]{1,0:T(8,128)(2,1)}, bf16[8192,256]{1,0:T(8,128)(2,1)}, u32[]{:S(2)}, u32[]{:S(2)}) collective-permute-start(bf16[8192,256]{1,0:T(8,128)(2,1)} %shard_map.95.own), channel_id=1, source_target_pairs={{4,8},{8,4},{5,9},{9,5},{6,10},{10,6},{7,11},{11,7},{20,24},{24,20... | collective-permute-start | bytes 12582920 | tf_op jit(solution)/shard_map/ppermute | solution.py:482
  267.7 47.4 %collective-permute-done.29.x_ref.rest_2_ = bf16[1824,256]{1,0:T(8,128)(2,1)} collective-permute-done((bf16[1824,256]{1,0:T(8,128)(2,1)}, bf16[1824,256]{1,0:T(8,128)(2,1)}, u32[]{:S(2)}, u32[]{:S(2)}) %collective-permute-start.29) | collective-permute-done | bytes 933920 | tf_op jit(solution)/shard_map/ppermute | solution.py:451
  315.1 1.3 shard_map.96._
  317.1 15.4 %shard_map.97 = bf16[8192,256]{1,0:T(8,128)(2,1)} custom-call(s32[1]{0:T(128)} %bitcast.2.me_ref, s32[8,64]{1,0:T(8,128)S(1)} %get-tuple-element.128.offs_ref, s32[384]{0:T(512)S(1)} %reshape.26.ids_ref, s32[64]{0:T(128)S(1)} %copy-done.27, s32[64,128]{1,0:T(8,128)S(1)} %get-tuple-element.129.pos_ref, bf16[64,6,128,128]{3,2,1,0:T(8,128)(2,1)} %weight_ref.3, ...), custom_call_target="tpu_custom_call" | custom-call | flops 3221225472 | bytes 29360128 | tf_op jit(solution)/shard_map/pallas_call | solution.py:358
  332.5 3.6 %collective-permute-done.31.rest_3_ = bf16[1824,256]{1,0:T(8,128)(2,1)S(1)} collective-permute-done((bf16[1824,256]{1,0:T(8,128)(2,1)}, bf16[1824,256]{1,0:T(8,128)(2,1)S(1)}, u32[]{:S(2)}, u32[]{:S(2)}) %collective-permute-start.31) | collective-permute-done | bytes 933920 | tf_op jit(solution)/shard_map/ppermute | solution.py:451
  336.1 6.2 %shard_map.98 = bf16[8192,256]{1,0:T(8,128)(2,1)} custom-call(s32[1]{0:T(128)} %bitcast.2.me_ref, s32[8,64]{1,0:T(8,128)S(1)} %get-tuple-element.128.offs_ref, s32[64,128]{1,0:T(8,128)S(1)} %get-tuple-element.129.pos_ref, bf16[1824,256]{1,0:T(8,128)(2,1)S(1)} %get-tuple-element.172.rest_0_, bf16[1824,256]{1,0:T(8,128)(2,1)S(1)} %collective-permute-done.30.rest_1_, ...), custom_call_target="tpu_custom_call" | custom-call | flops 1073741824 | bytes 8388608 | tf_op jit(solution)/shard_map/pallas_call | solution.py:251
  (57 shorter events, 12.8 us)
Async XLA Ops:
  0.6 8.0 %copy-start.24 = (s32[8192]{0:T(1024)S(1)}, s32[8192]{0:T(1024)}, u32[]{:S(2)}) copy-start(s32[8192]{0:T(1024)} %param.11) | copy-start | bytes 98308
  0.6 8.0 %copy-start.22 = (bf16[8192,256]{1,0:T(8,128)(2,1)S(1)}, bf16[8192,256]{1,0:T(8,128)(2,1)}, u32[]{:S(2)}) copy-start(bf16[8192,256]{1,0:T(8,128)(2,1)} %param.10) | copy-start | bytes 12582916
  7.3 21.8 %collective-permute-start.18 = (bf16[1824,256]{1,0:T(8,128)(2,1)}, bf16[1824,256]{1,0:T(8,128)(2,1)S(1)}, u32[]{:S(2)}, u32[]{:S(2)}) collective-permute-start(bf16[1824,256]{1,0:T(8,128)(2,1)} %get-tuple-element.131), channel_id=1, source_target_pairs={{0,1},{1,2},{2,3},{3,0},{4,5},{5,6},{6,7},{7,4},{8,9},{9,10},{10,1... | collective-permute-start | bytes 2801672 | tf_op jit(solution)/shard_map/ppermute | solution.py:451
  8.7 8.4 %copy-start.25 = (s32[64,6]{0,1:T(8,128)S(1)}, s32[64,6]{0,1:T(8,128)}, u32[]{:S(2)}) copy-start(s32[64,6]{0,1:T(8,128)} %param.12) | copy-start | bytes 4612
  11.3 50.5 %collective-permute-start.17 = (bf16[8192,256]{1,0:T(8,128)(2,1)}, bf16[8192,256]{1,0:T(8,128)(2,1)}, u32[]{:S(2)}, u32[]{:S(2)}) collective-permute-start(bf16[8192,256]{1,0:T(8,128)(2,1)} %broadcast_multiply_fusion.1.own), channel_id=1, source_target_pairs={{4,8},{8,4},{5,9},{9,5},{6,10},{10,6},{7,11},{11,7},{20,24},{24,20... | collective-permute-start | bytes 12582920 | tf_op jit(solution)/shard_map/ppermute | solution.py:482
  15.3 46.5 %collective-permute-start.16 = (bf16[8192,256]{1,0:T(8,128)(2,1)}, bf16[8192,256]{1,0:T(8,128)(2,1)}, u32[]{:S(2)}, u32[]{:S(2)}) collective-permute-start(bf16[8192,256]{1,0:T(8,128)(2,1)} %broadcast_multiply_fusion.1.own), channel_id=1, source_target_pairs={{0,4},{8,12},{4,0},{12,8},{1,5},{9,13},{5,1},{13,9},{2,6},{10,14},... | collective-permute-start | bytes 12582920 | tf_op jit(solution)/shard_map/ppermute | solution.py:484
  15.4 113.0 %collective-permute-start.19 = (bf16[1824,256]{1,0:T(8,128)(2,1)}, bf16[1824,256]{1,0:T(8,128)(2,1)S(1)}, u32[]{:S(2)}, u32[]{:S(2)}) collective-permute-start(bf16[1824,256]{1,0:T(8,128)(2,1)} %get-tuple-element.134), channel_id=1, source_target_pairs={{0,2},{1,3},{2,0},{3,1},{4,6},{5,7},{6,4},{7,5},{8,10},{9,11},{10,... | collective-permute-start | bytes 2801672 | tf_op jit(solution)/shard_map/ppermute | solution.py:451
  16.4 74.8 %collective-permute-start.20 = (bf16[1824,256]{1,0:T(8,128)(2,1)}, bf16[1824,256]{1,0:T(8,128)(2,1)}, u32[]{:S(2)}, u32[]{:S(2)}) collective-permute-start(bf16[1824,256]{1,0:T(8,128)(2,1)} %get-tuple-element.135), channel_id=1, source_target_pairs={{0,3},{1,0},{2,1},{3,2},{4,7},{5,4},{6,5},{7,6},{8,11},{9,8},{10,9... | collective-permute-start | bytes 2801672 | tf_op jit(solution)/shard_map/ppermute | solution.py:451
  17.3 44.5 %copy-start.27 = (s32[64]{0:T(128)S(1)}, s32[64]{0:T(128)}, u32[]{:S(2)}) copy-start(s32[64]{0:T(128)} %counts_ref.3) | copy-start | bytes 772
  62.5 69.8 %copy-start.5 = (bf16[1824,256]{1,0:T(8,128)(2,1)S(1)}, bf16[1824,256]{1,0:T(8,128)(2,1)}, u32[]{:S(2)}) copy-start(bf16[1824,256]{1,0:T(8,128)(2,1)} %copy-done.4) | copy-start | bytes 2801668
  62.5 69.8 %copy-start.20 = (bf16[1024,1024]{1,0:T(8,128)(2,1)S(1)}, bf16[1024,1024]{1,0:T(8,128)(2,1)}, u32[]{:S(2)}) copy-start(bf16[1024,1024]{1,0:T(8,128)(2,1)} %op_ref.3) | copy-start | bytes 6291460
  79.5 0.9 copy-start.8
  91.2 48.8 %collective-permute-start.25 = (bf16[1824,256]{1,0:T(8,128)(2,1)S(1)}, bf16[1824,256]{1,0:T(8,128)(2,1)S(1)}, u32[]{:S(2)}, u32[]{:S(2)}) collective-permute-start(bf16[1824,256]{1,0:T(8,128)(2,1)S(1)} %get-tuple-element.151), channel_id=1, source_target_pairs={{0,3},{1,0},{2,1},{3,2},{4,7},{5,4},{6,5},{7,6},{8,11},{9,8},{10,9... | collective-permute-start | bytes 2801672 | tf_op jit(solution)/shard_map/ppermute | solution.py:451
  129.3 22.5 %collective-permute-start.23 = (bf16[1824,256]{1,0:T(8,128)(2,1)S(1)}, bf16[1824,256]{1,0:T(8,128)(2,1)S(1)}, u32[]{:S(2)}, u32[]{:S(2)}) collective-permute-start(bf16[1824,256]{1,0:T(8,128)(2,1)S(1)} %get-tuple-element.147), channel_id=1, source_target_pairs={{0,2},{1,3},{2,0},{3,1},{4,6},{5,7},{6,4},{7,5},{8,10},{9,11},{10,... | collective-permute-start | bytes 2801672 | tf_op jit(solution)/shard_map/ppermute | solution.py:451
  132.3 78.6 %collective-permute-start.21 = (bf16[1824,256]{1,0:T(8,128)(2,1)S(1)}, bf16[1824,256]{1,0:T(8,128)(2,1)S(1)}, u32[]{:S(2)}, u32[]{:S(2)}) collective-permute-start(bf16[1824,256]{1,0:T(8,128)(2,1)S(1)} %get-tuple-element.143), channel_id=1, source_target_pairs={{0,1},{1,2},{2,3},{3,0},{4,5},{5,6},{6,7},{7,4},{8,9},{9,10},{10,1... | collective-permute-start | bytes 2801672 | tf_op jit(solution)/shard_map/ppermute | solution.py:451
  132.3 1.2 copy-start.7
  140.0 0.9 copy-start.10
  141.0 97.1 %collective-permute-start.26 = (bf16[1824,256]{1,0:T(8,128)(2,1)}, bf16[1824,256]{1,0:T(8,128)(2,1)S(1)}, u32[]{:S(2)}, u32[]{:S(2)}) collective-permute-start(bf16[1824,256]{1,0:T(8,128)(2,1)} %get-tuple-element.152), channel_id=1, source_target_pairs={{0,3},{1,0},{2,1},{3,2},{4,7},{5,4},{6,5},{7,6},{8,11},{9,8},{10,9... | collective-permute-start | bytes 2801672 | tf_op jit(solution)/shard_map/ppermute | solution.py:451
  151.9 1.0 copy-start.12
  152.9 85.3 %collective-permute-start.24 = (bf16[1824,256]{1,0:T(8,128)(2,1)}, bf16[1824,256]{1,0:T(8,128)(2,1)}, u32[]{:S(2)}, u32[]{:S(2)}) collective-permute-start(bf16[1824,256]{1,0:T(8,128)(2,1)} %get-tuple-element.148), channel_id=1, source_target_pairs={{0,2},{1,3},{2,0},{3,1},{4,6},{5,7},{6,4},{7,5},{8,10},{9,11},{10,... | collective-permute-start | bytes 2801672 | tf_op jit(solution)/shard_map/ppermute | solution.py:451
  210.9 1.0 copy-start.14
  211.9 39.2 %collective-permute-start.22 = (bf16[1824,256]{1,0:T(8,128)(2,1)}, bf16[1824,256]{1,0:T(8,128)(2,1)}, u32[]{:S(2)}, u32[]{:S(2)}) collective-permute-start(bf16[1824,256]{1,0:T(8,128)(2,1)} %get-tuple-element.144), channel_id=1, source_target_pairs={{0,1},{1,2},{2,3},{3,0},{4,5},{5,6},{6,7},{7,4},{8,9},{9,10},{10,1... | collective-permute-start | bytes 2801672 | tf_op jit(solution)/shard_map/ppermute | solution.py:451
  226.5 1.2 copy-start.9
  227.6 1.2 copy-start.11
  228.8 1.2 copy-start.13
  230.0 1.2 copy-start.15
  251.1 64.0 %collective-permute-start.29 = (bf16[1824,256]{1,0:T(8,128)(2,1)}, bf16[1824,256]{1,0:T(8,128)(2,1)}, u32[]{:S(2)}, u32[]{:S(2)}) collective-permute-start(bf16[1824,256]{1,0:T(8,128)(2,1)} %get-tuple-element.166), channel_id=1, source_target_pairs={{0,2},{1,3},{2,0},{3,1},{4,6},{5,7},{6,4},{7,5},{8,10},{9,11},{10,... | collective-permute-start | bytes 2801672 | tf_op jit(solution)/shard_map/ppermute | solution.py:451
  261.5 54.9 %collective-permute-start.28 = (bf16[8192,256]{1,0:T(8,128)(2,1)}, bf16[8192,256]{1,0:T(8,128)(2,1)}, u32[]{:S(2)}, u32[]{:S(2)}) collective-permute-start(bf16[8192,256]{1,0:T(8,128)(2,1)} %shard_map.95.own), channel_id=1, source_target_pairs={{4,8},{8,4},{5,9},{9,5},{6,10},{10,6},{7,11},{11,7},{20,24},{24,20... | collective-permute-start | bytes 12582920 | tf_op jit(solution)/shard_map/ppermute | solution.py:482
  266.1 50.3 %collective-permute-start.27 = (bf16[8192,256]{1,0:T(8,128)(2,1)}, bf16[8192,256]{1,0:T(8,128)(2,1)}, u32[]{:S(2)}, u32[]{:S(2)}) collective-permute-start(bf16[8192,256]{1,0:T(8,128)(2,1)} %shard_map.95.own), channel_id=1, source_target_pairs={{0,4},{8,12},{4,0},{12,8},{1,5},{9,13},{5,1},{13,9},{2,6},{10,14},... | collective-permute-start | bytes 12582920 | tf_op jit(solution)/shard_map/ppermute | solution.py:484
  266.2 69.9 %collective-permute-start.31 = (bf16[1824,256]{1,0:T(8,128)(2,1)}, bf16[1824,256]{1,0:T(8,128)(2,1)S(1)}, u32[]{:S(2)}, u32[]{:S(2)}) collective-permute-start(bf16[1824,256]{1,0:T(8,128)(2,1)} %get-tuple-element.171), channel_id=1, source_target_pairs={{0,3},{1,0},{2,1},{3,2},{4,7},{5,4},{6,5},{7,6},{8,11},{9,8},{10,9... | collective-permute-start | bytes 2801672 | tf_op jit(solution)/shard_map/ppermute | solution.py:451
  267.3 68.8 %collective-permute-start.30 = (bf16[1824,256]{1,0:T(8,128)(2,1)}, bf16[1824,256]{1,0:T(8,128)(2,1)S(1)}, u32[]{:S(2)}, u32[]{:S(2)}) collective-permute-start(bf16[1824,256]{1,0:T(8,128)(2,1)} %get-tuple-element.169), channel_id=1, source_target_pairs={{0,1},{1,2},{2,3},{3,0},{4,5},{5,6},{6,7},{7,4},{8,9},{9,10},{10,1... | collective-permute-start | bytes 2801672 | tf_op jit(solution)/shard_map/ppermute | solution.py:451
  332.5 9.8 %copy-start.26 = (s32[64,6]{0,1:T(8,128)S(1)}, s32[64,6]{0,1:T(8,128)}, u32[]{:S(2)}) copy-start(s32[64,6]{0,1:T(8,128)} %param.12) | copy-start | bytes 4612
  (4 other events, 3.3 us)

commit v5 on v4

--- a/solution.py
+++ b/solution.py
@@ -9,10 +9,10 @@
 
 MIB = 1024 * 1024
 ALIGN = 16
-DEPTH = 3
+DEPTH = 4
 PAIR = 2
 EXPAND = 1
-GROUP = 8
+GROUP = 16
 
 
 def params(mib):
@@ -201,20 +201,46 @@
     return pos, offs, tuple(parts)
 
 
+def load_owner(packed, ins, sems, me, owner):
+    count = len(ins)
+    size = ins[0].shape[0]
+    for shift, part in enumerate(ins):
+
+        @pl.when(lax.rem(me + count - shift, count) == owner)
+        def _():
+            pltpu.make_async_copy(
+                part, packed.at[pl.ds(owner * size, size), :], sems.at[owner]
+            ).start()
+
+
 def expand_kernel(me_ref, offs_ref, pos_ref, *rest):
     ins, (out_ref, packed, tiles, sems, out_sems) = rest[:-5], rest[-5:]
     nblk, block_rows = pos_ref.shape
     rounds = nblk // GROUP
     span = EXPAND * block_rows
     held = len(ins) * ins[0].shape[0]
-    copies = part_copies(packed, ins, sems, me_ref[0], False)
-    for copy in copies:
-        copy.start()
+    size = ins[0].shape[0]
+    for piece in range(len(ins)):
+        load_owner(packed, ins, sems, me_ref[0], piece)
     clear(packed, held)
-    for copy in copies:
-        copy.wait()
+
+    def need(step):
+        end = window(offs_ref, (step + 1) * GROUP - EXPAND) + span + ALIGN
+        return jnp.where(step == rounds - 1, held, jnp.minimum(end, held))
+
+    def arrive(step):
+        before = jnp.where(step == 0, 0, need(jnp.maximum(step - 1, 0)))
+        now = need(step)
+        for owner in range(len(ins)):
+
+            @pl.when((owner * size >= before) & (owner * size < now))
+            def _():
+                pltpu.make_async_copy(
+                    ins[0], packed.at[pl.ds(owner * size, size), :], sems.at[owner]
+                ).wait()
 
     def body(step, carry):
+        arrive(step)
         pos = pos_ref[pl.ds(pl.multiple_of(step * GROUP, GROUP), GROUP), :]
         made = []
         for i in range(0, GROUP, EXPAND):
@@ -230,12 +256,14 @@
                     preferred_element_type=jnp.float32,
                 ).astype(jnp.bfloat16)
             )
-        size = GROUP * block_rows
-        base = pl.multiple_of(step * size, size)
+        step_rows = GROUP * block_rows
+        base = pl.multiple_of(step * step_rows, step_rows)
         for i, rows in enumerate(made):
             tiles[pl.ds(pl.multiple_of(base + i * span, span), span), :] = rows
         pltpu.make_async_copy(
-            tiles.at[pl.ds(base, size)], out_ref.at[pl.ds(base, size)], out_sems.at[step]
+            tiles.at[pl.ds(base, step_rows)],
+            out_ref.at[pl.ds(base, step_rows)],
+            out_sems.at[step],
         ).start()
         return carry
 

time: 344 us -> 340 us (0.988)
  waiting for transfers between devices: 220 us -> 204 us
  blocking collectives: 11 us -> 21.2 us
  starting transfers between devices: 25.5 us -> 31.8 us
  Pallas kernels: 67.4 us -> 61.9 us
    ppermute x12, waiting for transfers between devices: 189 us -> 167 us  [exchange(): lax.ppermute(part, 'chan', [(i, (i + shift) % count) for i in range(count)])]
    ppermute x2, starting transfers between devices: 8.57 us -> 19.1 us  [halo_of(): far = lax.ppermute(x, 'orbit', far + [(b, a) for a, b in far])]
    pmax x1, blocking collectives: 11 us -> 21.2 us  [overfull(): return lax.pmax(more.astype(jnp.int32), ('grp', 'orbit'))]
    ppermute x2, waiting for transfers between devices: 30.5 us -> 37.6 us  [halo_of(): far = lax.ppermute(x, 'orbit', far + [(b, a) for a, b in far])]
    ppermute x12, starting transfers between devices: 16.8 us -> 12.6 us  [exchange(): lax.ppermute(part, 'chan', [(i, (i + shift) % count) for i in range(count)])]
  transfers between devices with their start and end apart: 16 -> 16, of which waited for: 9 -> 9; matrix products, arithmetic and copies ran while one was open for 1% -> 1% of each run, Pallas kernels for 16% -> 15%
where the time goes in v5:
time: 340 us; the launch traced here: 338 us
  waiting for transfers between devices  204 us (60%)
  Pallas kernels  61.9 us (18%)
  starting transfers between devices  31.8 us (9%)
  blocking collectives  21.2 us (6%)
  local copies, waits for them, and re-layouts  13.2 us (4%)
    ppermute x12, waiting for transfers between devices, exchange(): lax.ppermute(part, 'chan', [(i, (i + shift) % count) for i in range(count)])  167 us
    ppermute x2, waiting for transfers between devices, halo_of(): far = lax.ppermute(x, 'orbit', far + [(b, a) for a, b in far])  37.6 us
    pallas_call x2, Pallas kernels, spatial(): pl.pallas_call(functools.partial(spatial_kernel, size is not None), out_s...  29.9 us
    pmax x1, blocking collectives, overfull(): return lax.pmax(more.astype(jnp.int32), ('grp', 'orbit'))  21.2 us
    ppermute x2, starting transfers between devices, halo_of(): far = lax.ppermute(x, 'orbit', far + [(b, a) for a, b in far])  19.1 us
    pallas_call x2, Pallas kernels, mix(): pl.pallas_call(functools.partial(mix_kernel, count), out_shape=part_shape...  13.4 us
    unnamed x40, local copies, waits for them, and re-layouts  13 us
    ppermute x12, starting transfers between devices, exchange(): lax.ppermute(part, 'chan', [(i, (i + shift) % count) for i in range(count)])  12.6 us
  transfers between devices with their start and end apart: 16, of which 9 were waited for; matrix products, arithmetic and copies ran while one was open for 1% of the time, Pallas kernels for 15%

profile of v5, /device:TPU:11, one launch (start us, length us, event | category | flops | bytes accessed | tf_op | source)
XLA Modules:
  0.0 338.4 jit_solution(3795067024562080436)
XLA Ops:
  0.7 6.3 %shard_map.90 = (s32[64,128]{1,0:T(8,128)S(1)}, s32[8,64]{1,0:T(8,128)S(1)}, bf16[1824,256]{1,0:T(8,128)(2,1)S(1)}, bf16[1824,256]{1,0:T(8,128)(2,1)}, bf16[1824...) custom-call(s32[1]{0:T(128)} %bitcast.2.me_ref, s32[64,128]{1,0:T(8,128)} %bitcast.4, bf16[8192,256]{1,0:T(8,128)(2,1)} %v_ref.1), custom_call_target="tpu_custom_call" | custom-call | flops 1140850688 | bytes 8388608 | tf_op jit(solution)/shard_map/pallas_call | solution.py:172
  8.0 2.6 broadcast_multiply_fusion.1.own
  10.7 4.0 %collective-permute-start.17 = (bf16[8192,256]{1,0:T(8,128)(2,1)}, bf16[8192,256]{1,0:T(8,128)(2,1)}, u32[]{:S(2)}, u32[]{:S(2)}) collective-permute-start(bf16[8192,256]{1,0:T(8,128)(2,1)} %broadcast_multiply_fusion.1.own), channel_id=1, source_target_pairs={{4,8},{8,4},{5,9},{9,5},{6,10},{10,6},{7,11},{11,7},{20,24},{24,20... | collective-permute-start | bytes 12582920 | tf_op jit(solution)/shard_map/ppermute | solution.py:510
  14.7 1.3 collective-permute-start.19
  16.0 1.2 collective-permute-start.20
  17.5 11.2 %collective-permute-done.18.x_ref.rest_1_ = bf16[1824,256]{1,0:T(8,128)(2,1)S(1)} collective-permute-done((bf16[1824,256]{1,0:T(8,128)(2,1)}, bf16[1824,256]{1,0:T(8,128)(2,1)S(1)}, u32[]{:S(2)}, u32[]{:S(2)}) %collective-permute-start.18) | collective-permute-done | bytes 933920 | tf_op jit(solution)/shard_map/ppermute | solution.py:479
  29.7 1.3 shard_map.91._
  31.0 30.1 %collective-permute-done.17.far = bf16[8192,256]{1,0:T(8,128)(2,1)} collective-permute-done((bf16[8192,256]{1,0:T(8,128)(2,1)}, bf16[8192,256]{1,0:T(8,128)(2,1)}, u32[]{:S(2)}, u32[]{:S(2)}) %collective-permute-start.17) | collective-permute-done | bytes 4194336 | tf_op jit(solution)/shard_map/ppermute | solution.py:510
  61.8 15.8 %shard_map.92 = (bf16[1824,256]{1,0:T(8,128)(2,1)S(1)}, bf16[1824,256]{1,0:T(8,128)(2,1)S(1)}, bf16[1824,256]{1,0:T(8,128)(2,1)}, bf16[1824,256]{1,0:T(8,128)(2,1)S(1)}) custom-call(s32[1]{0:T(128)} %bitcast.2.me_ref, s32[8,64]{1,0:T(8,128)S(1)} %get-tuple-element.126.offs_ref, s32[384]{0:T(512)S(1)} %reshape.26.ids_ref, s32[64]{0:T(128)S(1)} %copy-done.27, ...), custom_call_target="tpu_custom_call" | custom-call | flops 3221225472 | bytes 29360128 | tf_op jit(solution)/shard_map/pallas_call | solution.py:386
  79.0 1.0 collective-permute-start.24
  80.1 27.7 %collective-permute-done.19.rest_2_ = bf16[1824,256]{1,0:T(8,128)(2,1)S(1)} collective-permute-done((bf16[1824,256]{1,0:T(8,128)(2,1)}, bf16[1824,256]{1,0:T(8,128)(2,1)S(1)}, u32[]{:S(2)}, u32[]{:S(2)}) %collective-permute-start.19) | collective-permute-done | bytes 933920 | tf_op jit(solution)/shard_map/ppermute | solution.py:479
  108.7 1.2 copy-done.7
  109.9 6.5 %shard_map.93 = (bf16[1824,256]{1,0:T(8,128)(2,1)S(1)}, bf16[1824,256]{1,0:T(8,128)(2,1)}, bf16[1824,256]{1,0:T(8,128)(2,1)}, bf16[1824,256]{1,0:T(8,128)(2,1)}) custom-call(s32[1]{0:T(128)} %bitcast.2.me_ref, bf16[1024,1024]{1,0:T(8,128)(2,1)S(1)} %copy-done.20, bf16[1824,256]{1,0:T(8,128)(2,1)S(1)} %get-tuple-element.134.rest_0_, ...), custom_call_target="tpu_custom_call" | custom-call | flops 1 | bytes 1 | tf_op jit(solution)/shard_map/pallas_call | solution.py:449
  116.5 3.0 collective-permute-start.26
  119.5 48.8 %collective-permute-done.22.rest_3_ = bf16[1824,256]{1,0:T(8,128)(2,1)S(1)} collective-permute-done((bf16[1824,256]{1,0:T(8,128)(2,1)S(1)}, bf16[1824,256]{1,0:T(8,128)(2,1)S(1)}, u32[]{:S(2)}, u32[]{:S(2)}) %collective-permute-start.22) | collective-permute-done | bytes 933920 | tf_op jit(solution)/shard_map/ppermute | solution.py:479
  172.1 21.2 %pmax.7 = s32[]{:T(128)} all-reduce(s32[]{:T(128)S(6)} %convert_element_type.13), channel_id=1, replica_groups=mesh['grp'=2,'orbit'=4,'chan'=4] {'grp','orbit'}, use_global_device_ids=true, to_apply=%region_1.2 | all-reduce | flops 1 | bytes 8 | tf_op jit(solution)/shard_map/pmax | solution.py:568
  193.3 34.5 %collective-permute-done.26.rest_2_ = bf16[1824,256]{1,0:T(8,128)(2,1)S(1)} collective-permute-done((bf16[1824,256]{1,0:T(8,128)(2,1)}, bf16[1824,256]{1,0:T(8,128)(2,1)S(1)}, u32[]{:S(2)}, u32[]{:S(2)}) %collective-permute-start.26) | collective-permute-done | bytes 933920 | tf_op jit(solution)/shard_map/ppermute | solution.py:479
  228.8 1.2 copy-done.9
  230.0 1.2 copy-done.11
  231.2 1.2 copy-done.13
  232.4 1.2 copy-done.15
  233.5 6.9 %shard_map.94 = (bf16[1824,256]{1,0:T(8,128)(2,1)S(1)}, bf16[1824,256]{1,0:T(8,128)(2,1)}, bf16[1824,256]{1,0:T(8,128)(2,1)}, bf16[1824,256]{1,0:T(8,128)(2,1)}) custom-call(s32[1]{0:T(128)} %bitcast.2.me_ref, bf16[1024,1024]{1,0:T(8,128)(2,1)} %op_ref.3, bf16[1824,256]{1,0:T(8,128)(2,1)S(1)} %copy-done.9, bf16[1824,256]{1,0:T(8,128)(2,1)S(1)} %copy-done.13, ...), custom_call_target="tpu_custom_call" | custom-call | flops 1 | bytes 1 | tf_op jit(solution)/shard_map/pallas_call | solution.py:449
  240.5 7.4 %collective-permute-done.23.rest_2_ = bf16[1824,256]{1,0:T(8,128)(2,1)} collective-permute-done((bf16[1824,256]{1,0:T(8,128)(2,1)}, bf16[1824,256]{1,0:T(8,128)(2,1)}, u32[]{:S(2)}, u32[]{:S(2)}) %collective-permute-start.23) | collective-permute-done | bytes 933920 | tf_op jit(solution)/shard_map/ppermute | solution.py:479
  248.5 2.5 collective-permute-start.29
  251.6 4.7 %shard_map.95.own = bf16[8192,256]{1,0:T(8,128)(2,1)} custom-call(s32[1]{0:T(128)} %bitcast.2.me_ref, s32[8,64]{1,0:T(8,128)S(1)} %get-tuple-element.126.offs_ref, s32[64,128]{1,0:T(8,128)S(1)} %get-tuple-element.127.pos_ref, bf16[1824,256]{1,0:T(8,128)(2,1)S(1)} %get-tuple-element.155.rest_0_, bf16[1824,256]{1,0:T(8,128)(2,1)S(1)} %collective-permute-done.21.rest_1_, ...), custom_call_target="tpu_custom_call" | custom-call | flops 1073741824 | bytes 8388608 | tf_op jit(solution)/shard_map/pallas_call | solution.py:279
  256.3 15.1 %collective-permute-start.28 = (bf16[8192,256]{1,0:T(8,128)(2,1)}, bf16[8192,256]{1,0:T(8,128)(2,1)}, u32[]{:S(2)}, u32[]{:S(2)}) collective-permute-start(bf16[8192,256]{1,0:T(8,128)(2,1)} %shard_map.95.own), channel_id=1, source_target_pairs={{4,8},{8,4},{5,9},{9,5},{6,10},{10,6},{7,11},{11,7},{20,24},{24,20... | collective-permute-start | bytes 12582920 | tf_op jit(solution)/shard_map/ppermute | solution.py:510
  271.6 1.5 collective-permute-start.30
  273.1 36.4 %collective-permute-done.29.x_ref.rest_2_ = bf16[1824,256]{1,0:T(8,128)(2,1)} collective-permute-done((bf16[1824,256]{1,0:T(8,128)(2,1)}, bf16[1824,256]{1,0:T(8,128)(2,1)}, u32[]{:S(2)}, u32[]{:S(2)}) %collective-permute-start.29) | collective-permute-done | bytes 933920 | tf_op jit(solution)/shard_map/ppermute | solution.py:479
  309.5 1.3 shard_map.96._
  310.7 7.4 %collective-permute-done.28.far = bf16[8192,256]{1,0:T(8,128)(2,1)} collective-permute-done((bf16[8192,256]{1,0:T(8,128)(2,1)}, bf16[8192,256]{1,0:T(8,128)(2,1)}, u32[]{:S(2)}, u32[]{:S(2)}) %collective-permute-start.28) | collective-permute-done | bytes 4194336 | tf_op jit(solution)/shard_map/ppermute | solution.py:510
  318.9 14.1 %shard_map.97 = bf16[8192,256]{1,0:T(8,128)(2,1)} custom-call(s32[1]{0:T(128)} %bitcast.2.me_ref, s32[8,64]{1,0:T(8,128)S(1)} %get-tuple-element.126.offs_ref, s32[384]{0:T(512)S(1)} %reshape.26.ids_ref, s32[64]{0:T(128)S(1)} %copy-done.27, s32[64,128]{1,0:T(8,128)S(1)} %get-tuple-element.127.pos_ref, bf16[64,6,128,128]{3,2,1,0:T(8,128)(2,1)} %weight_ref.3, ...), custom_call_target="tpu_custom_call" | custom-call | flops 3221225472 | bytes 29360128 | tf_op jit(solution)/shard_map/pallas_call | solution.py:386
  333.0 5.0 %shard_map.98 = bf16[8192,256]{1,0:T(8,128)(2,1)} custom-call(s32[1]{0:T(128)} %bitcast.2.me_ref, s32[8,64]{1,0:T(8,128)S(1)} %get-tuple-element.126.offs_ref, s32[64,128]{1,0:T(8,128)S(1)} %get-tuple-element.127.pos_ref, bf16[1824,256]{1,0:T(8,128)(2,1)S(1)} %get-tuple-element.169.rest_0_, bf16[1824,256]{1,0:T(8,128)(2,1)S(1)} %collective-permute-done.30.rest_1_, ...), custom_call_target="tpu_custom_call" | custom-call | flops 1073741824 | bytes 8388608 | tf_op jit(solution)/shard_map/pallas_call | solution.py:279
  (57 shorter events, 11.1 us)
Async XLA Ops:
  0.6 7.4 %copy-start.24 = (s32[8192]{0:T(1024)S(1)}, s32[8192]{0:T(1024)}, u32[]{:S(2)}) copy-start(s32[8192]{0:T(1024)} %param.11) | copy-start | bytes 98308
  0.6 7.4 %copy-start.22 = (bf16[8192,256]{1,0:T(8,128)(2,1)S(1)}, bf16[8192,256]{1,0:T(8,128)(2,1)}, u32[]{:S(2)}) copy-start(bf16[8192,256]{1,0:T(8,128)(2,1)} %param.10) | copy-start | bytes 12582916
  6.9 21.8 %collective-permute-start.18 = (bf16[1824,256]{1,0:T(8,128)(2,1)}, bf16[1824,256]{1,0:T(8,128)(2,1)S(1)}, u32[]{:S(2)}, u32[]{:S(2)}) collective-permute-start(bf16[1824,256]{1,0:T(8,128)(2,1)} %get-tuple-element.129), channel_id=1, source_target_pairs={{0,1},{1,2},{2,3},{3,0},{4,5},{5,6},{6,7},{7,4},{8,9},{9,10},{10,1... | collective-permute-start | bytes 2801672 | tf_op jit(solution)/shard_map/ppermute | solution.py:479
  8.0 9.3 %copy-start.25 = (s32[64,6]{0,1:T(8,128)S(1)}, s32[64,6]{0,1:T(8,128)}, u32[]{:S(2)}) copy-start(s32[64,6]{0,1:T(8,128)} %param.12) | copy-start | bytes 4612
  10.7 50.5 %collective-permute-start.17 = (bf16[8192,256]{1,0:T(8,128)(2,1)}, bf16[8192,256]{1,0:T(8,128)(2,1)}, u32[]{:S(2)}, u32[]{:S(2)}) collective-permute-start(bf16[8192,256]{1,0:T(8,128)(2,1)} %broadcast_multiply_fusion.1.own), channel_id=1, source_target_pairs={{4,8},{8,4},{5,9},{9,5},{6,10},{10,6},{7,11},{11,7},{20,24},{24,20... | collective-permute-start | bytes 12582920 | tf_op jit(solution)/shard_map/ppermute | solution.py:510
  14.6 46.5 %collective-permute-start.16 = (bf16[8192,256]{1,0:T(8,128)(2,1)}, bf16[8192,256]{1,0:T(8,128)(2,1)}, u32[]{:S(2)}, u32[]{:S(2)}) collective-permute-start(bf16[8192,256]{1,0:T(8,128)(2,1)} %broadcast_multiply_fusion.1.own), channel_id=1, source_target_pairs={{0,4},{8,12},{4,0},{12,8},{1,5},{9,13},{5,1},{13,9},{2,6},{10,14},... | collective-permute-start | bytes 12582920 | tf_op jit(solution)/shard_map/ppermute | solution.py:512
  14.7 93.1 %collective-permute-start.19 = (bf16[1824,256]{1,0:T(8,128)(2,1)}, bf16[1824,256]{1,0:T(8,128)(2,1)S(1)}, u32[]{:S(2)}, u32[]{:S(2)}) collective-permute-start(bf16[1824,256]{1,0:T(8,128)(2,1)} %get-tuple-element.132), channel_id=1, source_target_pairs={{0,2},{1,3},{2,0},{3,1},{4,6},{5,7},{6,4},{7,5},{8,10},{9,11},{10,... | collective-permute-start | bytes 2801672 | tf_op jit(solution)/shard_map/ppermute | solution.py:479
  16.0 92.7 %collective-permute-start.20 = (bf16[1824,256]{1,0:T(8,128)(2,1)}, bf16[1824,256]{1,0:T(8,128)(2,1)}, u32[]{:S(2)}, u32[]{:S(2)}) collective-permute-start(bf16[1824,256]{1,0:T(8,128)(2,1)} %get-tuple-element.133), channel_id=1, source_target_pairs={{0,3},{1,0},{2,1},{3,2},{4,7},{5,4},{6,5},{7,6},{8,11},{9,8},{10,9... | collective-permute-start | bytes 2801672 | tf_op jit(solution)/shard_map/ppermute | solution.py:479
  17.5 43.6 %copy-start.27 = (s32[64]{0:T(128)S(1)}, s32[64]{0:T(128)}, u32[]{:S(2)}) copy-start(s32[64]{0:T(128)} %counts_ref.3) | copy-start | bytes 772
  61.8 46.9 %copy-start.5 = (bf16[1824,256]{1,0:T(8,128)(2,1)S(1)}, bf16[1824,256]{1,0:T(8,128)(2,1)}, u32[]{:S(2)}) copy-start(bf16[1824,256]{1,0:T(8,128)(2,1)} %copy-done.4) | copy-start | bytes 2801668
  61.8 46.9 %copy-start.20 = (bf16[1024,1024]{1,0:T(8,128)(2,1)S(1)}, bf16[1024,1024]{1,0:T(8,128)(2,1)}, u32[]{:S(2)}) copy-start(bf16[1024,1024]{1,0:T(8,128)(2,1)} %op_ref.3) | copy-start | bytes 6291460
  77.6 0.9 copy-start.8
  78.6 89.7 %collective-permute-start.22 = (bf16[1824,256]{1,0:T(8,128)(2,1)S(1)}, bf16[1824,256]{1,0:T(8,128)(2,1)S(1)}, u32[]{:S(2)}, u32[]{:S(2)}) collective-permute-start(bf16[1824,256]{1,0:T(8,128)(2,1)S(1)} %get-tuple-element.143), channel_id=1, source_target_pairs={{0,3},{1,0},{2,1},{3,2},{4,7},{5,4},{6,5},{7,6},{8,11},{9,8},{10,9... | collective-permute-start | bytes 2801672 | tf_op jit(solution)/shard_map/ppermute | solution.py:479
  79.0 90.3 %collective-permute-start.24 = (bf16[1824,256]{1,0:T(8,128)(2,1)S(1)}, bf16[1824,256]{1,0:T(8,128)(2,1)S(1)}, u32[]{:S(2)}, u32[]{:S(2)}) collective-permute-start(bf16[1824,256]{1,0:T(8,128)(2,1)S(1)} %get-tuple-element.146), channel_id=1, source_target_pairs={{0,1},{1,2},{2,3},{3,0},{4,5},{5,6},{6,7},{7,4},{8,9},{9,10},{10,1... | collective-permute-start | bytes 2801672 | tf_op jit(solution)/shard_map/ppermute | solution.py:479
  108.7 1.2 copy-start.7
  116.4 124.1 %collective-permute-start.21 = (bf16[1824,256]{1,0:T(8,128)(2,1)}, bf16[1824,256]{1,0:T(8,128)(2,1)S(1)}, u32[]{:S(2)}, u32[]{:S(2)}) collective-permute-start(bf16[1824,256]{1,0:T(8,128)(2,1)} %get-tuple-element.140), channel_id=1, source_target_pairs={{0,1},{1,2},{2,3},{3,0},{4,5},{5,6},{6,7},{7,4},{8,9},{9,10},{10,1... | collective-permute-start | bytes 2801672 | tf_op jit(solution)/shard_map/ppermute | solution.py:479
  116.5 111.4 %collective-permute-start.26 = (bf16[1824,256]{1,0:T(8,128)(2,1)}, bf16[1824,256]{1,0:T(8,128)(2,1)S(1)}, u32[]{:S(2)}, u32[]{:S(2)}) collective-permute-start(bf16[1824,256]{1,0:T(8,128)(2,1)} %get-tuple-element.149), channel_id=1, source_target_pairs={{0,2},{1,3},{2,0},{3,1},{4,6},{5,7},{6,4},{7,5},{8,10},{9,11},{10,... | collective-permute-start | bytes 2801672 | tf_op jit(solution)/shard_map/ppermute | solution.py:479
  168.3 1.0 copy-start.10
  169.3 78.6 %collective-permute-start.23 = (bf16[1824,256]{1,0:T(8,128)(2,1)}, bf16[1824,256]{1,0:T(8,128)(2,1)}, u32[]{:S(2)}, u32[]{:S(2)}) collective-permute-start(bf16[1824,256]{1,0:T(8,128)(2,1)} %get-tuple-element.144), channel_id=1, source_target_pairs={{0,2},{1,3},{2,0},{3,1},{4,6},{5,7},{6,4},{7,5},{8,10},{9,11},{10,... | collective-permute-start | bytes 2801672 | tf_op jit(solution)/shard_map/ppermute | solution.py:479
  169.3 0.9 copy-start.12
  170.2 78.2 %collective-permute-start.25 = (bf16[1824,256]{1,0:T(8,128)(2,1)}, bf16[1824,256]{1,0:T(8,128)(2,1)}, u32[]{:S(2)}, u32[]{:S(2)}) collective-permute-start(bf16[1824,256]{1,0:T(8,128)(2,1)} %get-tuple-element.147), channel_id=1, source_target_pairs={{0,3},{1,0},{2,1},{3,2},{4,7},{5,4},{6,5},{7,6},{8,11},{9,8},{10,9... | collective-permute-start | bytes 2801672 | tf_op jit(solution)/shard_map/ppermute | solution.py:479
  227.8 1.0 copy-start.14
  228.8 1.2 copy-start.9
  230.0 1.2 copy-start.11
  231.2 1.2 copy-start.13
  232.4 1.2 copy-start.15
  248.5 61.0 %collective-permute-start.29 = (bf16[1824,256]{1,0:T(8,128)(2,1)}, bf16[1824,256]{1,0:T(8,128)(2,1)}, u32[]{:S(2)}, u32[]{:S(2)}) collective-permute-start(bf16[1824,256]{1,0:T(8,128)(2,1)} %get-tuple-element.163), channel_id=1, source_target_pairs={{0,2},{1,3},{2,0},{3,1},{4,6},{5,7},{6,4},{7,5},{8,10},{9,11},{10,... | collective-permute-start | bytes 2801672 | tf_op jit(solution)/shard_map/ppermute | solution.py:479
  256.3 61.8 %collective-permute-start.28 = (bf16[8192,256]{1,0:T(8,128)(2,1)}, bf16[8192,256]{1,0:T(8,128)(2,1)}, u32[]{:S(2)}, u32[]{:S(2)}) collective-permute-start(bf16[8192,256]{1,0:T(8,128)(2,1)} %shard_map.95.own), channel_id=1, source_target_pairs={{4,8},{8,4},{5,9},{9,5},{6,10},{10,6},{7,11},{11,7},{20,24},{24,20... | collective-permute-start | bytes 12582920 | tf_op jit(solution)/shard_map/ppermute | solution.py:510
  271.5 46.7 %collective-permute-start.27 = (bf16[8192,256]{1,0:T(8,128)(2,1)}, bf16[8192,256]{1,0:T(8,128)(2,1)}, u32[]{:S(2)}, u32[]{:S(2)}) collective-permute-start(bf16[8192,256]{1,0:T(8,128)(2,1)} %shard_map.95.own), channel_id=1, source_target_pairs={{0,4},{8,12},{4,0},{12,8},{1,5},{9,13},{5,1},{13,9},{2,6},{10,14},... | collective-permute-start | bytes 12582920 | tf_op jit(solution)/shard_map/ppermute | solution.py:512
  271.6 61.5 %collective-permute-start.31 = (bf16[1824,256]{1,0:T(8,128)(2,1)}, bf16[1824,256]{1,0:T(8,128)(2,1)S(1)}, u32[]{:S(2)}, u32[]{:S(2)}) collective-permute-start(bf16[1824,256]{1,0:T(8,128)(2,1)} %get-tuple-element.168), channel_id=1, source_target_pairs={{0,3},{1,0},{2,1},{3,2},{4,7},{5,4},{6,5},{7,6},{8,11},{9,8},{10,9... | collective-permute-start | bytes 2801672 | tf_op jit(solution)/shard_map/ppermute | solution.py:479
  271.6 61.4 %collective-permute-start.30 = (bf16[1824,256]{1,0:T(8,128)(2,1)}, bf16[1824,256]{1,0:T(8,128)(2,1)S(1)}, u32[]{:S(2)}, u32[]{:S(2)}) collective-permute-start(bf16[1824,256]{1,0:T(8,128)(2,1)} %get-tuple-element.166), channel_id=1, source_target_pairs={{0,1},{1,2},{2,3},{3,0},{4,5},{5,6},{6,7},{7,4},{8,9},{9,10},{10,1... | collective-permute-start | bytes 2801672 | tf_op jit(solution)/shard_map/ppermute | solution.py:479
  333.0 5.0 %copy-start.26 = (s32[64,6]{0,1:T(8,128)S(1)}, s32[64,6]{0,1:T(8,128)}, u32[]{:S(2)}) copy-start(s32[64,6]{0,1:T(8,128)} %param.12) | copy-start | bytes 4612
  (4 other events, 3.3 us)

commit v6 on v5

--- a/solution.py
+++ b/solution.py
@@ -299,12 +299,17 @@
     )(me, offs, pos, *parts)
 
 
+def rounds_of(nblk, compacting):
+    return nblk // GROUP if compacting else max(nblk // (2 * GROUP), 1)
+
+
 def spatial_kernel(
     compacting, me_ref, offs_ref, ids_ref, counts_ref, pos_ref, weight_ref, near, own, far, _, *rest
 ):
     nblk, block_rows = pos_ref.shape
     slots = weight_ref.shape[1]
-    rounds = nblk // GROUP
+    rounds = rounds_of(nblk, compacting)
+    group = nblk // rounds
     scratch = 6
     outs, (tiles, weights, halo_sems, weight_sems, made, sems) = rest[:-scratch], rest[-scratch:]
     rows = tiles.shape[0] // 3
@@ -322,7 +327,7 @@
         copy.wait()
 
     def product(step, i):
-        block = step * GROUP + i
+        block = step * group + i
         used = counts_ref[block]
         live = []
         picked = []
@@ -340,23 +345,23 @@
 
     def body(step, carry):
         group_wait(weight_ref, weights, weight_sems, step)
-        pos = pos_ref[pl.ds(pl.multiple_of(step * GROUP, GROUP), GROUP), :]
-        found = [product(step, i) for i in range(GROUP)]
+        pos = pos_ref[pl.ds(pl.multiple_of(step * group, group), group), :]
+        found = [product(step, i) for i in range(group)]
         if compacting:
             found = [
-                jnp.concatenate(found[i : i + PAIR], axis=0) for i in range(0, GROUP, PAIR)
+                jnp.concatenate(found[i : i + PAIR], axis=0) for i in range(0, group, PAIR)
             ]
             pack_round(step, rounds, pos, offs_ref, found, made, outs, sems, me_ref[0])
             return carry
-        a = lax.broadcasted_iota(jnp.int32, (block_rows, block_rows), 0)
-        b = lax.broadcasted_iota(jnp.int32, (block_rows, block_rows), 1)
-        size = GROUP * block_rows
+        size = group * block_rows
         base = pl.multiple_of(step * size, size)
-        for i in range(GROUP):
-            kept = jnp.where((a == b) & (pos[i : i + 1, :] >= 0), 1.0, 0.0).astype(jnp.bfloat16)
-            made[pl.ds(pl.multiple_of(base + i * block_rows, block_rows), block_rows), :] = jnp.dot(
-                kept, found[i], preferred_element_type=jnp.float32
-            ).astype(jnp.bfloat16)
+        for i in range(group):
+            kept = jnp.where(pos[i : i + 1, :] >= 0, 1.0, 0.0)
+            kept = jnp.broadcast_to(kept, (block_rows, block_rows)).T.astype(jnp.bfloat16)
+            kept = jnp.concatenate([kept] * (made.shape[1] // block_rows), axis=1)
+            made[pl.ds(pl.multiple_of(base + i * block_rows, block_rows), block_rows), :] = (
+                found[i] * kept
+            )
         pltpu.make_async_copy(
             made.at[pl.ds(base, size)], outs[0].at[pl.ds(base, size)], sems.at[step]
         ).start()
@@ -376,7 +381,7 @@
     nblk, block_rows = pos.shape
     slots = weights.shape[1]
     any_spec = pl.BlockSpec(memory_space=pl.ANY)
-    rounds = nblk // GROUP
+    rounds = rounds_of(nblk, size is not None)
     if size is None:
         shapes = (jax.ShapeDtypeStruct((rows, width), jnp.bfloat16),)
         made = (rows, rounds)

time: 340 us -> 338 us (level)
  transfers between devices with their start and end apart: 16 -> 16, of which waited for: 9 -> 9; matrix products, arithmetic and copies ran while one was open for 1% -> 1% of each run, Pallas kernels for 15% -> 14%
where the time goes in v6:
time: 338 us; the launch traced here: 337 us
  waiting for transfers between devices  204 us (60%)
  Pallas kernels  59.9 us (18%)
  starting transfers between devices  31.9 us (9%)
  blocking collectives  21.3 us (6%)
  local copies, waits for them, and re-layouts  13.2 us (4%)
    ppermute x12, waiting for transfers between devices, exchange(): lax.ppermute(part, 'chan', [(i, (i + shift) % count) for i in range(count)])  166 us
    ppermute x2, waiting for transfers between devices, halo_of(): far = lax.ppermute(x, 'orbit', far + [(b, a) for a, b in far])  37.7 us
    pallas_call x2, Pallas kernels, spatial(): pl.pallas_call(functools.partial(spatial_kernel, size is not None), out_s...  28 us
    pmax x1, blocking collectives, overfull(): return lax.pmax(more.astype(jnp.int32), ('grp', 'orbit'))  21.3 us
    ppermute x2, starting transfers between devices, halo_of(): far = lax.ppermute(x, 'orbit', far + [(b, a) for a, b in far])  19.2 us
    pallas_call x2, Pallas kernels, mix(): pl.pallas_call(functools.partial(mix_kernel, count), out_shape=part_shape...  13.4 us
    unnamed x40, local copies, waits for them, and re-layouts  13 us
    ppermute x12, starting transfers between devices, exchange(): lax.ppermute(part, 'chan', [(i, (i + shift) % count) for i in range(count)])  12.6 us
  transfers between devices with their start and end apart: 16, of which 9 were waited for; matrix products, arithmetic and copies ran while one was open for 1% of the time, Pallas kernels for 14%

profile of v6, /device:TPU:11, one launch (start us, length us, event | category | flops | bytes accessed | tf_op | source)
XLA Modules:
  0.0 336.5 jit_solution(11582590889109811329)
XLA Ops:
  0.7 6.3 %shard_map.90 = (s32[64,128]{1,0:T(8,128)S(1)}, s32[8,64]{1,0:T(8,128)S(1)}, bf16[1824,256]{1,0:T(8,128)(2,1)S(1)}, bf16[1824,256]{1,0:T(8,128)(2,1)}, bf16[1824...) custom-call(s32[1]{0:T(128)} %bitcast.2.me_ref, s32[64,128]{1,0:T(8,128)} %bitcast.4, bf16[8192,256]{1,0:T(8,128)(2,1)} %v_ref.1), custom_call_target="tpu_custom_call" | custom-call | flops 1140850688 | bytes 8388608 | tf_op jit(solution)/shard_map/pallas_call | solution.py:172
  8.0 2.6 broadcast_multiply_fusion.1.own
  10.7 4.0 %collective-permute-start.17 = (bf16[8192,256]{1,0:T(8,128)(2,1)}, bf16[8192,256]{1,0:T(8,128)(2,1)}, u32[]{:S(2)}, u32[]{:S(2)}) collective-permute-start(bf16[8192,256]{1,0:T(8,128)(2,1)} %broadcast_multiply_fusion.1.own), channel_id=1, source_target_pairs={{4,8},{8,4},{5,9},{9,5},{6,10},{10,6},{7,11},{11,7},{20,24},{24,20... | collective-permute-start | bytes 12582920 | tf_op jit(solution)/shard_map/ppermute | solution.py:515
  14.7 1.3 collective-permute-start.19
  16.1 1.2 collective-permute-start.20
  17.6 11.2 %collective-permute-done.18.x_ref.rest_1_ = bf16[1824,256]{1,0:T(8,128)(2,1)S(1)} collective-permute-done((bf16[1824,256]{1,0:T(8,128)(2,1)}, bf16[1824,256]{1,0:T(8,128)(2,1)S(1)}, u32[]{:S(2)}, u32[]{:S(2)}) %collective-permute-start.18) | collective-permute-done | bytes 933920 | tf_op jit(solution)/shard_map/ppermute | solution.py:484
  29.7 1.3 shard_map.91._
  31.0 30.2 %collective-permute-done.17.far = bf16[8192,256]{1,0:T(8,128)(2,1)} collective-permute-done((bf16[8192,256]{1,0:T(8,128)(2,1)}, bf16[8192,256]{1,0:T(8,128)(2,1)}, u32[]{:S(2)}, u32[]{:S(2)}) %collective-permute-start.17) | collective-permute-done | bytes 4194336 | tf_op jit(solution)/shard_map/ppermute | solution.py:515
  61.9 15.8 %shard_map.92 = (bf16[1824,256]{1,0:T(8,128)(2,1)S(1)}, bf16[1824,256]{1,0:T(8,128)(2,1)S(1)}, bf16[1824,256]{1,0:T(8,128)(2,1)}, bf16[1824,256]{1,0:T(8,128)(2,1)S(1)}) custom-call(s32[1]{0:T(128)} %bitcast.2.me_ref, s32[8,64]{1,0:T(8,128)S(1)} %get-tuple-element.126.offs_ref, s32[384]{0:T(512)S(1)} %reshape.26.ids_ref, s32[64]{0:T(128)S(1)} %copy-done.27, ...), custom_call_target="tpu_custom_call" | custom-call | flops 3221225472 | bytes 29360128 | tf_op jit(solution)/shard_map/pallas_call | solution.py:391
  79.0 1.0 collective-permute-start.24
  80.1 27.7 %collective-permute-done.19.rest_2_ = bf16[1824,256]{1,0:T(8,128)(2,1)S(1)} collective-permute-done((bf16[1824,256]{1,0:T(8,128)(2,1)}, bf16[1824,256]{1,0:T(8,128)(2,1)S(1)}, u32[]{:S(2)}, u32[]{:S(2)}) %collective-permute-start.19) | collective-permute-done | bytes 933920 | tf_op jit(solution)/shard_map/ppermute | solution.py:484
  108.7 1.2 copy-done.7
  109.9 6.5 %shard_map.93 = (bf16[1824,256]{1,0:T(8,128)(2,1)S(1)}, bf16[1824,256]{1,0:T(8,128)(2,1)}, bf16[1824,256]{1,0:T(8,128)(2,1)}, bf16[1824,256]{1,0:T(8,128)(2,1)}) custom-call(s32[1]{0:T(128)} %bitcast.2.me_ref, bf16[1024,1024]{1,0:T(8,128)(2,1)S(1)} %copy-done.20, bf16[1824,256]{1,0:T(8,128)(2,1)S(1)} %get-tuple-element.134.rest_0_, ...), custom_call_target="tpu_custom_call" | custom-call | flops 1 | bytes 1 | tf_op jit(solution)/shard_map/pallas_call | solution.py:454
  116.4 3.0 collective-permute-start.26
  119.5 48.8 %collective-permute-done.22.rest_3_ = bf16[1824,256]{1,0:T(8,128)(2,1)S(1)} collective-permute-done((bf16[1824,256]{1,0:T(8,128)(2,1)S(1)}, bf16[1824,256]{1,0:T(8,128)(2,1)S(1)}, u32[]{:S(2)}, u32[]{:S(2)}) %collective-permute-start.22) | collective-permute-done | bytes 933920 | tf_op jit(solution)/shard_map/ppermute | solution.py:484
  172.1 21.3 %pmax.7 = s32[]{:T(128)} all-reduce(s32[]{:T(128)S(6)} %convert_element_type.13), channel_id=1, replica_groups=mesh['grp'=2,'orbit'=4,'chan'=4] {'grp','orbit'}, use_global_device_ids=true, to_apply=%region_1.2 | all-reduce | flops 1 | bytes 8 | tf_op jit(solution)/shard_map/pmax | solution.py:573
  193.4 34.5 %collective-permute-done.26.rest_2_ = bf16[1824,256]{1,0:T(8,128)(2,1)S(1)} collective-permute-done((bf16[1824,256]{1,0:T(8,128)(2,1)}, bf16[1824,256]{1,0:T(8,128)(2,1)S(1)}, u32[]{:S(2)}, u32[]{:S(2)}) %collective-permute-start.26) | collective-permute-done | bytes 933920 | tf_op jit(solution)/shard_map/ppermute | solution.py:484
  228.8 1.2 copy-done.9
  230.0 1.2 copy-done.11
  231.2 1.2 copy-done.13
  232.3 1.2 copy-done.15
  233.5 6.9 %shard_map.94 = (bf16[1824,256]{1,0:T(8,128)(2,1)S(1)}, bf16[1824,256]{1,0:T(8,128)(2,1)}, bf16[1824,256]{1,0:T(8,128)(2,1)}, bf16[1824,256]{1,0:T(8,128)(2,1)}) custom-call(s32[1]{0:T(128)} %bitcast.2.me_ref, bf16[1024,1024]{1,0:T(8,128)(2,1)} %op_ref.3, bf16[1824,256]{1,0:T(8,128)(2,1)S(1)} %copy-done.9, bf16[1824,256]{1,0:T(8,128)(2,1)S(1)} %copy-done.13, ...), custom_call_target="tpu_custom_call" | custom-call | flops 1 | bytes 1 | tf_op jit(solution)/shard_map/pallas_call | solution.py:454
  240.5 7.4 %collective-permute-done.23.rest_2_ = bf16[1824,256]{1,0:T(8,128)(2,1)} collective-permute-done((bf16[1824,256]{1,0:T(8,128)(2,1)}, bf16[1824,256]{1,0:T(8,128)(2,1)}, u32[]{:S(2)}, u32[]{:S(2)}) %collective-permute-start.23) | collective-permute-done | bytes 933920 | tf_op jit(solution)/shard_map/ppermute | solution.py:484
  248.5 2.5 collective-permute-start.29
  251.6 4.7 %shard_map.95.own = bf16[8192,256]{1,0:T(8,128)(2,1)} custom-call(s32[1]{0:T(128)} %bitcast.2.me_ref, s32[8,64]{1,0:T(8,128)S(1)} %get-tuple-element.126.offs_ref, s32[64,128]{1,0:T(8,128)S(1)} %get-tuple-element.127.pos_ref, bf16[1824,256]{1,0:T(8,128)(2,1)S(1)} %get-tuple-element.155.rest_0_, bf16[1824,256]{1,0:T(8,128)(2,1)S(1)} %collective-permute-done.21.rest_1_, ...), custom_call_target="tpu_custom_call" | custom-call | flops 1073741824 | bytes 8388608 | tf_op jit(solution)/shard_map/pallas_call | solution.py:279
  256.3 15.2 %collective-permute-start.28 = (bf16[8192,256]{1,0:T(8,128)(2,1)}, bf16[8192,256]{1,0:T(8,128)(2,1)}, u32[]{:S(2)}, u32[]{:S(2)}) collective-permute-start(bf16[8192,256]{1,0:T(8,128)(2,1)} %shard_map.95.own), channel_id=1, source_target_pairs={{4,8},{8,4},{5,9},{9,5},{6,10},{10,6},{7,11},{11,7},{20,24},{24,20... | collective-permute-start | bytes 12582920 | tf_op jit(solution)/shard_map/ppermute | solution.py:515
  271.7 1.5 collective-permute-start.30
  273.1 36.3 %collective-permute-done.29.x_ref.rest_2_ = bf16[1824,256]{1,0:T(8,128)(2,1)} collective-permute-done((bf16[1824,256]{1,0:T(8,128)(2,1)}, bf16[1824,256]{1,0:T(8,128)(2,1)}, u32[]{:S(2)}, u32[]{:S(2)}) %collective-permute-start.29) | collective-permute-done | bytes 933920 | tf_op jit(solution)/shard_map/ppermute | solution.py:484
  309.4 1.3 shard_map.96._
  310.7 7.5 %collective-permute-done.28.far = bf16[8192,256]{1,0:T(8,128)(2,1)} collective-permute-done((bf16[8192,256]{1,0:T(8,128)(2,1)}, bf16[8192,256]{1,0:T(8,128)(2,1)}, u32[]{:S(2)}, u32[]{:S(2)}) %collective-permute-start.28) | collective-permute-done | bytes 4194336 | tf_op jit(solution)/shard_map/ppermute | solution.py:515
  318.9 12.2 %shard_map.97 = bf16[8192,256]{1,0:T(8,128)(2,1)} custom-call(s32[1]{0:T(128)} %bitcast.2.me_ref, s32[8,64]{1,0:T(8,128)S(1)} %get-tuple-element.126.offs_ref, s32[384]{0:T(512)S(1)} %reshape.26.ids_ref, s32[64]{0:T(128)S(1)} %copy-done.27, s32[64,128]{1,0:T(8,128)S(1)} %get-tuple-element.127.pos_ref, bf16[64,6,128,128]{3,2,1,0:T(8,128)(2,1)} %weight_ref.3, ...), custom_call_target="tpu_custom_call" | custom-call | flops 3221225472 | bytes 29360128 | tf_op jit(solution)/shard_map/pallas_call | solution.py:391
  331.1 5.0 %shard_map.98 = bf16[8192,256]{1,0:T(8,128)(2,1)} custom-call(s32[1]{0:T(128)} %bitcast.2.me_ref, s32[8,64]{1,0:T(8,128)S(1)} %get-tuple-element.126.offs_ref, s32[64,128]{1,0:T(8,128)S(1)} %get-tuple-element.127.pos_ref, bf16[1824,256]{1,0:T(8,128)(2,1)S(1)} %get-tuple-element.169.rest_0_, bf16[1824,256]{1,0:T(8,128)(2,1)S(1)} %collective-permute-done.30.rest_1_, ...), custom_call_target="tpu_custom_call" | custom-call | flops 1073741824 | bytes 8388608 | tf_op jit(solution)/shard_map/pallas_call | solution.py:279
  (57 shorter events, 11.1 us)
Async XLA Ops:
  0.6 7.4 %copy-start.24 = (s32[8192]{0:T(1024)S(1)}, s32[8192]{0:T(1024)}, u32[]{:S(2)}) copy-start(s32[8192]{0:T(1024)} %param.11) | copy-start | bytes 98308
  0.6 7.4 %copy-start.22 = (bf16[8192,256]{1,0:T(8,128)(2,1)S(1)}, bf16[8192,256]{1,0:T(8,128)(2,1)}, u32[]{:S(2)}) copy-start(bf16[8192,256]{1,0:T(8,128)(2,1)} %param.10) | copy-start | bytes 12582916
  7.0 21.8 %collective-permute-start.18 = (bf16[1824,256]{1,0:T(8,128)(2,1)}, bf16[1824,256]{1,0:T(8,128)(2,1)S(1)}, u32[]{:S(2)}, u32[]{:S(2)}) collective-permute-start(bf16[1824,256]{1,0:T(8,128)(2,1)} %get-tuple-element.129), channel_id=1, source_target_pairs={{0,1},{1,2},{2,3},{3,0},{4,5},{5,6},{6,7},{7,4},{8,9},{9,10},{10,1... | collective-permute-start | bytes 2801672 | tf_op jit(solution)/shard_map/ppermute | solution.py:484
  8.0 9.3 %copy-start.25 = (s32[64,6]{0,1:T(8,128)S(1)}, s32[64,6]{0,1:T(8,128)}, u32[]{:S(2)}) copy-start(s32[64,6]{0,1:T(8,128)} %param.12) | copy-start | bytes 4612
  10.7 50.5 %collective-permute-start.17 = (bf16[8192,256]{1,0:T(8,128)(2,1)}, bf16[8192,256]{1,0:T(8,128)(2,1)}, u32[]{:S(2)}, u32[]{:S(2)}) collective-permute-start(bf16[8192,256]{1,0:T(8,128)(2,1)} %broadcast_multiply_fusion.1.own), channel_id=1, source_target_pairs={{4,8},{8,4},{5,9},{9,5},{6,10},{10,6},{7,11},{11,7},{20,24},{24,20... | collective-permute-start | bytes 12582920 | tf_op jit(solution)/shard_map/ppermute | solution.py:515
  14.7 46.5 %collective-permute-start.16 = (bf16[8192,256]{1,0:T(8,128)(2,1)}, bf16[8192,256]{1,0:T(8,128)(2,1)}, u32[]{:S(2)}, u32[]{:S(2)}) collective-permute-start(bf16[8192,256]{1,0:T(8,128)(2,1)} %broadcast_multiply_fusion.1.own), channel_id=1, source_target_pairs={{0,4},{8,12},{4,0},{12,8},{1,5},{9,13},{5,1},{13,9},{2,6},{10,14},... | collective-permute-start | bytes 12582920 | tf_op jit(solution)/shard_map/ppermute | solution.py:517
  14.7 93.0 %collective-permute-start.19 = (bf16[1824,256]{1,0:T(8,128)(2,1)}, bf16[1824,256]{1,0:T(8,128)(2,1)S(1)}, u32[]{:S(2)}, u32[]{:S(2)}) collective-permute-start(bf16[1824,256]{1,0:T(8,128)(2,1)} %get-tuple-element.132), channel_id=1, source_target_pairs={{0,2},{1,3},{2,0},{3,1},{4,6},{5,7},{6,4},{7,5},{8,10},{9,11},{10,... | collective-permute-start | bytes 2801672 | tf_op jit(solution)/shard_map/ppermute | solution.py:484
  16.1 92.6 %collective-permute-start.20 = (bf16[1824,256]{1,0:T(8,128)(2,1)}, bf16[1824,256]{1,0:T(8,128)(2,1)}, u32[]{:S(2)}, u32[]{:S(2)}) collective-permute-start(bf16[1824,256]{1,0:T(8,128)(2,1)} %get-tuple-element.133), channel_id=1, source_target_pairs={{0,3},{1,0},{2,1},{3,2},{4,7},{5,4},{6,5},{7,6},{8,11},{9,8},{10,9... | collective-permute-start | bytes 2801672 | tf_op jit(solution)/shard_map/ppermute | solution.py:484
  17.5 43.6 %copy-start.27 = (s32[64]{0:T(128)S(1)}, s32[64]{0:T(128)}, u32[]{:S(2)}) copy-start(s32[64]{0:T(128)} %counts_ref.3) | copy-start | bytes 772
  61.9 46.8 %copy-start.5 = (bf16[1824,256]{1,0:T(8,128)(2,1)S(1)}, bf16[1824,256]{1,0:T(8,128)(2,1)}, u32[]{:S(2)}) copy-start(bf16[1824,256]{1,0:T(8,128)(2,1)} %copy-done.4) | copy-start | bytes 2801668
  61.9 46.8 %copy-start.20 = (bf16[1024,1024]{1,0:T(8,128)(2,1)S(1)}, bf16[1024,1024]{1,0:T(8,128)(2,1)}, u32[]{:S(2)}) copy-start(bf16[1024,1024]{1,0:T(8,128)(2,1)} %op_ref.3) | copy-start | bytes 6291460
  77.7 0.9 copy-start.8
  78.6 89.7 %collective-permute-start.22 = (bf16[1824,256]{1,0:T(8,128)(2,1)S(1)}, bf16[1824,256]{1,0:T(8,128)(2,1)S(1)}, u32[]{:S(2)}, u32[]{:S(2)}) collective-permute-start(bf16[1824,256]{1,0:T(8,128)(2,1)S(1)} %get-tuple-element.143), channel_id=1, source_target_pairs={{0,3},{1,0},{2,1},{3,2},{4,7},{5,4},{6,5},{7,6},{8,11},{9,8},{10,9... | collective-permute-start | bytes 2801672 | tf_op jit(solution)/shard_map/ppermute | solution.py:484
  79.0 90.2 %collective-permute-start.24 = (bf16[1824,256]{1,0:T(8,128)(2,1)S(1)}, bf16[1824,256]{1,0:T(8,128)(2,1)S(1)}, u32[]{:S(2)}, u32[]{:S(2)}) collective-permute-start(bf16[1824,256]{1,0:T(8,128)(2,1)S(1)} %get-tuple-element.146), channel_id=1, source_target_pairs={{0,1},{1,2},{2,3},{3,0},{4,5},{5,6},{6,7},{7,4},{8,9},{9,10},{10,1... | collective-permute-start | bytes 2801672 | tf_op jit(solution)/shard_map/ppermute | solution.py:484
  108.7 1.2 copy-start.7
  116.4 124.1 %collective-permute-start.21 = (bf16[1824,256]{1,0:T(8,128)(2,1)}, bf16[1824,256]{1,0:T(8,128)(2,1)S(1)}, u32[]{:S(2)}, u32[]{:S(2)}) collective-permute-start(bf16[1824,256]{1,0:T(8,128)(2,1)} %get-tuple-element.140), channel_id=1, source_target_pairs={{0,1},{1,2},{2,3},{3,0},{4,5},{5,6},{6,7},{7,4},{8,9},{9,10},{10,1... | collective-permute-start | bytes 2801672 | tf_op jit(solution)/shard_map/ppermute | solution.py:484
  116.4 111.4 %collective-permute-start.26 = (bf16[1824,256]{1,0:T(8,128)(2,1)}, bf16[1824,256]{1,0:T(8,128)(2,1)S(1)}, u32[]{:S(2)}, u32[]{:S(2)}) collective-permute-start(bf16[1824,256]{1,0:T(8,128)(2,1)} %get-tuple-element.149), channel_id=1, source_target_pairs={{0,2},{1,3},{2,0},{3,1},{4,6},{5,7},{6,4},{7,5},{8,10},{9,11},{10,... | collective-permute-start | bytes 2801672 | tf_op jit(solution)/shard_map/ppermute | solution.py:484
  168.3 1.0 copy-start.10
  169.3 78.6 %collective-permute-start.23 = (bf16[1824,256]{1,0:T(8,128)(2,1)}, bf16[1824,256]{1,0:T(8,128)(2,1)}, u32[]{:S(2)}, u32[]{:S(2)}) collective-permute-start(bf16[1824,256]{1,0:T(8,128)(2,1)} %get-tuple-element.144), channel_id=1, source_target_pairs={{0,2},{1,3},{2,0},{3,1},{4,6},{5,7},{6,4},{7,5},{8,10},{9,11},{10,... | collective-permute-start | bytes 2801672 | tf_op jit(solution)/shard_map/ppermute | solution.py:484
  169.3 0.9 copy-start.12
  170.2 78.2 %collective-permute-start.25 = (bf16[1824,256]{1,0:T(8,128)(2,1)}, bf16[1824,256]{1,0:T(8,128)(2,1)}, u32[]{:S(2)}, u32[]{:S(2)}) collective-permute-start(bf16[1824,256]{1,0:T(8,128)(2,1)} %get-tuple-element.147), channel_id=1, source_target_pairs={{0,3},{1,0},{2,1},{3,2},{4,7},{5,4},{6,5},{7,6},{8,11},{9,8},{10,9... | collective-permute-start | bytes 2801672 | tf_op jit(solution)/shard_map/ppermute | solution.py:484
  227.8 1.0 copy-start.14
  228.8 1.2 copy-start.9
  230.0 1.2 copy-start.11
  231.2 1.2 copy-start.13
  232.3 1.2 copy-start.15
  248.5 61.0 %collective-permute-start.29 = (bf16[1824,256]{1,0:T(8,128)(2,1)}, bf16[1824,256]{1,0:T(8,128)(2,1)}, u32[]{:S(2)}, u32[]{:S(2)}) collective-permute-start(bf16[1824,256]{1,0:T(8,128)(2,1)} %get-tuple-element.163), channel_id=1, source_target_pairs={{0,2},{1,3},{2,0},{3,1},{4,6},{5,7},{6,4},{7,5},{8,10},{9,11},{10,... | collective-permute-start | bytes 2801672 | tf_op jit(solution)/shard_map/ppermute | solution.py:484
  256.3 61.9 %collective-permute-start.28 = (bf16[8192,256]{1,0:T(8,128)(2,1)}, bf16[8192,256]{1,0:T(8,128)(2,1)}, u32[]{:S(2)}, u32[]{:S(2)}) collective-permute-start(bf16[8192,256]{1,0:T(8,128)(2,1)} %shard_map.95.own), channel_id=1, source_target_pairs={{4,8},{8,4},{5,9},{9,5},{6,10},{10,6},{7,11},{11,7},{20,24},{24,20... | collective-permute-start | bytes 12582920 | tf_op jit(solution)/shard_map/ppermute | solution.py:515
  271.5 46.7 %collective-permute-start.27 = (bf16[8192,256]{1,0:T(8,128)(2,1)}, bf16[8192,256]{1,0:T(8,128)(2,1)}, u32[]{:S(2)}, u32[]{:S(2)}) collective-permute-start(bf16[8192,256]{1,0:T(8,128)(2,1)} %shard_map.95.own), channel_id=1, source_target_pairs={{0,4},{8,12},{4,0},{12,8},{1,5},{9,13},{5,1},{13,9},{2,6},{10,14},... | collective-permute-start | bytes 12582920 | tf_op jit(solution)/shard_map/ppermute | solution.py:517
  271.6 59.5 %collective-permute-start.31 = (bf16[1824,256]{1,0:T(8,128)(2,1)}, bf16[1824,256]{1,0:T(8,128)(2,1)S(1)}, u32[]{:S(2)}, u32[]{:S(2)}) collective-permute-start(bf16[1824,256]{1,0:T(8,128)(2,1)} %get-tuple-element.168), channel_id=1, source_target_pairs={{0,3},{1,0},{2,1},{3,2},{4,7},{5,4},{6,5},{7,6},{8,11},{9,8},{10,9... | collective-permute-start | bytes 2801672 | tf_op jit(solution)/shard_map/ppermute | solution.py:484
  271.7 59.5 %collective-permute-start.30 = (bf16[1824,256]{1,0:T(8,128)(2,1)}, bf16[1824,256]{1,0:T(8,128)(2,1)S(1)}, u32[]{:S(2)}, u32[]{:S(2)}) collective-permute-start(bf16[1824,256]{1,0:T(8,128)(2,1)} %get-tuple-element.166), channel_id=1, source_target_pairs={{0,1},{1,2},{2,3},{3,0},{4,5},{5,6},{6,7},{7,4},{8,9},{9,10},{10,1... | collective-permute-start | bytes 2801672 | tf_op jit(solution)/shard_map/ppermute | solution.py:484
  331.1 5.0 %copy-start.26 = (s32[64,6]{0,1:T(8,128)S(1)}, s32[64,6]{0,1:T(8,128)}, u32[]{:S(2)}) copy-start(s32[64,6]{0,1:T(8,128)} %param.12) | copy-start | bytes 4612
  (4 other events, 3.3 us)

commit v7 on v6

--- a/solution.py
+++ b/solution.py
@@ -21,7 +21,7 @@
     )
 
 
-def plan(quality, pos_ref, offs_ref):
+def plan(quality, pos_ref, offs_ref, started):
     blocks, rows = quality.shape
     ones = quality.astype(jnp.float32).astype(jnp.bfloat16)
 
@@ -33,10 +33,11 @@
     def dot(a, b, dims=((1,), (0,))):
         return lax.dot_general(a, b, (dims, ((), ())), preferred_element_type=jnp.float32)
 
-    within = dot(ones, ahead(rows))
     totals = dot(jnp.ones((8, rows), jnp.bfloat16), ones, ((1,), (1,)))
     first = dot(totals.astype(jnp.bfloat16), ahead(blocks))
     offs_ref[...] = first.astype(jnp.int32)
+    started()
+    within = dot(ones, ahead(rows))
     wide = jnp.broadcast_to(jnp.sum(ones.astype(jnp.float32), axis=1, keepdims=True), (blocks, rows))
     before = dot(ahead(blocks), wide.astype(jnp.bfloat16), ((0,), (0,)))
     pos_ref[...] = jnp.where(quality > 0, (before + within).astype(jnp.int32), -1)
@@ -135,9 +136,8 @@
     rounds = nblk // GROUP
     for copy in group_copies(v_ref, tiles, in_sems):
         copy.start()
-    plan(quality_ref[...], pos_ref, offs_ref)
     copy = pltpu.make_async_copy(offs_ref, offs, offs_sem)
-    copy.start()
+    plan(quality_ref[...], pos_ref, offs_ref, copy.start)
     packed[:ALIGN, :] = jnp.zeros((ALIGN, packed.shape[1]), packed.dtype)
     copy.wait()
 

time: 338 us -> 339 us (level)
  no operation moved by 1% of the time
where the time goes in v7:
time: 339 us; the launch traced here: 337 us
  waiting for transfers between devices  204 us (60%)
  Pallas kernels  59.9 us (18%)
  starting transfers between devices  32 us (9%)
  blocking collectives  21.3 us (6%)
  local copies, waits for them, and re-layouts  13.2 us (4%)
    ppermute x12, waiting for transfers between devices, exchange(): lax.ppermute(part, 'chan', [(i, (i + shift) % count) for i in range(count)])  166 us
    ppermute x2, waiting for transfers between devices, halo_of(): far = lax.ppermute(x, 'orbit', far + [(b, a) for a, b in far])  37.7 us
    pallas_call x2, Pallas kernels, spatial(): pl.pallas_call(functools.partial(spatial_kernel, size is not None), out_s...  28 us
    pmax x1, blocking collectives, overfull(): return lax.pmax(more.astype(jnp.int32), ('grp', 'orbit'))  21.3 us
    ppermute x2, starting transfers between devices, halo_of(): far = lax.ppermute(x, 'orbit', far + [(b, a) for a, b in far])  19.2 us
    pallas_call x2, Pallas kernels, mix(): pl.pallas_call(functools.partial(mix_kernel, count), out_shape=part_shape...  13.4 us
    unnamed x40, local copies, waits for them, and re-layouts  13 us
    ppermute x12, starting transfers between devices, exchange(): lax.ppermute(part, 'chan', [(i, (i + shift) % count) for i in range(count)])  12.6 us
  transfers between devices with their start and end apart: 16, of which 9 were waited for; matrix products, arithmetic and copies ran while one was open for 1% of the time, Pallas kernels for 14%

profile of v7, /device:TPU:11, one launch (start us, length us, event | category | flops | bytes accessed | tf_op | source)
XLA Modules:
  0.0 336.6 jit_solution(5703227558586083526)
XLA Ops:
  0.7 6.3 %shard_map.90 = (s32[64,128]{1,0:T(8,128)S(1)}, s32[8,64]{1,0:T(8,128)S(1)}, bf16[1824,256]{1,0:T(8,128)(2,1)S(1)}, bf16[1824,256]{1,0:T(8,128)(2,1)}, bf16[1824...) custom-call(s32[1]{0:T(128)} %bitcast.2.me_ref, s32[64,128]{1,0:T(8,128)} %bitcast.4, bf16[8192,256]{1,0:T(8,128)(2,1)} %v_ref.1), custom_call_target="tpu_custom_call" | custom-call | flops 1140850688 | bytes 8388608 | tf_op jit(solution)/shard_map/pallas_call | solution.py:172
  6.9 1.0 collective-permute-start.18
  8.0 2.6 broadcast_multiply_fusion.1.own
  10.7 4.0 %collective-permute-start.17 = (bf16[8192,256]{1,0:T(8,128)(2,1)}, bf16[8192,256]{1,0:T(8,128)(2,1)}, u32[]{:S(2)}, u32[]{:S(2)}) collective-permute-start(bf16[8192,256]{1,0:T(8,128)(2,1)} %broadcast_multiply_fusion.1.own), channel_id=1, source_target_pairs={{4,8},{8,4},{5,9},{9,5},{6,10},{10,6},{7,11},{11,7},{20,24},{24,20... | collective-permute-start | bytes 12582920 | tf_op jit(solution)/shard_map/ppermute | solution.py:515
  14.7 1.3 collective-permute-start.19
  16.1 1.2 collective-permute-start.20
  17.6 11.2 %collective-permute-done.18.x_ref.rest_1_ = bf16[1824,256]{1,0:T(8,128)(2,1)S(1)} collective-permute-done((bf16[1824,256]{1,0:T(8,128)(2,1)}, bf16[1824,256]{1,0:T(8,128)(2,1)S(1)}, u32[]{:S(2)}, u32[]{:S(2)}) %collective-permute-start.18) | collective-permute-done | bytes 933920 | tf_op jit(solution)/shard_map/ppermute | solution.py:484
  29.7 1.3 shard_map.91._
  31.0 30.2 %collective-permute-done.17.far = bf16[8192,256]{1,0:T(8,128)(2,1)} collective-permute-done((bf16[8192,256]{1,0:T(8,128)(2,1)}, bf16[8192,256]{1,0:T(8,128)(2,1)}, u32[]{:S(2)}, u32[]{:S(2)}) %collective-permute-start.17) | collective-permute-done | bytes 4194336 | tf_op jit(solution)/shard_map/ppermute | solution.py:515
  61.9 15.8 %shard_map.92 = (bf16[1824,256]{1,0:T(8,128)(2,1)S(1)}, bf16[1824,256]{1,0:T(8,128)(2,1)S(1)}, bf16[1824,256]{1,0:T(8,128)(2,1)}, bf16[1824,256]{1,0:T(8,128)(2,1)S(1)}) custom-call(s32[1]{0:T(128)} %bitcast.2.me_ref, s32[8,64]{1,0:T(8,128)S(1)} %get-tuple-element.126.offs_ref, s32[384]{0:T(512)S(1)} %reshape.26.ids_ref, s32[64]{0:T(128)S(1)} %copy-done.27, ...), custom_call_target="tpu_custom_call" | custom-call | flops 3221225472 | bytes 29360128 | tf_op jit(solution)/shard_map/pallas_call | solution.py:391
  80.1 27.7 %collective-permute-done.19.rest_2_ = bf16[1824,256]{1,0:T(8,128)(2,1)S(1)} collective-permute-done((bf16[1824,256]{1,0:T(8,128)(2,1)}, bf16[1824,256]{1,0:T(8,128)(2,1)S(1)}, u32[]{:S(2)}, u32[]{:S(2)}) %collective-permute-start.19) | collective-permute-done | bytes 933920 | tf_op jit(solution)/shard_map/ppermute | solution.py:484
  108.7 1.2 copy-done.7
  109.9 6.5 %shard_map.93 = (bf16[1824,256]{1,0:T(8,128)(2,1)S(1)}, bf16[1824,256]{1,0:T(8,128)(2,1)}, bf16[1824,256]{1,0:T(8,128)(2,1)}, bf16[1824,256]{1,0:T(8,128)(2,1)}) custom-call(s32[1]{0:T(128)} %bitcast.2.me_ref, bf16[1024,1024]{1,0:T(8,128)(2,1)S(1)} %copy-done.20, bf16[1824,256]{1,0:T(8,128)(2,1)S(1)} %get-tuple-element.134.rest_0_, ...), custom_call_target="tpu_custom_call" | custom-call | flops 1 | bytes 1 | tf_op jit(solution)/shard_map/pallas_call | solution.py:454
  116.5 3.0 collective-permute-start.26
  119.5 48.8 %collective-permute-done.22.rest_3_ = bf16[1824,256]{1,0:T(8,128)(2,1)S(1)} collective-permute-done((bf16[1824,256]{1,0:T(8,128)(2,1)S(1)}, bf16[1824,256]{1,0:T(8,128)(2,1)S(1)}, u32[]{:S(2)}, u32[]{:S(2)}) %collective-permute-start.22) | collective-permute-done | bytes 933920 | tf_op jit(solution)/shard_map/ppermute | solution.py:484
  172.1 21.3 %pmax.7 = s32[]{:T(128)} all-reduce(s32[]{:T(128)S(6)} %convert_element_type.13), channel_id=1, replica_groups=mesh['grp'=2,'orbit'=4,'chan'=4] {'grp','orbit'}, use_global_device_ids=true, to_apply=%region_1.2 | all-reduce | flops 1 | bytes 8 | tf_op jit(solution)/shard_map/pmax | solution.py:573
  193.4 34.4 %collective-permute-done.26.rest_2_ = bf16[1824,256]{1,0:T(8,128)(2,1)S(1)} collective-permute-done((bf16[1824,256]{1,0:T(8,128)(2,1)}, bf16[1824,256]{1,0:T(8,128)(2,1)S(1)}, u32[]{:S(2)}, u32[]{:S(2)}) %collective-permute-start.26) | collective-permute-done | bytes 933920 | tf_op jit(solution)/shard_map/ppermute | solution.py:484
  228.8 1.2 copy-done.9
  230.0 1.2 copy-done.11
  231.2 1.2 copy-done.13
  232.4 1.2 copy-done.15
  233.5 6.9 %shard_map.94 = (bf16[1824,256]{1,0:T(8,128)(2,1)S(1)}, bf16[1824,256]{1,0:T(8,128)(2,1)}, bf16[1824,256]{1,0:T(8,128)(2,1)}, bf16[1824,256]{1,0:T(8,128)(2,1)}) custom-call(s32[1]{0:T(128)} %bitcast.2.me_ref, bf16[1024,1024]{1,0:T(8,128)(2,1)} %op_ref.3, bf16[1824,256]{1,0:T(8,128)(2,1)S(1)} %copy-done.9, bf16[1824,256]{1,0:T(8,128)(2,1)S(1)} %copy-done.13, ...), custom_call_target="tpu_custom_call" | custom-call | flops 1 | bytes 1 | tf_op jit(solution)/shard_map/pallas_call | solution.py:454
  240.5 7.4 %collective-permute-done.23.rest_2_ = bf16[1824,256]{1,0:T(8,128)(2,1)} collective-permute-done((bf16[1824,256]{1,0:T(8,128)(2,1)}, bf16[1824,256]{1,0:T(8,128)(2,1)}, u32[]{:S(2)}, u32[]{:S(2)}) %collective-permute-start.23) | collective-permute-done | bytes 933920 | tf_op jit(solution)/shard_map/ppermute | solution.py:484
  248.5 2.5 collective-permute-start.29
  251.6 4.7 %shard_map.95.own = bf16[8192,256]{1,0:T(8,128)(2,1)} custom-call(s32[1]{0:T(128)} %bitcast.2.me_ref, s32[8,64]{1,0:T(8,128)S(1)} %get-tuple-element.126.offs_ref, s32[64,128]{1,0:T(8,128)S(1)} %get-tuple-element.127.pos_ref, bf16[1824,256]{1,0:T(8,128)(2,1)S(1)} %get-tuple-element.155.rest_0_, bf16[1824,256]{1,0:T(8,128)(2,1)S(1)} %collective-permute-done.21.rest_1_, ...), custom_call_target="tpu_custom_call" | custom-call | flops 1073741824 | bytes 8388608 | tf_op jit(solution)/shard_map/pallas_call | solution.py:279
  256.3 15.2 %collective-permute-start.28 = (bf16[8192,256]{1,0:T(8,128)(2,1)}, bf16[8192,256]{1,0:T(8,128)(2,1)}, u32[]{:S(2)}, u32[]{:S(2)}) collective-permute-start(bf16[8192,256]{1,0:T(8,128)(2,1)} %shard_map.95.own), channel_id=1, source_target_pairs={{4,8},{8,4},{5,9},{9,5},{6,10},{10,6},{7,11},{11,7},{20,24},{24,20... | collective-permute-start | bytes 12582920 | tf_op jit(solution)/shard_map/ppermute | solution.py:515
  271.7 1.5 collective-permute-start.30
  273.2 36.3 %collective-permute-done.29.x_ref.rest_2_ = bf16[1824,256]{1,0:T(8,128)(2,1)} collective-permute-done((bf16[1824,256]{1,0:T(8,128)(2,1)}, bf16[1824,256]{1,0:T(8,128)(2,1)}, u32[]{:S(2)}, u32[]{:S(2)}) %collective-permute-start.29) | collective-permute-done | bytes 933920 | tf_op jit(solution)/shard_map/ppermute | solution.py:484
  309.4 1.3 shard_map.96._
  310.7 7.5 %collective-permute-done.28.far = bf16[8192,256]{1,0:T(8,128)(2,1)} collective-permute-done((bf16[8192,256]{1,0:T(8,128)(2,1)}, bf16[8192,256]{1,0:T(8,128)(2,1)}, u32[]{:S(2)}, u32[]{:S(2)}) %collective-permute-start.28) | collective-permute-done | bytes 4194336 | tf_op jit(solution)/shard_map/ppermute | solution.py:515
  319.0 12.2 %shard_map.97 = bf16[8192,256]{1,0:T(8,128)(2,1)} custom-call(s32[1]{0:T(128)} %bitcast.2.me_ref, s32[8,64]{1,0:T(8,128)S(1)} %get-tuple-element.126.offs_ref, s32[384]{0:T(512)S(1)} %reshape.26.ids_ref, s32[64]{0:T(128)S(1)} %copy-done.27, s32[64,128]{1,0:T(8,128)S(1)} %get-tuple-element.127.pos_ref, bf16[64,6,128,128]{3,2,1,0:T(8,128)(2,1)} %weight_ref.3, ...), custom_call_target="tpu_custom_call" | custom-call | flops 3221225472 | bytes 29360128 | tf_op jit(solution)/shard_map/pallas_call | solution.py:391
  331.2 5.0 %shard_map.98 = bf16[8192,256]{1,0:T(8,128)(2,1)} custom-call(s32[1]{0:T(128)} %bitcast.2.me_ref, s32[8,64]{1,0:T(8,128)S(1)} %get-tuple-element.126.offs_ref, s32[64,128]{1,0:T(8,128)S(1)} %get-tuple-element.127.pos_ref, bf16[1824,256]{1,0:T(8,128)(2,1)S(1)} %get-tuple-element.169.rest_0_, bf16[1824,256]{1,0:T(8,128)(2,1)S(1)} %collective-permute-done.30.rest_1_, ...), custom_call_target="tpu_custom_call" | custom-call | flops 1073741824 | bytes 8388608 | tf_op jit(solution)/shard_map/pallas_call | solution.py:279
  (57 shorter events, 11.1 us)
Async XLA Ops:
  0.6 7.4 %copy-start.24 = (s32[8192]{0:T(1024)S(1)}, s32[8192]{0:T(1024)}, u32[]{:S(2)}) copy-start(s32[8192]{0:T(1024)} %param.11) | copy-start | bytes 98308
  0.6 7.4 %copy-start.22 = (bf16[8192,256]{1,0:T(8,128)(2,1)S(1)}, bf16[8192,256]{1,0:T(8,128)(2,1)}, u32[]{:S(2)}) copy-start(bf16[8192,256]{1,0:T(8,128)(2,1)} %param.10) | copy-start | bytes 12582916
  6.9 21.8 %collective-permute-start.18 = (bf16[1824,256]{1,0:T(8,128)(2,1)}, bf16[1824,256]{1,0:T(8,128)(2,1)S(1)}, u32[]{:S(2)}, u32[]{:S(2)}) collective-permute-start(bf16[1824,256]{1,0:T(8,128)(2,1)} %get-tuple-element.129), channel_id=1, source_target_pairs={{0,1},{1,2},{2,3},{3,0},{4,5},{5,6},{6,7},{7,4},{8,9},{9,10},{10,1... | collective-permute-start | bytes 2801672 | tf_op jit(solution)/shard_map/ppermute | solution.py:484
  8.0 9.3 %copy-start.25 = (s32[64,6]{0,1:T(8,128)S(1)}, s32[64,6]{0,1:T(8,128)}, u32[]{:S(2)}) copy-start(s32[64,6]{0,1:T(8,128)} %param.12) | copy-start | bytes 4612
  10.7 50.5 %collective-permute-start.17 = (bf16[8192,256]{1,0:T(8,128)(2,1)}, bf16[8192,256]{1,0:T(8,128)(2,1)}, u32[]{:S(2)}, u32[]{:S(2)}) collective-permute-start(bf16[8192,256]{1,0:T(8,128)(2,1)} %broadcast_multiply_fusion.1.own), channel_id=1, source_target_pairs={{4,8},{8,4},{5,9},{9,5},{6,10},{10,6},{7,11},{11,7},{20,24},{24,20... | collective-permute-start | bytes 12582920 | tf_op jit(solution)/shard_map/ppermute | solution.py:515
  14.7 46.5 %collective-permute-start.16 = (bf16[8192,256]{1,0:T(8,128)(2,1)}, bf16[8192,256]{1,0:T(8,128)(2,1)}, u32[]{:S(2)}, u32[]{:S(2)}) collective-permute-start(bf16[8192,256]{1,0:T(8,128)(2,1)} %broadcast_multiply_fusion.1.own), channel_id=1, source_target_pairs={{0,4},{8,12},{4,0},{12,8},{1,5},{9,13},{5,1},{13,9},{2,6},{10,14},... | collective-permute-start | bytes 12582920 | tf_op jit(solution)/shard_map/ppermute | solution.py:517
  14.7 93.0 %collective-permute-start.19 = (bf16[1824,256]{1,0:T(8,128)(2,1)}, bf16[1824,256]{1,0:T(8,128)(2,1)S(1)}, u32[]{:S(2)}, u32[]{:S(2)}) collective-permute-start(bf16[1824,256]{1,0:T(8,128)(2,1)} %get-tuple-element.132), channel_id=1, source_target_pairs={{0,2},{1,3},{2,0},{3,1},{4,6},{5,7},{6,4},{7,5},{8,10},{9,11},{10,... | collective-permute-start | bytes 2801672 | tf_op jit(solution)/shard_map/ppermute | solution.py:484
  16.1 92.6 %collective-permute-start.20 = (bf16[1824,256]{1,0:T(8,128)(2,1)}, bf16[1824,256]{1,0:T(8,128)(2,1)}, u32[]{:S(2)}, u32[]{:S(2)}) collective-permute-start(bf16[1824,256]{1,0:T(8,128)(2,1)} %get-tuple-element.133), channel_id=1, source_target_pairs={{0,3},{1,0},{2,1},{3,2},{4,7},{5,4},{6,5},{7,6},{8,11},{9,8},{10,9... | collective-permute-start | bytes 2801672 | tf_op jit(solution)/shard_map/ppermute | solution.py:484
  17.6 43.6 %copy-start.27 = (s32[64]{0:T(128)S(1)}, s32[64]{0:T(128)}, u32[]{:S(2)}) copy-start(s32[64]{0:T(128)} %counts_ref.3) | copy-start | bytes 772
  61.9 46.8 %copy-start.5 = (bf16[1824,256]{1,0:T(8,128)(2,1)S(1)}, bf16[1824,256]{1,0:T(8,128)(2,1)}, u32[]{:S(2)}) copy-start(bf16[1824,256]{1,0:T(8,128)(2,1)} %copy-done.4) | copy-start | bytes 2801668
  61.9 46.8 %copy-start.20 = (bf16[1024,1024]{1,0:T(8,128)(2,1)S(1)}, bf16[1024,1024]{1,0:T(8,128)(2,1)}, u32[]{:S(2)}) copy-start(bf16[1024,1024]{1,0:T(8,128)(2,1)} %op_ref.3) | copy-start | bytes 6291460
  77.7 0.9 copy-start.8
  78.6 89.7 %collective-permute-start.22 = (bf16[1824,256]{1,0:T(8,128)(2,1)S(1)}, bf16[1824,256]{1,0:T(8,128)(2,1)S(1)}, u32[]{:S(2)}, u32[]{:S(2)}) collective-permute-start(bf16[1824,256]{1,0:T(8,128)(2,1)S(1)} %get-tuple-element.143), channel_id=1, source_target_pairs={{0,3},{1,0},{2,1},{3,2},{4,7},{5,4},{6,5},{7,6},{8,11},{9,8},{10,9... | collective-permute-start | bytes 2801672 | tf_op jit(solution)/shard_map/ppermute | solution.py:484
  79.0 90.3 %collective-permute-start.24 = (bf16[1824,256]{1,0:T(8,128)(2,1)S(1)}, bf16[1824,256]{1,0:T(8,128)(2,1)S(1)}, u32[]{:S(2)}, u32[]{:S(2)}) collective-permute-start(bf16[1824,256]{1,0:T(8,128)(2,1)S(1)} %get-tuple-element.146), channel_id=1, source_target_pairs={{0,1},{1,2},{2,3},{3,0},{4,5},{5,6},{6,7},{7,4},{8,9},{9,10},{10,1... | collective-permute-start | bytes 2801672 | tf_op jit(solution)/shard_map/ppermute | solution.py:484
  108.7 1.2 copy-start.7
  116.4 124.1 %collective-permute-start.21 = (bf16[1824,256]{1,0:T(8,128)(2,1)}, bf16[1824,256]{1,0:T(8,128)(2,1)S(1)}, u32[]{:S(2)}, u32[]{:S(2)}) collective-permute-start(bf16[1824,256]{1,0:T(8,128)(2,1)} %get-tuple-element.140), channel_id=1, source_target_pairs={{0,1},{1,2},{2,3},{3,0},{4,5},{5,6},{6,7},{7,4},{8,9},{9,10},{10,1... | collective-permute-start | bytes 2801672 | tf_op jit(solution)/shard_map/ppermute | solution.py:484
  116.5 111.4 %collective-permute-start.26 = (bf16[1824,256]{1,0:T(8,128)(2,1)}, bf16[1824,256]{1,0:T(8,128)(2,1)S(1)}, u32[]{:S(2)}, u32[]{:S(2)}) collective-permute-start(bf16[1824,256]{1,0:T(8,128)(2,1)} %get-tuple-element.149), channel_id=1, source_target_pairs={{0,2},{1,3},{2,0},{3,1},{4,6},{5,7},{6,4},{7,5},{8,10},{9,11},{10,... | collective-permute-start | bytes 2801672 | tf_op jit(solution)/shard_map/ppermute | solution.py:484
  168.3 1.0 copy-start.10
  169.3 78.6 %collective-permute-start.23 = (bf16[1824,256]{1,0:T(8,128)(2,1)}, bf16[1824,256]{1,0:T(8,128)(2,1)}, u32[]{:S(2)}, u32[]{:S(2)}) collective-permute-start(bf16[1824,256]{1,0:T(8,128)(2,1)} %get-tuple-element.144), channel_id=1, source_target_pairs={{0,2},{1,3},{2,0},{3,1},{4,6},{5,7},{6,4},{7,5},{8,10},{9,11},{10,... | collective-permute-start | bytes 2801672 | tf_op jit(solution)/shard_map/ppermute | solution.py:484
  169.3 0.9 copy-start.12
  170.2 78.2 %collective-permute-start.25 = (bf16[1824,256]{1,0:T(8,128)(2,1)}, bf16[1824,256]{1,0:T(8,128)(2,1)}, u32[]{:S(2)}, u32[]{:S(2)}) collective-permute-start(bf16[1824,256]{1,0:T(8,128)(2,1)} %get-tuple-element.147), channel_id=1, source_target_pairs={{0,3},{1,0},{2,1},{3,2},{4,7},{5,4},{6,5},{7,6},{8,11},{9,8},{10,9... | collective-permute-start | bytes 2801672 | tf_op jit(solution)/shard_map/ppermute | solution.py:484
  227.8 1.0 copy-start.14
  228.8 1.2 copy-start.9
  230.0 1.2 copy-start.11
  231.2 1.2 copy-start.13
  232.3 1.2 copy-start.15
  248.5 61.0 %collective-permute-start.29 = (bf16[1824,256]{1,0:T(8,128)(2,1)}, bf16[1824,256]{1,0:T(8,128)(2,1)}, u32[]{:S(2)}, u32[]{:S(2)}) collective-permute-start(bf16[1824,256]{1,0:T(8,128)(2,1)} %get-tuple-element.163), channel_id=1, source_target_pairs={{0,2},{1,3},{2,0},{3,1},{4,6},{5,7},{6,4},{7,5},{8,10},{9,11},{10,... | collective-permute-start | bytes 2801672 | tf_op jit(solution)/shard_map/ppermute | solution.py:484
  256.3 61.9 %collective-permute-start.28 = (bf16[8192,256]{1,0:T(8,128)(2,1)}, bf16[8192,256]{1,0:T(8,128)(2,1)}, u32[]{:S(2)}, u32[]{:S(2)}) collective-permute-start(bf16[8192,256]{1,0:T(8,128)(2,1)} %shard_map.95.own), channel_id=1, source_target_pairs={{4,8},{8,4},{5,9},{9,5},{6,10},{10,6},{7,11},{11,7},{20,24},{24,20... | collective-permute-start | bytes 12582920 | tf_op jit(solution)/shard_map/ppermute | solution.py:515
  271.6 46.7 %collective-permute-start.27 = (bf16[8192,256]{1,0:T(8,128)(2,1)}, bf16[8192,256]{1,0:T(8,128)(2,1)}, u32[]{:S(2)}, u32[]{:S(2)}) collective-permute-start(bf16[8192,256]{1,0:T(8,128)(2,1)} %shard_map.95.own), channel_id=1, source_target_pairs={{0,4},{8,12},{4,0},{12,8},{1,5},{9,13},{5,1},{13,9},{2,6},{10,14},... | collective-permute-start | bytes 12582920 | tf_op jit(solution)/shard_map/ppermute | solution.py:517
  271.7 59.5 %collective-permute-start.31 = (bf16[1824,256]{1,0:T(8,128)(2,1)}, bf16[1824,256]{1,0:T(8,128)(2,1)S(1)}, u32[]{:S(2)}, u32[]{:S(2)}) collective-permute-start(bf16[1824,256]{1,0:T(8,128)(2,1)} %get-tuple-element.168), channel_id=1, source_target_pairs={{0,3},{1,0},{2,1},{3,2},{4,7},{5,4},{6,5},{7,6},{8,11},{9,8},{10,9... | collective-permute-start | bytes 2801672 | tf_op jit(solution)/shard_map/ppermute | solution.py:484
  271.7 59.5 %collective-permute-start.30 = (bf16[1824,256]{1,0:T(8,128)(2,1)}, bf16[1824,256]{1,0:T(8,128)(2,1)S(1)}, u32[]{:S(2)}, u32[]{:S(2)}) collective-permute-start(bf16[1824,256]{1,0:T(8,128)(2,1)} %get-tuple-element.166), channel_id=1, source_target_pairs={{0,1},{1,2},{2,3},{3,0},{4,5},{5,6},{6,7},{7,4},{8,9},{9,10},{10,1... | collective-permute-start | bytes 2801672 | tf_op jit(solution)/shard_map/ppermute | solution.py:484
  331.2 5.0 %copy-start.26 = (s32[64,6]{0,1:T(8,128)S(1)}, s32[64,6]{0,1:T(8,128)}, u32[]{:S(2)}) copy-start(s32[64,6]{0,1:T(8,128)} %param.12) | copy-start | bytes 4612
  (4 other events, 3.3 us)
